TPU v7x, 32 devices: a whole 2x2x4 slice. The times are simulated.
32 devices in a mesh: seq: 8 (over z, x), fsdp: 4 (over y, core).
Axes of the slice: x: 2, y: 2, z: 4, core: 2. Of those that a mesh axis runs over, the one named last changes fastest.
Arguments:
- image_query: bfloat16 [4, 2048, 1536], P('fsdp', 'seq'), may hold values from -6 to 6
- image_key: bfloat16 [4, 2048, 1536], P('fsdp', 'seq'), may hold values from -6 to 6
- image_value: bfloat16 [4, 2048, 1536], P('fsdp', 'seq'), may hold values from -6 to 6
- text_key: bfloat16 [4, 512, 1536], P('fsdp'), may hold values from -6 to 6
- text_value: bfloat16 [4, 512, 1536], P('fsdp'), may hold values from -6 to 6
- out_weight: bfloat16 [1536, 1536], P('fsdp'), may hold values from -0.15625 to 0.15625
- cotangent: bfloat16 [4, 2048, 1536], P('fsdp', 'seq'), may hold values from -6 to 6
Outputs:
- image_out: bfloat16 [4, 2048, 1536], P('fsdp', 'seq')
- grad_query: bfloat16 [4, 2048, 1536], P('fsdp', 'seq')
- grad_key: bfloat16 [4, 2048, 1536], P('fsdp', 'seq')
- grad_value: bfloat16 [4, 2048, 1536], P('fsdp', 'seq')
- grad_weight: float32 [1536, 1536], P(('fsdp', 'seq'))
All inputs are finite; a program needn't handle non-finite values.
Results may differ from a plain program's by a relative error of at most 0.0095.
Values may be sent and summed in bfloat16 or wider, within the bound.
No kernel may reach another device: no remote copies, remote signals or barrier semaphores. Data moves between devices by JAX's collectives and lax.ppermute only.
A program may use at most 128 MiB of HBM per device.

v0:
```python
import math

import jax
import jax.numpy as jnp
from jax import lax
from jax.sharding import PartitionSpec as P

HEAD_DIM = 128
STEPS = 4


def from_behind(block, axis, distance):
    devices = range(lax.axis_size(axis))
    route = [((i - distance) % len(devices), i) for i in devices]
    return lax.ppermute(block, axis, route)


def head_pass(inputs):
    head_query, head_key, head_value, head_grad = inputs
    scaling = 1.0 / math.sqrt(head_query.shape[1])
    scores = (
        lax.dot_general(
            head_query, head_key, (((1,), (1,)), ((), ())), preferred_element_type=jnp.float32
        )
        * scaling
    )
    row_peak = jnp.max(scores, axis=1, keepdims=True)
    shifted = jnp.exp(scores - row_peak)
    softmax = shifted / jnp.sum(shifted, axis=1, keepdims=True)
    prob_low = softmax.astype(jnp.bfloat16)
    attended = jnp.dot(prob_low, head_value, preferred_element_type=jnp.float32).astype(
        jnp.bfloat16
    )
    row_delta = jnp.sum(
        head_grad.astype(jnp.float32) * attended.astype(jnp.float32), axis=1, keepdims=True
    )
    grad_prob = lax.dot_general(
        head_grad, head_value, (((1,), (1,)), ((), ())), preferred_element_type=jnp.float32
    )
    grad_score = (softmax * (grad_prob - row_delta) * scaling).astype(jnp.bfloat16)
    grad_q = jnp.dot(grad_score, head_key, preferred_element_type=jnp.float32).astype(jnp.bfloat16)
    grad_k = lax.dot_general(
        grad_score, head_query, (((0,), (0,)), ((), ())), preferred_element_type=jnp.float32
    )
    grad_v = lax.dot_general(
        prob_low, head_grad, (((0,), (0,)), ((), ())), preferred_element_type=jnp.float32
    )
    return (attended, grad_q, grad_k, grad_v)


def split_heads(matrix, width):
    return matrix.reshape(matrix.shape[0], -1, width).transpose(1, 0, 2)


def merge_heads(stacked):
    return stacked.transpose(1, 0, 2).reshape(stacked.shape[1], -1)


def per_device(image_query, image_key, image_value, text_key, text_value, out_weight, cotangent):
    queries = image_query[0]
    own_keys = image_key[0]
    own_values = image_value[0]
    grad_out = cotangent[0]
    tokens = queries.shape[0]
    earlier = []
    moving = (own_keys, own_values)
    for distance in range(1, STEPS):
        moving = from_behind((moving[0], moving[1]), "seq", 1)
        earlier.append(moving)
    full_weight = lax.all_gather(out_weight, "fsdp", axis=0, tiled=True)
    grad_attended = lax.dot_general(
        grad_out, full_weight, (((1,), (1,)), ((), ())), preferred_element_type=jnp.float32
    ).astype(jnp.bfloat16)
    ordered = [earlier[distance - 1] for distance in range(STEPS - 1, 0, -1)]
    set_keys = jnp.concatenate(
        [text_key[0]] + [member[0] for member in ordered] + [own_keys], axis=0
    )
    set_values = jnp.concatenate(
        [text_value[0]] + [member[1] for member in ordered] + [own_values], axis=0
    )
    attended, grad_q, grad_k, grad_v = lax.map(
        head_pass,
        (
            split_heads(queries, HEAD_DIM),
            split_heads(set_keys, HEAD_DIM),
            split_heads(set_values, HEAD_DIM),
            split_heads(grad_attended, HEAD_DIM),
        ),
    )
    attended = merge_heads(attended)
    grad_q = merge_heads(grad_q)
    grad_k = merge_heads(grad_k)
    grad_v = merge_heads(grad_v)
    text_rows = text_key.shape[1]

    def block_part(distance):
        first_row = text_rows + (STEPS - 1 - distance) * tokens
        return (grad_k[first_row : first_row + tokens], grad_v[first_row : first_row + tokens])

    carried = block_part(STEPS - 1)
    for distance in range(STEPS - 2, -1, -1):
        carried = from_behind((carried[0], carried[1]), "seq", -1)
        own_part = block_part(distance)
        carried = (carried[0] + own_part[0], carried[1] + own_part[1])
    image_out = jnp.dot(attended, full_weight, preferred_element_type=jnp.float32).astype(
        jnp.bfloat16
    )
    weight_terms = lax.dot_general(
        attended, grad_out, (((0,), (0,)), ((), ())), preferred_element_type=jnp.float32
    )
    weight_rows = lax.psum_scatter(
        weight_terms.astype(jnp.bfloat16), "fsdp", scatter_dimension=0, tiled=True
    ).astype(jnp.float32)
    grad_weight = lax.psum_scatter(weight_rows, "seq", scatter_dimension=0, tiled=True)
    return (
        image_out[None],
        grad_q[None],
        carried[0].astype(jnp.bfloat16)[None],
        carried[1].astype(jnp.bfloat16)[None],
        grad_weight,
    )


def solution(mesh):
    in_specs = (
        P("fsdp", "seq", None),
        P("fsdp", "seq", None),
        P("fsdp", "seq", None),
        P("fsdp", None, None),
        P("fsdp", None, None),
        P("fsdp", None),
        P("fsdp", "seq", None),
    )
    out_specs = (
        P("fsdp", "seq", None),
        P("fsdp", "seq", None),
        P("fsdp", "seq", None),
        P("fsdp", "seq", None),
        P(("fsdp", "seq"), None),
    )
    return jax.shard_map(
        per_device, mesh=mesh, in_specs=in_specs, out_specs=out_specs, check_vma=False
    )
```

profile of v0, /device:TPU:0, one launch (start us, length us, event | category | flops | bytes accessed | tf_op | source)
XLA Modules:
  0.0 557.1 jit_solution(4339564061911567871)
XLA Ops:
  14.7 18.4 %collective-permute-done.3 = bf16[256,1536]{0,1:T(8,128)(2,1)S(1)} collective-permute-done((bf16[256,1536]{0,1:T(8,128)(2,1)S(1)}, bf16[256,1536]{0,1:T(8,128)(2,1)S(1)}, u32[]{:S(2)}, u32[]{:S(2)}) %collective-permute-start.3) | collective-permute-done | bytes 786464 | tf_op jit(solution)/shard_map/ppermute | solution.py:15
  33.1 17.0 %collective-permute-done = bf16[256,1536]{0,1:T(8,128)(2,1)} collective-permute-done((bf16[256,1536]{0,1:T(8,128)(2,1)S(1)}, bf16[256,1536]{0,1:T(8,128)(2,1)}, u32[]{:S(2)}, u32[]{:S(2)}) %collective-permute-start) | collective-permute-done | bytes 786464 | tf_op jit(solution)/shard_map/ppermute | solution.py:15
  50.0 16.8 %collective-permute-done.4 = bf16[256,1536]{0,1:T(8,128)(2,1)} collective-permute-done((bf16[256,1536]{0,1:T(8,128)(2,1)S(1)}, bf16[256,1536]{0,1:T(8,128)(2,1)}, u32[]{:S(2)}, u32[]{:S(2)}) %collective-permute-start.4) | collective-permute-done | bytes 786464 | tf_op jit(solution)/shard_map/ppermute | solution.py:15
  73.6 10.1 %collective-permute-done.1 = bf16[256,1536]{0,1:T(8,128)(2,1)} collective-permute-done((bf16[256,1536]{0,1:T(8,128)(2,1)}, bf16[256,1536]{0,1:T(8,128)(2,1)}, u32[]{:S(2)}, u32[]{:S(2)}) %collective-permute-start.1) | collective-permute-done | bytes 786464 | tf_op jit(solution)/shard_map/ppermute | solution.py:15
  86.7 13.9 %collective-permute-done.5 = bf16[256,1536]{0,1:T(8,128)(2,1)} collective-permute-done((bf16[256,1536]{0,1:T(8,128)(2,1)}, bf16[256,1536]{0,1:T(8,128)(2,1)}, u32[]{:S(2)}, u32[]{:S(2)}) %collective-permute-start.5) | collective-permute-done | bytes 786464 | tf_op jit(solution)/shard_map/ppermute | solution.py:15
  103.3 13.2 %collective-permute-done.2 = bf16[256,1536]{0,1:T(8,128)(2,1)S(1)} collective-permute-done((bf16[256,1536]{0,1:T(8,128)(2,1)}, bf16[256,1536]{0,1:T(8,128)(2,1)S(1)}, u32[]{:S(2)}, u32[]{:S(2)}) %collective-permute-start.2) | collective-permute-done | bytes 786464 | tf_op jit(solution)/shard_map/ppermute | solution.py:15
  122.8 3.7 convolution_convert_fusion.4
  127.8 154.1 %while.16 = (s32[]{:T(128)}, bf16[12,256,128]{1,2,0:T(8,128)(2,1)}, bf16[12,256,128]{1,2,0:T(8,128)(2,1)}, f32[12,1536,128]{1,2,0:T(8,128)}, f32[12,1536,128]{1,...) while((s32[]{:T(128)}, bf16[12,256,128]{1,2,0:T(8,128)(2,1)}, ...), condition=%wide.region_4.5_spmd, body=%wide.region_0.4_spmd.sunk | while | flops 610467072 | bytes 14237817 | solution.py:81
  281.8 4.7 convolution_convert_fusion.2
  286.6 4.9 fusion.40
  293.3 3.1 fusion.41
  297.8 31.1 %collective-permute-done.9 = f32[256,1536]{0,1:T(8,128)S(1)} collective-permute-done((f32[256,1536]{0,1:T(8,128)S(1)}, f32[256,1536]{0,1:T(8,128)S(1)}, u32[]{:S(2)}, u32[]{:S(2)}) %collective-permute-start.9) | collective-permute-done | bytes 1572896 | tf_op jit(solution)/shard_map/ppermute | solution.py:15
  330.3 4.4 collective-permute-start.10
  334.7 3.0 convert_element_type.41
  337.8 41.4 %collective-permute-done.6 = f32[256,1536]{0,1:T(8,128)} collective-permute-done((f32[256,1536]{0,1:T(8,128)}, f32[256,1536]{0,1:T(8,128)}, u32[]{:S(2)}, u32[]{:S(2)}) %collective-permute-start.6) | collective-permute-done | bytes 1572896 | tf_op jit(solution)/shard_map/ppermute | solution.py:15
  381.4 5.3 collective-permute-start.7
  386.6 28.0 %collective-permute-done.10 = f32[256,1536]{0,1:T(8,128)} collective-permute-done((f32[256,1536]{0,1:T(8,128)}, f32[256,1536]{0,1:T(8,128)}, u32[]{:S(2)}, u32[]{:S(2)}) %collective-permute-start.10) | collective-permute-done | bytes 1572896 | tf_op jit(solution)/shard_map/ppermute | solution.py:15
  417.5 5.3 collective-permute-start.11
  422.7 25.5 %collective-permute-done.7 = f32[256,1536]{0,1:T(8,128)S(1)} collective-permute-done((f32[256,1536]{0,1:T(8,128)S(1)}, f32[256,1536]{0,1:T(8,128)S(1)}, u32[]{:S(2)}, u32[]{:S(2)}) %collective-permute-start.7) | collective-permute-done | bytes 1572896 | tf_op jit(solution)/shard_map/ppermute | solution.py:15
  449.6 5.3 collective-permute-start.8
  456.0 4.9 fusion.34
  460.9 21.1 %collective-permute-done.11 = f32[256,1536]{0,1:T(8,128)} collective-permute-done((f32[256,1536]{0,1:T(8,128)}, f32[256,1536]{0,1:T(8,128)}, u32[]{:S(2)}, u32[]{:S(2)}) %collective-permute-start.11) | collective-permute-done | bytes 1572896 | tf_op jit(solution)/shard_map/ppermute | solution.py:15
  484.8 28.9 %collective-permute-done.8 = f32[256,1536]{0,1:T(8,128)} collective-permute-done((f32[256,1536]{0,1:T(8,128)}, f32[256,1536]{0,1:T(8,128)}, u32[]{:S(2)}, u32[]{:S(2)}) %collective-permute-start.8) | collective-permute-done | bytes 1572896 | tf_op jit(solution)/shard_map/ppermute | solution.py:15
  516.5 34.1 %reduce-scatter.5.cloned.1.call-done = f32[48,1536]{1,0:T(8,128)} async-done(((f32[384,1536]{1,0:T(8,128)}), f32[48,1536]{1,0:T(8,128)}) %reduce-scatter.5.cloned.1.call-update) | async-done | bytes 294928 | tf_op jit(solution)/shard_map/reduce_scatter | solution.py:114
  (189 shorter events, 198.8 us)
Async XLA Ops:
  7.2 115.7 %copy-start = (bf16[1,256,1536]{2,1,0:T(8,128)(2,1)S(1)}, bf16[1,256,1536]{2,1,0:T(8,128)(2,1)}, u32[]{:S(2)}) copy-start(bf16[1,256,1536]{2,1,0:T(8,128)(2,1)} %param.15) | copy-start | bytes 2359300
  7.2 115.7 %all-gather.2.cloned.1.call-start = ((), (), s32[]{:S(2)}) async-start(), calls=%async_computation.2 | async-start | bytes 5898240 | tf_op jit(solution)/shard_map/all_gather | solution.py:70
  7.9 326.8 %reduce-scatter.3.cloned.1.call-start = ((), (), s32[]{:S(2)}) async-start(), calls=%async_computation.3 | async-start | bytes 5898240 | tf_op jit(solution)/shard_map/reduce_scatter | solution.py:111
  8.7 58.2 %copy-start.5 = (bf16[1,256,1536]{1,2,0:T(8,128)(2,1)}, bf16[1,256,1536]{1,2,0:T(8,128)(2,1)S(1)}, u32[]{:S(2)}) copy-start(bf16[1,256,1536]{1,2,0:T(8,128)(2,1)S(1)} %copy.28) | copy-start | bytes 2359300
  8.7 24.4 %collective-permute-start.3 = (bf16[256,1536]{0,1:T(8,128)(2,1)S(1)}, bf16[256,1536]{0,1:T(8,128)(2,1)S(1)}, u32[]{:S(2)}, u32[]{:S(2)}) collective-permute-start(bf16[256,1536]{0,1:T(8,128)(2,1)S(1)} %bitcast.144), channel_id=1, source_target_pairs={{28,0},{0,4},{4,8},{8,12},{12,16},{16,20},{20,24},{24,28},{29,1},{... | collective-permute-start | bytes 2359304 | tf_op jit(solution)/shard_map/ppermute | solution.py:15
  13.1 37.0 %collective-permute-start = (bf16[256,1536]{0,1:T(8,128)(2,1)S(1)}, bf16[256,1536]{0,1:T(8,128)(2,1)}, u32[]{:S(2)}, u32[]{:S(2)}) collective-permute-start(bf16[256,1536]{0,1:T(8,128)(2,1)S(1)} %bitcast.142), channel_id=1, source_target_pairs={{28,0},{0,4},{4,8},{8,12},{12,16},{16,20},{20,24},{24,28},{29,1},{... | collective-permute-start | bytes 2359304 | tf_op jit(solution)/shard_map/ppermute | solution.py:15
  33.1 33.8 %copy-start.9 = (bf16[256,1536]{0,1:T(8,128)(2,1)}, bf16[256,1536]{0,1:T(8,128)(2,1)S(1)}, u32[]{:S(2)}) copy-start(bf16[256,1536]{0,1:T(8,128)(2,1)S(1)} %collective-permute-done.3) | copy-start | bytes 2359300
  33.1 33.8 %collective-permute-start.4 = (bf16[256,1536]{0,1:T(8,128)(2,1)S(1)}, bf16[256,1536]{0,1:T(8,128)(2,1)}, u32[]{:S(2)}, u32[]{:S(2)}) collective-permute-start(bf16[256,1536]{0,1:T(8,128)(2,1)S(1)} %collective-permute-done.3), channel_id=1, source_target_pairs={{28,0},{0,4},{4,8},{8,12},{12,16},{16,20},{20,24},{24,28},{29,1},{... | collective-permute-start | bytes 2359304 | tf_op jit(solution)/shard_map/ppermute | solution.py:15
  50.0 33.7 %collective-permute-start.1 = (bf16[256,1536]{0,1:T(8,128)(2,1)}, bf16[256,1536]{0,1:T(8,128)(2,1)}, u32[]{:S(2)}, u32[]{:S(2)}) collective-permute-start(bf16[256,1536]{0,1:T(8,128)(2,1)} %collective-permute-done), channel_id=1, source_target_pairs={{28,0},{0,4},{4,8},{8,12},{12,16},{16,20},{20,24},{24,28},{29,1},{... | collective-permute-start | bytes 2359304 | tf_op jit(solution)/shard_map/ppermute | solution.py:15
  66.9 33.7 %collective-permute-start.5 = (bf16[256,1536]{0,1:T(8,128)(2,1)}, bf16[256,1536]{0,1:T(8,128)(2,1)}, u32[]{:S(2)}, u32[]{:S(2)}) collective-permute-start(bf16[256,1536]{0,1:T(8,128)(2,1)} %collective-permute-done.4), channel_id=1, source_target_pairs={{28,0},{0,4},{4,8},{8,12},{12,16},{16,20},{20,24},{24,28},{29,1},{... | collective-permute-start | bytes 2359304 | tf_op jit(solution)/shard_map/ppermute | solution.py:15
  83.7 32.8 %collective-permute-start.2 = (bf16[256,1536]{0,1:T(8,128)(2,1)}, bf16[256,1536]{0,1:T(8,128)(2,1)S(1)}, u32[]{:S(2)}, u32[]{:S(2)}) collective-permute-start(bf16[256,1536]{0,1:T(8,128)(2,1)} %collective-permute-done.1), channel_id=1, source_target_pairs={{28,0},{0,4},{4,8},{8,12},{12,16},{16,20},{20,24},{24,28},{29,1},{... | collective-permute-start | bytes 2359304 | tf_op jit(solution)/shard_map/ppermute | solution.py:15
  103.3 14.2 %copy-start.11 = (bf16[1536,12,128]{0,2,1:T(8,128)(2,1)}, bf16[1536,12,128]{0,2,1:T(8,128)(2,1)S(1)}, u32[]{:S(2)}) copy-start(bf16[1536,12,128]{0,2,1:T(8,128)(2,1)S(1)} %constant_dynamic-update-slice_fusion.6) | copy-start | bytes 14155780
  286.6 264.0 %reduce-scatter.5.cloned.1.call-start = ((), (), s32[]{:S(2)}) async-start(), calls=%async_computation.4 | async-start | bytes 2654208 | tf_op jit(solution)/shard_map/reduce_scatter | solution.py:114
  286.6 6.7 %copy-start.4 = (f32[12,1536,128]{1,2,0:T(8,128)S(1)}, f32[12,1536,128]{1,2,0:T(8,128)}, u32[]{:S(2)}) copy-start(f32[12,1536,128]{1,2,0:T(8,128)} %get-tuple-element.57) | copy-start | bytes 28311556
  291.5 37.3 %collective-permute-start.9 = (f32[256,1536]{0,1:T(8,128)S(1)}, f32[256,1536]{0,1:T(8,128)S(1)}, u32[]{:S(2)}, u32[]{:S(2)}) collective-permute-start(f32[256,1536]{0,1:T(8,128)S(1)} %bitcast.148), channel_id=1, source_target_pairs={{4,0},{8,4},{12,8},{16,12},{20,16},{24,20},{28,24},{0,28},{5,1},{9... | collective-permute-start | bytes 4718600 | tf_op jit(solution)/shard_map/ppermute | solution.py:15
  296.4 82.7 %collective-permute-start.6 = (f32[256,1536]{0,1:T(8,128)}, f32[256,1536]{0,1:T(8,128)}, u32[]{:S(2)}, u32[]{:S(2)}) collective-permute-start(f32[256,1536]{0,1:T(8,128)} %bitcast.33), channel_id=1, source_target_pairs={{4,0},{8,4},{12,8},{16,12},{20,16},{24,20},{28,24},{0,28},{5,1},{9... | collective-permute-start | bytes 4718600 | tf_op jit(solution)/shard_map/ppermute | solution.py:15
  330.3 84.3 %collective-permute-start.10 = (f32[256,1536]{0,1:T(8,128)}, f32[256,1536]{0,1:T(8,128)}, u32[]{:S(2)}, u32[]{:S(2)}) collective-permute-start(f32[256,1536]{0,1:T(8,128)} %bitcast_add_fusion.2), channel_id=1, source_target_pairs={{4,0},{8,4},{12,8},{16,12},{20,16},{24,20},{28,24},{0,28},{5,1},{9... | collective-permute-start | bytes 4718600 | tf_op jit(solution)/shard_map/ppermute | solution.py:15
  379.2 35.5 %copy-start.3 = (f32[256,12,128]{0,2,1:T(8,128)S(1)}, f32[256,12,128]{0,2,1:T(8,128)}, u32[]{:S(2)}) copy-start(f32[256,12,128]{0,2,1:T(8,128)} %get-tuple-element.105) | copy-start | bytes 4718596
  381.4 66.8 %collective-permute-start.7 = (f32[256,1536]{0,1:T(8,128)S(1)}, f32[256,1536]{0,1:T(8,128)S(1)}, u32[]{:S(2)}, u32[]{:S(2)}) collective-permute-start(f32[256,1536]{0,1:T(8,128)S(1)} %bitcast_add_fusion.5), channel_id=1, source_target_pairs={{4,0},{8,4},{12,8},{16,12},{20,16},{24,20},{28,24},{0,28},{5,1},{9... | collective-permute-start | bytes 4718600 | tf_op jit(solution)/shard_map/ppermute | solution.py:15
  414.6 33.6 %copy-start.2 = (f32[256,12,128]{0,2,1:T(8,128)S(1)}, f32[256,12,128]{0,2,1:T(8,128)}, u32[]{:S(2)}) copy-start(f32[256,12,128]{0,2,1:T(8,128)} %get-tuple-element.109) | copy-start | bytes 4718596
  417.5 64.6 %collective-permute-start.11 = (f32[256,1536]{0,1:T(8,128)}, f32[256,1536]{0,1:T(8,128)}, u32[]{:S(2)}, u32[]{:S(2)}) collective-permute-start(f32[256,1536]{0,1:T(8,128)} %bitcast_add_fusion.1), channel_id=1, source_target_pairs={{4,0},{8,4},{12,8},{16,12},{20,16},{24,20},{28,24},{0,28},{5,1},{9... | collective-permute-start | bytes 4718600 | tf_op jit(solution)/shard_map/ppermute | solution.py:15
  448.2 6.6 %copy-start.8 = (bf16[12,256,128]{1,2,0:T(8,128)(2,1)S(1)}, bf16[12,256,128]{1,2,0:T(8,128)(2,1)}, u32[]{:S(2)}) copy-start(bf16[12,256,128]{1,2,0:T(8,128)(2,1)} %get-tuple-element.56) | copy-start | bytes 2359300
  449.6 64.1 %collective-permute-start.8 = (f32[256,1536]{0,1:T(8,128)}, f32[256,1536]{0,1:T(8,128)}, u32[]{:S(2)}, u32[]{:S(2)}) collective-permute-start(f32[256,1536]{0,1:T(8,128)} %bitcast_add_fusion.4), channel_id=1, source_target_pairs={{4,0},{8,4},{12,8},{16,12},{20,16},{24,20},{28,24},{0,28},{5,1},{9... | collective-permute-start | bytes 4718600 | tf_op jit(solution)/shard_map/ppermute | solution.py:15
  483.7 30.0 %copy-start.1 = (f32[256,12,128]{0,2,1:T(8,128)S(1)}, f32[256,12,128]{0,2,1:T(8,128)}, u32[]{:S(2)}) copy-start(f32[256,12,128]{0,2,1:T(8,128)} %get-tuple-element.108) | copy-start | bytes 4718596
  (3 other events, 5.2 us)
Sparse Core Ops, SparseCore 0:
  9.6 40.1 all-gather.1
  286.7 46.2 reduce-scatter.2
  337.9 212.6 reduce-scatter.4
where the time goes:
time: 561 us; the launch traced here: 557 us
  waiting for transfers between devices  300 us (53%)
  matrix products  143 us (25%)
  local copies, waits for them, and re-layouts  42.4 us (8%)
  other arithmetic  29 us (5%)
  starting transfers between devices  28.1 us (5%)
  between operations  13.9 us (2%)
    ppermute x12, waiting for transfers between devices, from_behind(): return lax.ppermute(block, axis, route)  265 us
    reduce_scatter x1, waiting for transfers between devices, per_device(): lax.psum_scatter(weight_rows, 'seq', scatter_dimension=0, tiled=True)  34.1 us
    ppermute x12, starting transfers between devices, from_behind(): return lax.ppermute(block, axis, route)  28 us
    dot_general x12, matrix products, head_pass(): lax.dot_general(prob_low, head_grad, (((0,), (0,)), ((), ())), preferred_...  26.9 us
    dot_general x12, matrix products, head_pass(): jnp.dot(prob_low, head_value, preferred_element_type=jnp.float32)  25.7 us
    dot_general x12, matrix products, head_pass(): lax.dot_general(grad_score, head_query, (((0,), (0,)), ((), ())), preferr...  24.1 us
    unnamed x40, local copies, waits for them, and re-layouts  23.2 us
    dot_general x12, matrix products, head_pass(): lax.dot_general(head_grad, head_value, (((1,), (1,)), ((), ())), preferre...  18.8 us
  transfers between devices with their start and end apart: 15, of which 13 were waited for; matrix products, arithmetic and copies ran while one was open for 9% of the time, Pallas kernels for 0%

commit v1 on v0

v1 whole, which is shorter than its diff:
```python
import functools
import math

import jax
import jax.numpy as jnp
from jax import lax
from jax.experimental import pallas as pl
from jax.experimental.pallas import tpu as pltpu
from jax.sharding import PartitionSpec as P

HEAD_DIM = 128
STEPS = 4
F32 = jnp.float32
BF16 = jnp.bfloat16


def rows_dot(a, b):
    return lax.dot_general(a, b, (((1,), (1,)), ((), ())), preferred_element_type=F32)


def cols_dot(a, b):
    return lax.dot_general(a, b, (((0,), (0,)), ((), ())), preferred_element_type=F32)


def attention_body(
    place, q_own, q_par, k_own, v_own, kv_par, near_own, near_par, far, t_k, t_v, g_own, g_par,
    od_own, od_par, d_own, d_par, d_near_own, d_near_par, d_far,
    k_all, v_all, dk_all, dv_all,
):
    tokens = q_own.shape[0]
    col = place[1]
    scale = 1.0 / math.sqrt(q_own.shape[1])
    to_log2 = scale * math.log2(math.e)

    def block(first, which):
        return pl.ds(pl.multiple_of((first + which) * tokens, tokens), tokens)

    at_far = pl.ds(0, tokens)
    at_near_own, at_near_par = block(1, col), block(1, 1 - col)
    at_own, at_par = block(3, col), block(3, 1 - col)
    k_all[at_far] = far[0]
    v_all[at_far] = far[1]
    k_all[at_near_own] = near_own[0]
    v_all[at_near_own] = near_own[1]
    k_all[at_near_par] = near_par[0]
    v_all[at_near_par] = near_par[1]
    k_all[at_own] = k_own[...]
    v_all[at_own] = v_own[...]
    k_all[at_par] = kv_par[0]
    v_all[at_par] = kv_par[1]
    dk_all[...] = jnp.zeros_like(dk_all)
    dv_all[...] = jnp.zeros_like(dv_all)

    def one(q_ref, g_ref, od_ref, first):
        window = pl.ds(pl.multiple_of(first * tokens, tokens), STEPS * tokens)
        q = q_ref[...]
        g = g_ref[...]
        s_t = rows_dot(q, t_k[...])
        s_i = rows_dot(q, k_all[window])
        peak = jnp.maximum(jnp.max(s_t, axis=1, keepdims=True), jnp.max(s_i, axis=1, keepdims=True))
        e_t = jnp.exp2((s_t - peak) * to_log2)
        e_i = jnp.exp2((s_i - peak) * to_log2)
        total = jnp.sum(e_t, axis=1, keepdims=True) + jnp.sum(e_i, axis=1, keepdims=True)
        inverse = 1.0 / total
        p_t = e_t * inverse
        p_i = e_i * inverse
        low_t = p_t.astype(BF16)
        low_i = p_i.astype(BF16)
        out = jnp.dot(low_t, t_v[...], preferred_element_type=F32)
        out += jnp.dot(low_i, v_all[window], preferred_element_type=F32)
        out = out.astype(BF16)
        od_ref[0] = out
        delta = jnp.sum(g.astype(F32) * out.astype(F32), axis=1, keepdims=True)
        ds_t = (p_t * ((rows_dot(g, t_v[...]) - delta) * scale)).astype(BF16)
        ds_i = (p_i * ((rows_dot(g, v_all[window]) - delta) * scale)).astype(BF16)
        dq = jnp.dot(ds_t, t_k[...], preferred_element_type=F32)
        dq += jnp.dot(ds_i, k_all[window], preferred_element_type=F32)
        od_ref[1] = dq.astype(BF16)
        dk_all[window] += cols_dot(ds_i, q)
        dv_all[window] += cols_dot(low_i, g)

    one(q_own, g_own, od_own, col)
    one(q_par, g_par, od_par, 1 - col)
    for ref, rows in (
        (d_own, at_own), (d_par, at_par), (d_near_own, at_near_own), (d_near_par, at_near_par), (d_far, at_far),
    ):
        ref[0] = dk_all[rows].astype(BF16)
        ref[1] = dv_all[rows].astype(BF16)


def attention(place, q, q_par, k, v, kv_par, near_own, near_par, far, t_k, t_v, g_own, g_par):
    tokens = q.shape[0]
    width = q_par.shape[1]
    text = t_k.shape[0]
    heads = width // HEAD_DIM
    whole = lambda rows: pl.BlockSpec((rows, HEAD_DIM), lambda h, place: (0, place[0] * heads + h))
    part = pl.BlockSpec((tokens, HEAD_DIM), lambda h, place: (0, h))
    double = pl.BlockSpec((2, tokens, HEAD_DIM), lambda h, place: (0, 0, h))
    keys = text + STEPS * tokens
    macs = heads * 2 * tokens * HEAD_DIM * (4 * keys + 2 * STEPS * tokens)
    out = jax.ShapeDtypeStruct((2, tokens, width), BF16)
    image_rows = (STEPS + 1) * tokens
    return pl.pallas_call(
        attention_body,
        out_shape=(out,) * 7,
        grid_spec=pltpu.PrefetchScalarGridSpec(
            num_scalar_prefetch=1,
            grid=(heads,),
            in_specs=[whole(tokens), part, whole(tokens), whole(tokens), double, double, double, double,
                      whole(text), whole(text), part, part],
            out_specs=[double] * 7,
            scratch_shapes=[
                pltpu.VMEM((image_rows, HEAD_DIM), BF16),
                pltpu.VMEM((image_rows, HEAD_DIM), BF16),
                pltpu.VMEM((image_rows, HEAD_DIM), F32),
                pltpu.VMEM((image_rows, HEAD_DIM), F32),
            ],
        ),
        compiler_params=pltpu.CompilerParams(vmem_limit_bytes=48 * 1024 * 1024),
        cost_estimate=pl.CostEstimate(
            flops=4 * macs, bytes_accessed=24 * tokens * width * 2, transcendentals=heads * 2 * tokens * keys
        ),
        name="attention",
    )(place, q, q_par, k, v, kv_par, near_own, near_par, far, t_k, t_v, g_own, g_par)


def per_device(image_query, image_key, image_value, text_key, text_value, out_weight, cotangent):
    q, k, v = image_query[0], image_key[0], image_value[0]
    t_k, t_v = text_key[0], text_value[0]
    cot = cotangent[0]
    shards = lax.axis_size("fsdp")
    blocks = lax.axis_size("seq")
    pairs = blocks // 2
    groups = shards // 2
    width = out_weight.shape[0]
    tokens = q.shape[0]
    f, s = lax.axis_index("fsdp"), lax.axis_index("seq")
    col, core, row = s % 2, f % 2, f // 2

    def shift(a, axis, by):
        n = lax.axis_size(axis)
        return lax.ppermute(a, axis, [(i, (i + by) % n) for i in range(n)])

    def swap(a, axis):
        return lax.ppermute(a, axis, [(i, i ^ 1) for i in range(lax.axis_size(axis))])

    shard = [((row + 1 + g) % groups) * 2 + col for g in range(groups)]
    other = [((row + 1 + g) % groups) * 2 + 1 - col for g in range(groups)]

    def cut(a, index):
        return lax.dynamic_slice_in_dim(a, index * width, width, 1)

    def cut_two(index):
        return jnp.stack([cut(k, index), cut(v, index)])

    near_own, near_par, far, kv_par, q_par = [], [], [], [], []
    for g in range(groups):
        near_own.append(shift(cut_two(shard[g]), "seq", 2))
        kv_par.append(swap(cut_two(other[g]), "seq"))
        near_par.append(shift(kv_par[g], "seq", 2))
        far.append(shift(jnp.where(col == 0, near_par[g], near_own[g]), "seq", 2))
        q_par.append(swap(cut(q, other[g]), "seq"))
    cot_par = swap(cot, "seq")

    held = [shift(out_weight, "fsdp", -2 * (1 + g)) if g < groups - 1 else out_weight for g in range(groups)]
    weight = []
    for g in range(groups):
        from_core = swap(held[g], "fsdp")
        weight.append((jnp.where(core == col, held[g], from_core), jnp.where(core == col, from_core, held[g])))

    own_od, par_od, own_d, weight_terms = [], [], [], []
    for g in range(groups):
        g_own = rows_dot(cot, weight[g][0]).astype(BF16)
        g_par = rows_dot(cot_par, weight[g][0]).astype(BF16)
        place = jnp.stack([shard[g], col]).astype(jnp.int32)
        od_own, od_par, d_own, d_par, d_near_own, d_near_par, d_far = attention(
            place, q, q_par[g], k, v, kv_par[g], near_own[g], near_par[g], far[g], t_k, t_v, g_own, g_par
        )
        own_od.append(od_own)
        par_od.append(swap(od_par, "seq"))
        back = shift(d_far, "seq", -2).astype(F32)
        near_p = (d_near_par.astype(F32) + jnp.where(col == 0, back, 0.0)).astype(BF16)
        near_o = (d_near_own.astype(F32) + jnp.where(col == 1, back, 0.0)).astype(BF16)
        sum_p = (d_par.astype(F32) + shift(near_p, "seq", -2).astype(F32)).astype(BF16)
        from_par = swap(sum_p, "seq")
        sum_o = (d_own.astype(F32) + shift(near_o, "seq", -2).astype(F32)).astype(BF16)
        own_d.append((sum_o, from_par))
        weight_terms.append(cols_dot(od_own[0], cot) + cols_dot(od_par[0], cot_par))

    rel_out = jnp.concatenate([p for g in range(groups) for p in (own_od[g][0], par_od[g][0])], axis=1)
    rel_weight = jnp.concatenate([p for g in range(groups) for p in weight[g]], axis=0)
    image_out = jnp.dot(rel_out, rel_weight, preferred_element_type=F32).astype(BF16)

    total = None
    rows = width // blocks
    for g in range(groups):
        terms = weight_terms[g].reshape(pairs, 2, rows, -1)
        keep = lax.dynamic_index_in_dim(terms, core, 1, keepdims=False)
        give = lax.dynamic_index_in_dim(terms, 1 - core, 1, keepdims=False).astype(BF16)
        both = keep + swap(give, "fsdp").astype(F32)
        if g < groups - 1:
            both = shift(both.astype(BF16), "fsdp", 2 * (1 + g)).astype(F32)
        total = both if total is None else total + both
    z = s // 2
    mine = lax.dynamic_index_in_dim(total, z, 0, keepdims=False)
    total = total.astype(BF16)
    for by in range(1, pairs):
        there = lax.dynamic_index_in_dim(total, (z + by) % pairs, 0, keepdims=False)
        mine = mine + shift(there, "seq", 2 * by).astype(F32)
    n = blocks * shards

    def mirror(i):
        ss, ff = divmod(i, shards)
        return (ss - ss % 2 + ff % 2) * shards + ff - ff % 2 + ss % 2

    crossed = lax.ppermute(mine.astype(BF16), ("seq", "fsdp"), [(i, mirror(i)) for i in range(n)])
    grad_weight = jnp.where(core == col, mine, crossed.astype(F32))

    def assemble(pieces):
        whole = jnp.zeros((tokens, width * shards), BF16)
        for g in range(groups):
            whole = lax.dynamic_update_slice_in_dim(whole, pieces[g][0], shard[g] * width, 1)
            whole = lax.dynamic_update_slice_in_dim(whole, pieces[g][1], other[g] * width, 1)
        return whole

    grad_q = assemble([(own_od[g][1], par_od[g][1]) for g in range(groups)])
    grad_k = assemble([(own_d[g][0][0], own_d[g][1][0]) for g in range(groups)])
    grad_v = assemble([(own_d[g][0][1], own_d[g][1][1]) for g in range(groups)])
    return image_out[None], grad_q[None], grad_k[None], grad_v[None], grad_weight


def solution(mesh):
    in_specs = (
        P("fsdp", "seq", None),
        P("fsdp", "seq", None),
        P("fsdp", "seq", None),
        P("fsdp", None, None),
        P("fsdp", None, None),
        P("fsdp", None),
        P("fsdp", "seq", None),
    )
    out_specs = (
        P("fsdp", "seq", None),
        P("fsdp", "seq", None),
        P("fsdp", "seq", None),
        P("fsdp", "seq", None),
        P(("fsdp", "seq"), None),
    )
    return jax.shard_map(
        per_device, mesh=mesh, in_specs=in_specs, out_specs=out_specs, check_vma=False
    )
```

time: 561 us -> 180 us (0.32)
  waiting for transfers between devices: 300 us -> 94.3 us
  matrix products: 143 us -> 6.58 us
  local copies, waits for them, and re-layouts: 42.4 us -> 6.84 us
  Pallas kernels: 0 us -> 25 us
  other arithmetic: 29 us -> 8.57 us
  between operations: 13.9 us -> 1.03 us
  starting transfers between devices: 28.1 us -> 34 us
    ppermute x12 -> x31, waiting for transfers between devices: 265 us -> 94.3 us  [the longest x17 68.9 us: shift(): return lax.ppermute(a, axis, [(i, (i + by) % n) for i in range(n)])]
    dot_general x75 -> x9, matrix products: 143 us -> 6.58 us  [the longest x4 2.34 us: rows_dot(): lax.dot_general(a, b, (((1,), (1,)), ((), ())), preferred_element_type=F32)]
    reduce_scatter x2 -> x0, waiting for transfers between devices: 34.1 us -> none  [the longest x1 34.1 us: per_device(): lax.psum_scatter(weight_rows, 'seq', scatter_dimension=0, tiled=True)]
    pallas_call x0 -> x2, Pallas kernels: none -> 25 us  [attention(): pl.pallas_call(attention_body, out_shape=(out,) * 7, grid_spec=pltpu.Pref...]
    unnamed x40 -> x18, local copies, waits for them, and re-layouts: 23.2 us -> 0.7 us
    reduce_sum x24 -> x0, other arithmetic: 14.9 us -> none  [the longest x12 10.5 us: head_pass(): jnp.sum(head_grad.astype(jnp.float32) * attended.astype(jnp.float32), axi...]
    slice x2 -> x0, local copies, waits for them, and re-layouts: 7.99 us -> none  [the longest x1 4.92 us: block_part(): grad_v[first_row:first_row + tokens]]
    add x4 -> x0, other arithmetic: 7.82 us -> none  [per_device(): carried = (carried[0] + own_part[0], carried[1] + own_part[1])]
  transfers between devices with their start and end apart: 15 -> 31, of which waited for: 13 -> 13; matrix products, arithmetic and copies ran while one was open for 9% -> 12% of each run, Pallas kernels for 0% -> 14%
where the time goes in v1:
time: 180 us; the launch traced here: 176 us
  waiting for transfers between devices  94.3 us (52%)
  starting transfers between devices  34 us (19%)
  Pallas kernels  25 us (14%)
  other arithmetic  8.57 us (5%)
  local copies, waits for them, and re-layouts  6.84 us (4%)
  matrix products  6.58 us (4%)
    ppermute x17, waiting for transfers between devices, shift(): return lax.ppermute(a, axis, [(i, (i + by) % n) for i in range(n)])  68.9 us
    ppermute x13, waiting for transfers between devices, swap(): lax.ppermute(a, axis, [(i, i ^ 1) for i in range(lax.axis_size(axis))])  25.4 us
    pallas_call x2, Pallas kernels, attention(): pl.pallas_call(attention_body, out_shape=(out,) * 7, grid_spec=pltpu.Pref...  25 us
    ppermute x17, starting transfers between devices, shift(): return lax.ppermute(a, axis, [(i, (i + by) % n) for i in range(n)])  19.9 us
    ppermute x13, starting transfers between devices, swap(): lax.ppermute(a, axis, [(i, i ^ 1) for i in range(lax.axis_size(axis))])  13.4 us
    select_n x2, other arithmetic, per_device(): jnp.where(core == col, held[g], from_core)  4.29 us
  transfers between devices with their start and end apart: 31, of which 13 were waited for; matrix products, arithmetic and copies ran while one was open for 12% of the time, Pallas kernels for 14%

profile of v1, /device:TPU:0, one launch (start us, length us, event | category | flops | bytes accessed | tf_op | source)
XLA Modules:
  0.0 176.3 jit_solution(11035612825154896428)
XLA Ops:
  1.2 2.4 %constant_dynamic-slice_fusion.4 = (bf16[1,256,384]{2,1,0:T(8,128)(2,1)S(1)}, bf16[1,256,384]{2,1,0:T(8,128)(2,1)S(1)}, bf16[1,256,384]{2,1,0:T(8,128)(2,1)S(1)}...) fusion(bf16[1,256,1536]{2,1,0:T(8,128)(2,1)} %param.9, ...), kind=kLoop, calls=%fused_computation.96 | loop fusion | bytes 3145744 | tf_op jit(solution)/shard_map/dynamic_slice | solution.py:151
  3.6 2.7 %collective-permute-start.10 = (bf16[2,256,384]{2,1,0:T(8,128)(2,1)S(1)}, bf16[2,256,384]{2,1,0:T(8,128)(2,1)S(1)}, u32[]{:S(2)}, u32[]{:S(2)}) collective-permute-start(bf16[2,256,384]{2,1,0:T(8,128)(2,1)S(1)} %pad_maximum_fusion.2), channel_id=1, source_target_pairs={{0,4},{4,0},{8,12},{12,8},{16,20},{20,16},{24,28},{28,24},{1,5},{5... | collective-permute-start | bytes 1179656 | tf_op jit(solution)/shard_map/ppermute | solution.py:145
  9.9 1.6 collective-permute-start.11
  11.5 4.7 %collective-permute-done.10.kv_par = bf16[2,256,384]{2,1,0:T(8,128)(2,1)S(1)} collective-permute-done((bf16[2,256,384]{2,1,0:T(8,128)(2,1)S(1)}, bf16[2,256,384]{2,1,0:T(8,128)(2,1)S(1)}, u32[]{:S(2)}, u32[]{:S(2)}) %collective-permute-start.10) | collective-permute-done | bytes 393248 | tf_op jit(solution)/shard_map/ppermute | solution.py:145
  16.2 2.1 %collective-permute-start.12 = (bf16[2,256,384]{2,1,0:T(8,128)(2,1)S(1)}, bf16[2,256,384]{2,1,0:T(8,128)(2,1)S(1)}, u32[]{:S(2)}, u32[]{:S(2)}) collective-permute-start(bf16[2,256,384]{2,1,0:T(8,128)(2,1)S(1)} %collective-permute-done.10.kv_par), channel_id=1, source_target_pairs={{0,8},{4,12},{8,16},{12,20},{16,24},{20,28},{24,0},{28,4},{1,9},{5... | collective-permute-start | bytes 1179656 | tf_op jit(solution)/shard_map/ppermute | solution.py:142
  19.5 4.5 %collective-permute-done.11.near_own = bf16[2,256,384]{2,1,0:T(8,128)(2,1)S(1)} collective-permute-done((bf16[2,256,384]{2,1,0:T(8,128)(2,1)}, bf16[2,256,384]{2,1,0:T(8,128)(2,1)S(1)}, u32[]{:S(2)}, u32[]{:S(2)}) %collective-permute-start.11) | collective-permute-done | bytes 393248 | tf_op jit(solution)/shard_map/ppermute | solution.py:142
  25.4 5.5 %collective-permute-done.12.near_par = bf16[2,256,384]{2,1,0:T(8,128)(2,1)S(1)} collective-permute-done((bf16[2,256,384]{2,1,0:T(8,128)(2,1)S(1)}, bf16[2,256,384]{2,1,0:T(8,128)(2,1)S(1)}, u32[]{:S(2)}, u32[]{:S(2)}) %collective-permute-start.12) | collective-permute-done | bytes 393248 | tf_op jit(solution)/shard_map/ppermute | solution.py:142
  32.6 2.9 %broadcast_select_fusion.2 = (bf16[384,1536]{1,0:T(8,128)(2,1)S(1)}, bf16[384,1536]{1,0:T(8,128)(2,1)}) fusion(bf16[384,1536]{1,0:T(8,128)(2,1)} %param.12, bf16[384,1536]{1,0:T(8,128)(2,1)} %collective-permute-done.14, pred[]{:T(512)S(6)} %eq.28), kind=kLoop, calls=%fused_computation.20 | loop fusion | flops 1179648 | bytes 4718593 | tf_op jit(solution)/shard_map/jit(_where)/select_n | solution.py:169
  36.0 13.1 %collective-permute-done.7 = bf16[256,1536]{1,0:T(8,128)(2,1)S(1)} collective-permute-done((bf16[256,1536]{1,0:T(8,128)(2,1)S(1)}, bf16[256,1536]{1,0:T(8,128)(2,1)S(1)}, u32[]{:S(2)}, u32[]{:S(2)}) %collective-permute-start.7) | collective-permute-done | bytes 786464 | tf_op jit(solution)/shard_map/ppermute | solution.py:145
  51.2 3.6 %collective-permute-done.9.q_par = bf16[256,384]{1,0:T(8,128)(2,1)S(1)} collective-permute-done((bf16[256,384]{1,0:T(8,128)(2,1)S(1)}, bf16[256,384]{1,0:T(8,128)(2,1)S(1)}, u32[]{:S(2)}, u32[]{:S(2)}) %collective-permute-start.9) | collective-permute-done | bytes 196640 | tf_op jit(solution)/shard_map/ppermute | solution.py:145
  56.1 12.5 %attention.3 = (bf16[2,256,384]{2,1,0:T(8,128)(2,1)S(1)}, bf16[2,256,384]{2,1,0:T(8,128)(2,1)S(1)}, bf16[2,256,384]{2,1,0:T(8,128)(2,1)S(1)}, bf16[2,256,384]{2,...) custom-call(s32[2]{0:T(128)S(1)} %pad_add_fusion.1.place, ...), custom_call_target="tpu_custom_call" | custom-call | flops 6442450944 | bytes 4718592 | tf_op jit(solution)/shard_map/attention/pallas_call | solution.py:103
  68.5 2.6 %collective-permute-start.20 = (bf16[2,256,384]{2,1,0:T(8,128)(2,1)S(1)}, bf16[2,256,384]{2,1,0:T(8,128)(2,1)S(1)}, u32[]{:S(2)}, u32[]{:S(2)}) collective-permute-start(bf16[2,256,384]{2,1,0:T(8,128)(2,1)S(1)} %get-tuple-element.30), channel_id=1, source_target_pairs={{0,24},{4,28},{8,0},{12,4},{16,8},{20,12},{24,16},{28,20},{1,25},{... | collective-permute-start | bytes 1179656 | tf_op jit(solution)/shard_map/ppermute | solution.py:142
  71.1 4.2 %collective-permute-done.3.near_par = bf16[2,256,384]{2,1,0:T(8,128)(2,1)S(1)} collective-permute-done((bf16[2,256,384]{2,1,0:T(8,128)(2,1)S(1)}, bf16[2,256,384]{2,1,0:T(8,128)(2,1)S(1)}, u32[]{:S(2)}, u32[]{:S(2)}) %collective-permute-start.3) | collective-permute-done | bytes 393248 | tf_op jit(solution)/shard_map/ppermute | solution.py:142
  76.2 7.6 %collective-permute-done.20 = bf16[2,256,384]{2,1,0:T(8,128)(2,1)S(1)} collective-permute-done((bf16[2,256,384]{2,1,0:T(8,128)(2,1)S(1)}, bf16[2,256,384]{2,1,0:T(8,128)(2,1)S(1)}, u32[]{:S(2)}, u32[]{:S(2)}) %collective-permute-start.20) | collective-permute-done | bytes 393248 | tf_op jit(solution)/shard_map/ppermute | solution.py:142
  86.9 12.4 %collective-permute-done.21 = bf16[2,256,384]{2,1,0:T(8,128)(2,1)S(1)} collective-permute-done((bf16[2,256,384]{2,1,0:T(8,128)(2,1)S(1)}, bf16[2,256,384]{2,1,0:T(8,128)(2,1)S(1)}, u32[]{:S(2)}, u32[]{:S(2)}) %collective-permute-start.21) | collective-permute-done | bytes 393248 | tf_op jit(solution)/shard_map/ppermute | solution.py:142
  100.9 5.5 %collective-permute-done.22 = bf16[2,256,384]{2,1,0:T(8,128)(2,1)S(1)} collective-permute-done((bf16[2,256,384]{2,1,0:T(8,128)(2,1)S(1)}, bf16[2,256,384]{2,1,0:T(8,128)(2,1)S(1)}, u32[]{:S(2)}, u32[]{:S(2)}) %collective-permute-start.22) | collective-permute-done | bytes 393248 | tf_op jit(solution)/shard_map/ppermute | solution.py:142
  110.7 12.5 %attention.2 = (bf16[2,256,384]{2,1,0:T(8,128)(2,1)S(1)}, bf16[2,256,384]{2,1,0:T(8,128)(2,1)S(1)}, bf16[2,256,384]{2,1,0:T(8,128)(2,1)S(1)}, bf16[2,256,384]{2,...) custom-call(s32[2]{0:T(128)S(1)} %pad_add_fusion.place, ...), custom_call_target="tpu_custom_call" | custom-call | flops 6442450944 | bytes 4718592 | tf_op jit(solution)/shard_map/attention/pallas_call | solution.py:103
  125.2 9.5 %collective-permute-done.16 = bf16[2,256,384]{2,1,0:T(8,128)(2,1)S(1)} collective-permute-done((bf16[2,256,384]{2,1,0:T(8,128)(2,1)S(1)}, bf16[2,256,384]{2,1,0:T(8,128)(2,1)S(1)}, u32[]{:S(2)}, u32[]{:S(2)}) %collective-permute-start.16) | collective-permute-done | bytes 393248 | tf_op jit(solution)/shard_map/ppermute | solution.py:142
  135.0 2.1 %collective-permute-start.17 = (bf16[2,256,384]{2,1,0:T(8,128)(2,1)S(1)}, bf16[2,256,384]{2,1,0:T(8,128)(2,1)S(1)}, u32[]{:S(2)}, u32[]{:S(2)}) collective-permute-start(bf16[2,256,384]{2,1,0:T(8,128)(2,1)S(1)} %get-tuple-element.61), channel_id=1, source_target_pairs={{0,24},{4,28},{8,0},{12,4},{16,8},{20,12},{24,16},{28,20},{1,25},{... | collective-permute-start | bytes 1179656 | tf_op jit(solution)/shard_map/ppermute | solution.py:142
  139.0 2.3 %fusion.11 = bf16[1,256,1536]{2,1,0:T(8,128)(2,1)} fusion(bf16[384,1536]{1,0:T(8,128)(2,1)S(1)} %copy-done.4, bf16[384,1536]{1,0:T(8,128)(2,1)S(1)} %copy-done.3, bf16[384,1536]{1,0:T(8,128)(2,1)S(1)} %get-tuple-element.36, bf16[384,1536]{1,0:T(8,128)(2,1)S(1)} %get-tuple-element.35, bf16[256,384]{1,0:T(8,128)(2,1)S(1)} %get-tuple-element.63, ...), kind=kOutput, calls=%fused_computation.11 | convolution fusion | flops 1230372864 | bytes 6291456 | tf_op jit(solution)/shard_map/dot_general | solution.py:192
  142.4 12.6 %collective-permute-done.18 = bf16[2,256,384]{2,1,0:T(8,128)(2,1)S(1)} collective-permute-done((bf16[2,256,384]{2,1,0:T(8,128)(2,1)S(1)}, bf16[2,256,384]{2,1,0:T(8,128)(2,1)S(1)}, u32[]{:S(2)}, u32[]{:S(2)}) %collective-permute-start.18) | collective-permute-done | bytes 393248 | tf_op jit(solution)/shard_map/ppermute | solution.py:142
  157.3 3.9 %collective-permute-start.29 = (bf16[48,1536]{1,0:T(8,128)(2,1)S(1)}, bf16[48,1536]{1,0:T(8,128)(2,1)S(1)}, u32[]{:S(2)}, u32[]{:S(2)}) collective-permute-start(bf16[48,1536]{1,0:T(8,128)(2,1)S(1)} %get-tuple-element.50), channel_id=1, source_target_pairs={{0,24},{4,28},{8,0},{12,4},{16,8},{20,12},{24,16},{28,20},{1,25},{... | collective-permute-start | bytes 442376 | tf_op jit(solution)/shard_map/ppermute | solution.py:142
  161.9 4.0 %collective-permute-done.19 = bf16[2,256,384]{2,1,0:T(8,128)(2,1)S(1)} collective-permute-done((bf16[2,256,384]{2,1,0:T(8,128)(2,1)S(1)}, bf16[2,256,384]{2,1,0:T(8,128)(2,1)S(1)}, u32[]{:S(2)}, u32[]{:S(2)}) %collective-permute-start.19) | collective-permute-done | bytes 393248 | tf_op jit(solution)/shard_map/ppermute | solution.py:145
  166.1 7.1 %collective-permute-done.28 = bf16[48,1536]{1,0:T(8,128)(2,1)S(1)} collective-permute-done((bf16[48,1536]{1,0:T(8,128)(2,1)S(1)}, bf16[48,1536]{1,0:T(8,128)(2,1)S(1)}, u32[]{:S(2)}, u32[]{:S(2)}) %collective-permute-start.28) | collective-permute-done | bytes 147488 | tf_op jit(solution)/shard_map/ppermute | solution.py:142
  (104 shorter events, 33.5 us)
Async XLA Ops:
  0.6 31.9 %collective-permute-start.14 = (bf16[384,1536]{1,0:T(8,128)(2,1)}, bf16[384,1536]{1,0:T(8,128)(2,1)}, u32[]{:S(2)}, u32[]{:S(2)}) collective-permute-start(bf16[384,1536]{1,0:T(8,128)(2,1)} %param.12), channel_id=1, source_target_pairs={{0,1},{1,0},{2,3},{3,2},{4,5},{5,4},{6,7},{7,6},{8,9},{9,8},{10,11... | collective-permute-start | bytes 3538952 | tf_op jit(solution)/shard_map/ppermute | solution.py:145
  3.6 12.6 %collective-permute-start.10 = (bf16[2,256,384]{2,1,0:T(8,128)(2,1)S(1)}, bf16[2,256,384]{2,1,0:T(8,128)(2,1)S(1)}, u32[]{:S(2)}, u32[]{:S(2)}) collective-permute-start(bf16[2,256,384]{2,1,0:T(8,128)(2,1)S(1)} %pad_maximum_fusion.2), channel_id=1, source_target_pairs={{0,4},{4,0},{8,12},{12,8},{16,20},{20,16},{24,28},{28,24},{1,5},{5... | collective-permute-start | bytes 1179656 | tf_op jit(solution)/shard_map/ppermute | solution.py:145
  6.3 69.5 %collective-permute-start.5 = (bf16[384,1536]{1,0:T(8,128)(2,1)}, bf16[384,1536]{1,0:T(8,128)(2,1)}, u32[]{:S(2)}, u32[]{:S(2)}) collective-permute-start(bf16[384,1536]{1,0:T(8,128)(2,1)} %param.12), channel_id=1, source_target_pairs={{0,2},{1,3},{2,0},{3,1},{4,6},{5,7},{6,4},{7,5},{8,10},{9,11},{10,... | collective-permute-start | bytes 3538952 | tf_op jit(solution)/shard_map/ppermute | solution.py:142
  8.6 102.1 %collective-permute-start = (bf16[256,384]{1,0:T(8,128)(2,1)}, bf16[256,384]{1,0:T(8,128)(2,1)S(1)}, u32[]{:S(2)}, u32[]{:S(2)}) collective-permute-start(bf16[256,384]{1,0:T(8,128)(2,1)} %get-tuple-element.47), channel_id=1, source_target_pairs={{0,4},{4,0},{8,12},{12,8},{16,20},{20,16},{24,28},{28,24},{1,5},{5... | collective-permute-start | bytes 589832 | tf_op jit(solution)/shard_map/ppermute | solution.py:145
  9.9 14.0 %collective-permute-start.11 = (bf16[2,256,384]{2,1,0:T(8,128)(2,1)}, bf16[2,256,384]{2,1,0:T(8,128)(2,1)S(1)}, u32[]{:S(2)}, u32[]{:S(2)}) collective-permute-start(bf16[2,256,384]{2,1,0:T(8,128)(2,1)} %pad_maximum_fusion.3), channel_id=1, source_target_pairs={{0,8},{4,12},{8,16},{12,20},{16,24},{20,28},{24,0},{28,4},{1,9},{5... | collective-permute-start | bytes 1179656 | tf_op jit(solution)/shard_map/ppermute | solution.py:142
  16.2 14.7 %collective-permute-start.12 = (bf16[2,256,384]{2,1,0:T(8,128)(2,1)S(1)}, bf16[2,256,384]{2,1,0:T(8,128)(2,1)S(1)}, u32[]{:S(2)}, u32[]{:S(2)}) collective-permute-start(bf16[2,256,384]{2,1,0:T(8,128)(2,1)S(1)} %collective-permute-done.10.kv_par), channel_id=1, source_target_pairs={{0,8},{4,12},{8,16},{12,20},{16,24},{20,28},{24,0},{28,4},{1,9},{5... | collective-permute-start | bytes 1179656 | tf_op jit(solution)/shard_map/ppermute | solution.py:142
  23.9 30.8 %collective-permute-start.1 = (bf16[2,256,384]{2,1,0:T(8,128)(2,1)S(1)}, bf16[2,256,384]{2,1,0:T(8,128)(2,1)S(1)}, u32[]{:S(2)}, u32[]{:S(2)}) collective-permute-start(bf16[2,256,384]{2,1,0:T(8,128)(2,1)S(1)} %pad_maximum_fusion), channel_id=1, source_target_pairs={{0,4},{4,0},{8,12},{12,8},{16,20},{20,16},{24,28},{28,24},{1,5},{5... | collective-permute-start | bytes 1179656 | tf_op jit(solution)/shard_map/ppermute | solution.py:145
  30.9 18.1 %collective-permute-start.7 = (bf16[256,1536]{1,0:T(8,128)(2,1)S(1)}, bf16[256,1536]{1,0:T(8,128)(2,1)S(1)}, u32[]{:S(2)}, u32[]{:S(2)}) collective-permute-start(bf16[256,1536]{1,0:T(8,128)(2,1)S(1)} %bitcast.96), channel_id=1, source_target_pairs={{0,4},{4,0},{8,12},{12,8},{16,20},{20,16},{24,28},{28,24},{1,5},{5... | collective-permute-start | bytes 2359304 | tf_op jit(solution)/shard_map/ppermute | solution.py:145
  32.5 23.6 %collective-permute-start.13 = (bf16[2,256,384]{2,1,0:T(8,128)(2,1)S(1)}, bf16[2,256,384]{2,1,0:T(8,128)(2,1)S(1)}, u32[]{:S(2)}, u32[]{:S(2)}) collective-permute-start(bf16[2,256,384]{2,1,0:T(8,128)(2,1)S(1)} %broadcast_select_fusion.4), channel_id=1, source_target_pairs={{0,8},{4,12},{8,16},{12,20},{16,24},{20,28},{24,0},{28,4},{1,9},{5... | collective-permute-start | bytes 1179656 | tf_op jit(solution)/shard_map/ppermute | solution.py:142
  54.7 16.4 %collective-permute-start.2 = (bf16[2,256,384]{2,1,0:T(8,128)(2,1)S(1)}, bf16[2,256,384]{2,1,0:T(8,128)(2,1)S(1)}, u32[]{:S(2)}, u32[]{:S(2)}) collective-permute-start(bf16[2,256,384]{2,1,0:T(8,128)(2,1)S(1)} %pad_maximum_fusion.1), channel_id=1, source_target_pairs={{0,8},{4,12},{8,16},{12,20},{16,24},{20,28},{24,0},{28,4},{1,9},{5... | collective-permute-start | bytes 1179656 | tf_op jit(solution)/shard_map/ppermute | solution.py:142
  54.7 20.6 %collective-permute-start.3 = (bf16[2,256,384]{2,1,0:T(8,128)(2,1)S(1)}, bf16[2,256,384]{2,1,0:T(8,128)(2,1)S(1)}, u32[]{:S(2)}, u32[]{:S(2)}) collective-permute-start(bf16[2,256,384]{2,1,0:T(8,128)(2,1)S(1)} %collective-permute-done.1.kv_par), channel_id=1, source_target_pairs={{0,8},{4,12},{8,16},{12,20},{16,24},{20,28},{24,0},{28,4},{1,9},{5... | collective-permute-start | bytes 1179656 | tf_op jit(solution)/shard_map/ppermute | solution.py:142
  68.5 15.3 %collective-permute-start.20 = (bf16[2,256,384]{2,1,0:T(8,128)(2,1)S(1)}, bf16[2,256,384]{2,1,0:T(8,128)(2,1)S(1)}, u32[]{:S(2)}, u32[]{:S(2)}) collective-permute-start(bf16[2,256,384]{2,1,0:T(8,128)(2,1)S(1)} %get-tuple-element.30), channel_id=1, source_target_pairs={{0,24},{4,28},{8,0},{12,4},{16,8},{20,12},{24,16},{28,20},{1,25},{... | collective-permute-start | bytes 1179656 | tf_op jit(solution)/shard_map/ppermute | solution.py:142
  75.4 35.3 %collective-permute-start.4 = (bf16[2,256,384]{2,1,0:T(8,128)(2,1)S(1)}, bf16[2,256,384]{2,1,0:T(8,128)(2,1)S(1)}, u32[]{:S(2)}, u32[]{:S(2)}) collective-permute-start(bf16[2,256,384]{2,1,0:T(8,128)(2,1)S(1)} %broadcast_select_fusion.5), channel_id=1, source_target_pairs={{0,8},{4,12},{8,16},{12,20},{16,24},{20,28},{24,0},{28,4},{1,9},{5... | collective-permute-start | bytes 1179656 | tf_op jit(solution)/shard_map/ppermute | solution.py:142
  75.8 30.8 %collective-permute-start.6 = (bf16[384,1536]{1,0:T(8,128)(2,1)}, bf16[384,1536]{1,0:T(8,128)(2,1)S(1)}, u32[]{:S(2)}, u32[]{:S(2)}) collective-permute-start(bf16[384,1536]{1,0:T(8,128)(2,1)} %collective-permute-done.5), channel_id=1, source_target_pairs={{0,1},{1,0},{2,3},{3,2},{4,5},{5,4},{6,7},{7,6},{8,9},{9,8},{10,11... | collective-permute-start | bytes 3538952 | tf_op jit(solution)/shard_map/ppermute | solution.py:145
  84.0 15.3 %collective-permute-start.21 = (bf16[2,256,384]{2,1,0:T(8,128)(2,1)S(1)}, bf16[2,256,384]{2,1,0:T(8,128)(2,1)S(1)}, u32[]{:S(2)}, u32[]{:S(2)}) collective-permute-start(bf16[2,256,384]{2,1,0:T(8,128)(2,1)S(1)} %get-tuple-element.59), channel_id=1, source_target_pairs={{0,24},{4,28},{8,0},{12,4},{16,8},{20,12},{24,16},{28,20},{1,25},{... | collective-permute-start | bytes 1179656 | tf_op jit(solution)/shard_map/ppermute | solution.py:142
  85.8 20.6 %collective-permute-start.22 = (bf16[2,256,384]{2,1,0:T(8,128)(2,1)S(1)}, bf16[2,256,384]{2,1,0:T(8,128)(2,1)S(1)}, u32[]{:S(2)}, u32[]{:S(2)}) collective-permute-start(bf16[2,256,384]{2,1,0:T(8,128)(2,1)S(1)} %get-tuple-element.58), channel_id=1, source_target_pairs={{0,24},{4,28},{8,0},{12,4},{16,8},{20,12},{24,16},{28,20},{1,25},{... | collective-permute-start | bytes 1179656 | tf_op jit(solution)/shard_map/ppermute | solution.py:142
  99.3 37.9 %collective-permute-start.15 = (bf16[2,256,384]{2,1,0:T(8,128)(2,1)S(1)}, bf16[2,256,384]{2,1,0:T(8,128)(2,1)}, u32[]{:S(2)}, u32[]{:S(2)}) collective-permute-start(bf16[2,256,384]{2,1,0:T(8,128)(2,1)S(1)} %get-tuple-element.22), channel_id=1, source_target_pairs={{0,4},{4,0},{8,12},{12,8},{16,20},{20,16},{24,28},{28,24},{1,5},{5... | collective-permute-start | bytes 1179656 | tf_op jit(solution)/shard_map/ppermute | solution.py:145
  106.4 50.6 %collective-permute-start.26 = (bf16[4,48,1536]{2,1,0:T(8,128)(2,1)S(1)}, bf16[4,48,1536]{2,1,0:T(8,128)(2,1)S(1)}, u32[]{:S(2)}, u32[]{:S(2)}) collective-permute-start(bf16[4,48,1536]{2,1,0:T(8,128)(2,1)S(1)} %fusion.36), channel_id=1, source_target_pairs={{0,1},{1,0},{2,3},{3,2},{4,5},{5,4},{6,7},{7,6},{8,9},{9,8},{10,11... | collective-permute-start | bytes 1769480 | tf_op jit(solution)/shard_map/ppermute | solution.py:145
  106.5 67.4 %collective-permute-start.23 = (bf16[2,256,384]{2,1,0:T(8,128)(2,1)S(1)}, bf16[2,256,384]{2,1,0:T(8,128)(2,1)}, u32[]{:S(2)}, u32[]{:S(2)}) collective-permute-start(bf16[2,256,384]{2,1,0:T(8,128)(2,1)S(1)} %add_convert_fusion), channel_id=1, source_target_pairs={{0,4},{4,0},{8,12},{12,8},{16,20},{20,16},{24,28},{28,24},{1,5},{5... | collective-permute-start | bytes 1179656 | tf_op jit(solution)/shard_map/ppermute | solution.py:145
  135.0 21.7 %collective-permute-start.17 = (bf16[2,256,384]{2,1,0:T(8,128)(2,1)S(1)}, bf16[2,256,384]{2,1,0:T(8,128)(2,1)S(1)}, u32[]{:S(2)}, u32[]{:S(2)}) collective-permute-start(bf16[2,256,384]{2,1,0:T(8,128)(2,1)S(1)} %get-tuple-element.61), channel_id=1, source_target_pairs={{0,24},{4,28},{8,0},{12,4},{16,8},{20,12},{24,16},{28,20},{1,25},{... | collective-permute-start | bytes 1179656 | tf_op jit(solution)/shard_map/ppermute | solution.py:142
  137.3 17.7 %collective-permute-start.18 = (bf16[2,256,384]{2,1,0:T(8,128)(2,1)S(1)}, bf16[2,256,384]{2,1,0:T(8,128)(2,1)S(1)}, u32[]{:S(2)}, u32[]{:S(2)}) collective-permute-start(bf16[2,256,384]{2,1,0:T(8,128)(2,1)S(1)} %get-tuple-element.60), channel_id=1, source_target_pairs={{0,24},{4,28},{8,0},{12,4},{16,8},{20,12},{24,16},{28,20},{1,25},{... | collective-permute-start | bytes 1179656 | tf_op jit(solution)/shard_map/ppermute | solution.py:142
  141.4 15.6 %collective-permute-start.25 = (bf16[4,48,1536]{2,1,0:T(8,128)(2,1)S(1)}, bf16[4,48,1536]{2,1,0:T(8,128)(2,1)S(1)}, u32[]{:S(2)}, u32[]{:S(2)}) collective-permute-start(bf16[4,48,1536]{2,1,0:T(8,128)(2,1)S(1)} %fusion.15), channel_id=1, source_target_pairs={{0,2},{1,3},{2,0},{3,1},{4,6},{5,7},{6,4},{7,5},{8,10},{9,11},{10,... | collective-permute-start | bytes 1769480 | tf_op jit(solution)/shard_map/ppermute | solution.py:142
  161.2 11.9 %collective-permute-start.28 = (bf16[48,1536]{1,0:T(8,128)(2,1)S(1)}, bf16[48,1536]{1,0:T(8,128)(2,1)S(1)}, u32[]{:S(2)}, u32[]{:S(2)}) collective-permute-start(bf16[48,1536]{1,0:T(8,128)(2,1)S(1)} %get-tuple-element.51), channel_id=1, source_target_pairs={{0,16},{4,20},{8,24},{12,28},{16,0},{20,4},{24,8},{28,12},{1,17},{... | collective-permute-start | bytes 442376 | tf_op jit(solution)/shard_map/ppermute | solution.py:142
  161.2 11.9 %collective-permute-start.27 = (bf16[48,1536]{1,0:T(8,128)(2,1)S(1)}, bf16[48,1536]{1,0:T(8,128)(2,1)S(1)}, u32[]{:S(2)}, u32[]{:S(2)}) collective-permute-start(bf16[48,1536]{1,0:T(8,128)(2,1)S(1)} %get-tuple-element.49), channel_id=1, source_target_pairs={{0,8},{4,12},{8,16},{12,20},{16,24},{20,28},{24,0},{28,4},{1,9},{5... | collective-permute-start | bytes 442376 | tf_op jit(solution)/shard_map/ppermute | solution.py:142
  (16 other events, 122.3 us)

commit v2 on v1

--- a/solution.py
+++ b/solution.py
@@ -24,7 +24,7 @@
 
 def attention_body(
     place, q_own, q_par, k_own, v_own, kv_par, near_own, near_par, far, t_k, t_v, g_own, g_par,
-    od_own, od_par, d_own, d_par, d_near_own, d_near_par, d_far,
+    od_own, od_par, d_a, d_b, d_near_a, d_near_b, d_far,
     k_all, v_all, dk_all, dv_all,
 ):
     tokens = q_own.shape[0]
@@ -81,9 +81,8 @@
 
     one(q_own, g_own, od_own, col)
     one(q_par, g_par, od_par, 1 - col)
-    for ref, rows in (
-        (d_own, at_own), (d_par, at_par), (d_near_own, at_near_own), (d_near_par, at_near_par), (d_far, at_far),
-    ):
+    for place_at, ref in enumerate((d_far, d_near_a, d_near_b, d_a, d_b)):
+        rows = pl.ds(place_at * tokens, tokens)
         ref[0] = dk_all[rows].astype(BF16)
         ref[1] = dv_all[rows].astype(BF16)
 
@@ -147,66 +146,109 @@
     shard = [((row + 1 + g) % groups) * 2 + col for g in range(groups)]
     other = [((row + 1 + g) % groups) * 2 + 1 - col for g in range(groups)]
 
+    def after(operands, *others):
+        return lax.optimization_barrier((tuple(operands), others))[0]
+
+    every = range(groups)
+    last = groups - 1
+
     def cut(a, index):
         return lax.dynamic_slice_in_dim(a, index * width, width, 1)
 
     def cut_two(index):
         return jnp.stack([cut(k, index), cut(v, index)])
 
-    near_own, near_par, far, kv_par, q_par = [], [], [], [], []
-    for g in range(groups):
-        near_own.append(shift(cut_two(shard[g]), "seq", 2))
-        kv_par.append(swap(cut_two(other[g]), "seq"))
-        near_par.append(shift(kv_par[g], "seq", 2))
+    half = tokens // 2
+    near_own = [shift(cut_two(shard[g]), "seq", 2) for g in every]
+    kv_par = [swap(cut_two(other[g]), "seq") for g in every]
+    held = [shift(out_weight, "fsdp", -2 * (1 + g)) if g < last else out_weight for g in every]
+    cot_par, near_par, far, q_par = [], [], [], []
+    for g in every:
+        kv, = after([kv_par[g]], near_own[g])
+        near_par.append(shift(kv, "seq", 2))
+        if g < 2:
+            c, = after([cot[g * half : (g + 1) * half]], kv_par[g])
+            cot_par.append(swap(c, "seq"))
+    for g in every:
         far.append(shift(jnp.where(col == 0, near_par[g], near_own[g]), "seq", 2))
-        q_par.append(swap(cut(q, other[g]), "seq"))
-    cot_par = swap(cot, "seq")
-
-    held = [shift(out_weight, "fsdp", -2 * (1 + g)) if g < groups - 1 else out_weight for g in range(groups)]
+        c, = after([cut(q, other[g])], cot_par[min(g, 1)], *held[:last])
+        q_par.append(swap(c, "seq"))
+    cot_par = jnp.concatenate(cot_par, axis=0)
+
     weight = []
-    for g in range(groups):
+    for g in every:
         from_core = swap(held[g], "fsdp")
         weight.append((jnp.where(core == col, held[g], from_core), jnp.where(core == col, from_core, held[g])))
 
-    own_od, par_od, own_d, weight_terms = [], [], [], []
-    for g in range(groups):
+    rows = width // blocks
+
+    def terms_of(od_own, od_par):
+        terms = cols_dot(od_own[0], cot) + cols_dot(od_par[0], cot_par)
+        terms = terms.reshape(pairs, 2, rows, -1)
+        keep = lax.dynamic_index_in_dim(terms, core, 1, keepdims=False)
+        give = lax.dynamic_index_in_dim(terms, 1 - core, 1, keepdims=False).astype(BF16)
+        return keep, give
+
+    def add(a, b):
+        return (a.astype(F32) + b.astype(F32)).astype(BF16)
+
+    def run(g, others):
         g_own = rows_dot(cot, weight[g][0]).astype(BF16)
         g_par = rows_dot(cot_par, weight[g][0]).astype(BF16)
         place = jnp.stack([shard[g], col]).astype(jnp.int32)
-        od_own, od_par, d_own, d_par, d_near_own, d_near_par, d_far = attention(
+        g_own, g_par = after([g_own, g_par], *others)
+        return attention(
             place, q, q_par[g], k, v, kv_par[g], near_own[g], near_par[g], far[g], t_k, t_v, g_own, g_par
         )
+
+    own_od, par_od, own_d, total = [], [], [], None
+    waited = ()
+    for g in every:
+        od_own, od_par, d_a, d_b, d_near_a, d_near_b, d_far = run(g, waited)
         own_od.append(od_own)
-        par_od.append(swap(od_par, "seq"))
-        back = shift(d_far, "seq", -2).astype(F32)
-        near_p = (d_near_par.astype(F32) + jnp.where(col == 0, back, 0.0)).astype(BF16)
-        near_o = (d_near_own.astype(F32) + jnp.where(col == 1, back, 0.0)).astype(BF16)
-        sum_p = (d_par.astype(F32) + shift(near_p, "seq", -2).astype(F32)).astype(BF16)
-        from_par = swap(sum_p, "seq")
-        sum_o = (d_own.astype(F32) + shift(near_o, "seq", -2).astype(F32)).astype(BF16)
-        own_d.append((sum_o, from_par))
-        weight_terms.append(cols_dot(od_own[0], cot) + cols_dot(od_par[0], cot_par))
+        if g < last:
+            back = shift(d_far, "seq", -2)
+            par_od.append(swap(od_par, "seq"))
+            keep, give = terms_of(od_own, od_par)
+            from_a = shift(d_near_a, "seq", -2)
+            from_b = shift(add(d_near_b, back), "seq", -2)
+            both = (keep + swap(give, "fsdp").astype(F32)).astype(BF16)
+            waited = (back, both)
+            both = shift(both, "fsdp", 2 * (1 + g)).astype(F32)
+            total = both if total is None else total + both
+            sum_a, sum_b = add(d_a, from_a), add(d_b, from_b)
+            sum_o, sum_p = jnp.where(col == 0, sum_a, sum_b), jnp.where(col == 0, sum_b, sum_a)
+            own_d.append((sum_o, swap(sum_p, "seq")))
+        else:
+            keep, give = terms_of(*after([od_own, od_par], from_b, total))
+            d_far, = after([d_far], from_a)
+            back = shift(d_far, "seq", -2)
+            par_od.append(swap(od_par, "seq"))
+            total = total + keep + swap(give, "fsdp").astype(F32)
+            z = s // 2
+            mine = lax.dynamic_index_in_dim(total, z, 0, keepdims=False)
+            total = total.astype(BF16)
+            pieces = []
+            for by in range(1, pairs):
+                there = lax.dynamic_index_in_dim(total, (z + by) % pairs, 0, keepdims=False)
+                pieces.append(shift(there, "seq", 2 * by))
+            near_b = add(d_near_b, back)
+            from_p = shift(jnp.where(col == 0, near_b, d_near_a), "seq", -2)
+            own, = after([jnp.where(col == 0, d_near_a, near_b)], from_p)
+            from_o = shift(own, "seq", -2)
+            sum_p = add(jnp.where(col == 0, d_b, d_a), from_p)
+            par_od = list(after(par_od, from_p))
+            for_own = swap(sum_p, "seq")
+            from_o, *pieces = after([from_o, *pieces], for_own)
+            sum_o = add(jnp.where(col == 0, d_a, d_b), from_o)
+            for piece in pieces:
+                mine = mine + piece.astype(F32)
+            own_d.append((sum_o, for_own))
 
     rel_out = jnp.concatenate([p for g in range(groups) for p in (own_od[g][0], par_od[g][0])], axis=1)
     rel_weight = jnp.concatenate([p for g in range(groups) for p in weight[g]], axis=0)
     image_out = jnp.dot(rel_out, rel_weight, preferred_element_type=F32).astype(BF16)
 
-    total = None
-    rows = width // blocks
-    for g in range(groups):
-        terms = weight_terms[g].reshape(pairs, 2, rows, -1)
-        keep = lax.dynamic_index_in_dim(terms, core, 1, keepdims=False)
-        give = lax.dynamic_index_in_dim(terms, 1 - core, 1, keepdims=False).astype(BF16)
-        both = keep + swap(give, "fsdp").astype(F32)
-        if g < groups - 1:
-            both = shift(both.astype(BF16), "fsdp", 2 * (1 + g)).astype(F32)
-        total = both if total is None else total + both
-    z = s // 2
-    mine = lax.dynamic_index_in_dim(total, z, 0, keepdims=False)
-    total = total.astype(BF16)
-    for by in range(1, pairs):
-        there = lax.dynamic_index_in_dim(total, (z + by) % pairs, 0, keepdims=False)
-        mine = mine + shift(there, "seq", 2 * by).astype(F32)
     n = blocks * shards
 
     def mirror(i):

time: 180 us -> 144 us (0.80)
  the two profiles are of different devices: /device:TPU:0 before, /device:TPU:25 now
where the time goes in v2:
time: 144 us; the launch traced here: 143 us
  waiting for transfers between devices  56.7 us (39%)
  starting transfers between devices  41.9 us (29%)
  Pallas kernels  25 us (17%)
  other arithmetic  7.83 us (5%)
  matrix products  6.61 us (5%)
  local copies, waits for them, and re-layouts  4.11 us (3%)
    ppermute x17, waiting for transfers between devices, shift(): return lax.ppermute(a, axis, [(i, (i + by) % n) for i in range(n)])  39 us
    pallas_call x2, Pallas kernels, attention(): pl.pallas_call(attention_body, out_shape=(out,) * 7, grid_spec=pltpu.Pref...  25 us
    ppermute x14, starting transfers between devices, swap(): lax.ppermute(a, axis, [(i, i ^ 1) for i in range(lax.axis_size(axis))])  18.4 us
    ppermute x17, starting transfers between devices, shift(): return lax.ppermute(a, axis, [(i, (i + by) % n) for i in range(n)])  15.5 us
    ppermute x14, waiting for transfers between devices, swap(): lax.ppermute(a, axis, [(i, i ^ 1) for i in range(lax.axis_size(axis))])  15.1 us
    ppermute x1, starting transfers between devices, per_device(): lax.ppermute(mine.astype(BF16), ('seq', 'fsdp'), [(i, mirror(i)) for i in...  7.98 us
    select_n x2, other arithmetic, per_device(): jnp.where(core == col, held[g], from_core)  5.32 us
  transfers between devices with their start and end apart: 32, of which 14 were waited for; matrix products, arithmetic and copies ran while one was open for 11% of the time, Pallas kernels for 17%

profile of v2, /device:TPU:25, one launch (start us, length us, event | category | flops | bytes accessed | tf_op | source)
XLA Modules:
  0.0 143.4 jit_solution(866018205502049187)
XLA Ops:
  6.6 5.9 %collective-permute-done.kv_par = bf16[2,256,384]{2,1,0:T(8,128)(2,1)S(1)} collective-permute-done((bf16[2,256,384]{2,1,0:T(8,128)(2,1)S(1)}, bf16[2,256,384]{2,1,0:T(8,128)(2,1)S(1)}, u32[]{:S(2)}, u32[]{:S(2)}) %collective-permute-start) | collective-permute-done | bytes 393248 | tf_op jit(solution)/shard_map/ppermute | solution.py:144
  13.6 1.8 %collective-permute-start.5 = (bf16[2,256,384]{2,1,0:T(8,128)(2,1)S(1)}, bf16[2,256,384]{2,1,0:T(8,128)(2,1)S(1)}, u32[]{:S(2)}, u32[]{:S(2)}) collective-permute-start(bf16[2,256,384]{2,1,0:T(8,128)(2,1)S(1)} %collective-permute-done.kv_par), channel_id=1, source_target_pairs={{0,8},{4,12},{8,16},{12,20},{16,24},{20,28},{24,0},{28,4},{1,9},{5... | collective-permute-start | bytes 1179656 | tf_op jit(solution)/shard_map/ppermute | solution.py:141
  16.2 4.8 %collective-permute-done.8.kv_par = bf16[2,256,384]{2,1,0:T(8,128)(2,1)S(1)} collective-permute-done((bf16[2,256,384]{2,1,0:T(8,128)(2,1)S(1)}, bf16[2,256,384]{2,1,0:T(8,128)(2,1)S(1)}, u32[]{:S(2)}, u32[]{:S(2)}) %collective-permute-start.8) | collective-permute-done | bytes 393248 | tf_op jit(solution)/shard_map/ppermute | solution.py:144
  24.5 4.7 %collective-permute-done.5.near_par = bf16[2,256,384]{2,1,0:T(8,128)(2,1)S(1)} collective-permute-done((bf16[2,256,384]{2,1,0:T(8,128)(2,1)S(1)}, bf16[2,256,384]{2,1,0:T(8,128)(2,1)S(1)}, u32[]{:S(2)}, u32[]{:S(2)}) %collective-permute-start.5) | collective-permute-done | bytes 393248 | tf_op jit(solution)/shard_map/ppermute | solution.py:141
  30.4 7.1 %collective-permute-done.13.near_par = bf16[2,256,384]{2,1,0:T(8,128)(2,1)S(1)} collective-permute-done((bf16[2,256,384]{2,1,0:T(8,128)(2,1)S(1)}, bf16[2,256,384]{2,1,0:T(8,128)(2,1)S(1)}, u32[]{:S(2)}, u32[]{:S(2)}) %collective-permute-start.13) | collective-permute-done | bytes 393248 | tf_op jit(solution)/shard_map/ppermute | solution.py:141
  37.4 2.1 %collective-permute-start.6 = (bf16[2,256,384]{2,1,0:T(8,128)(2,1)S(1)}, bf16[2,256,384]{2,1,0:T(8,128)(2,1)S(1)}, u32[]{:S(2)}, u32[]{:S(2)}) collective-permute-start(bf16[2,256,384]{2,1,0:T(8,128)(2,1)S(1)} %broadcast_select_fusion.9), channel_id=1, source_target_pairs={{0,8},{4,12},{8,16},{12,20},{16,24},{20,28},{24,0},{28,4},{1,9},{5... | collective-permute-start | bytes 1179656 | tf_op jit(solution)/shard_map/ppermute | solution.py:141
  39.7 3.6 %collective-permute-start.7 = (bf16[384,1536]{1,0:T(8,128)(2,1)}, bf16[384,1536]{1,0:T(8,128)(2,1)S(1)}, u32[]{:S(2)}, u32[]{:S(2)}) collective-permute-start(bf16[384,1536]{1,0:T(8,128)(2,1)} %collective-permute-done.2), channel_id=1, source_target_pairs={{0,1},{1,0},{2,3},{3,2},{4,5},{5,4},{6,7},{7,6},{8,9},{9,8},{10,11... | collective-permute-start | bytes 3538952 | tf_op jit(solution)/shard_map/ppermute | solution.py:144
  44.6 2.8 %broadcast_select_fusion.2 = (bf16[384,1536]{1,0:T(8,128)(2,1)S(1)}, bf16[384,1536]{1,0:T(8,128)(2,1)}) fusion(bf16[384,1536]{1,0:T(8,128)(2,1)} %param.12, bf16[384,1536]{1,0:T(8,128)(2,1)} %collective-permute-done.15, pred[]{:T(512)S(6)} %eq.28), kind=kLoop, calls=%fused_computation.20 | loop fusion | flops 1179648 | bytes 4718593 | tf_op jit(solution)/shard_map/jit(_where)/select_n | solution.py:181
  48.1 2.5 %broadcast_select_fusion.3 = (bf16[384,1536]{1,0:T(8,128)(2,1)S(1)}, bf16[384,1536]{1,0:T(8,128)(2,1)}) fusion(bf16[384,1536]{1,0:T(8,128)(2,1)} %collective-permute-done.2, bf16[384,1536]{1,0:T(8,128)(2,1)S(1)} %collective-permute-done.7, pred[]{:T(512)S(6)} %eq.28), kind=kLoop, calls=%fused_computation.21 | loop fusion | flops 1179648 | bytes 4718593 | tf_op jit(solution)/shard_map/jit(_where)/select_n | solution.py:181
  51.8 12.5 %attention.2 = (bf16[2,256,384]{2,1,0:T(8,128)(2,1)S(1)}, bf16[2,256,384]{2,1,0:T(8,128)(2,1)S(1)}, bf16[2,256,384]{2,1,0:T(8,128)(2,1)S(1)}, bf16[2,256,384]{2,...) custom-call(s32[2]{0:T(128)S(1)} %pad_add_fusion.place, ...), custom_call_target="tpu_custom_call" | custom-call | flops 6442450944 | bytes 4718592 | tf_op jit(solution)/shard_map/attention/pallas_call | solution.py:102
  64.3 1.7 %collective-permute-start.16 = (bf16[2,256,384]{2,1,0:T(8,128)(2,1)S(1)}, bf16[2,256,384]{2,1,0:T(8,128)(2,1)S(1)}, u32[]{:S(2)}, u32[]{:S(2)}) collective-permute-start(bf16[2,256,384]{2,1,0:T(8,128)(2,1)S(1)} %get-tuple-element.49), channel_id=1, source_target_pairs={{0,24},{4,28},{8,0},{12,4},{16,8},{20,12},{24,16},{28,20},{1,25},{... | collective-permute-start | bytes 1179656 | tf_op jit(solution)/shard_map/ppermute | solution.py:141
  70.0 4.9 %collective-permute-done.16 = bf16[2,256,384]{2,1,0:T(8,128)(2,1)S(1)} collective-permute-done((bf16[2,256,384]{2,1,0:T(8,128)(2,1)S(1)}, bf16[2,256,384]{2,1,0:T(8,128)(2,1)S(1)}, u32[]{:S(2)}, u32[]{:S(2)}) %collective-permute-start.16) | collective-permute-done | bytes 393248 | tf_op jit(solution)/shard_map/ppermute | solution.py:141
  78.1 12.5 %attention.3 = (bf16[2,256,384]{2,1,0:T(8,128)(2,1)S(1)}, bf16[2,256,384]{2,1,0:T(8,128)(2,1)S(1)}, bf16[2,256,384]{2,1,0:T(8,128)(2,1)S(1)}, bf16[2,256,384]{2,...) custom-call(s32[2]{0:T(128)S(1)} %pad_add_fusion.1.place, ...), custom_call_target="tpu_custom_call" | custom-call | flops 6442450944 | bytes 4718592 | tf_op jit(solution)/shard_map/attention/pallas_call | solution.py:102
  90.7 2.2 %collective-permute-done.22 = bf16[2,256,384]{2,1,0:T(8,128)(2,1)S(1)} collective-permute-done((bf16[2,256,384]{2,1,0:T(8,128)(2,1)S(1)}, bf16[2,256,384]{2,1,0:T(8,128)(2,1)S(1)}, u32[]{:S(2)}, u32[]{:S(2)}) %collective-permute-start.22) | collective-permute-done | bytes 393248 | tf_op jit(solution)/shard_map/ppermute | solution.py:141
  94.3 4.7 %collective-permute-start.26 = (bf16[4,48,1536]{2,1,0:T(8,128)(2,1)S(1)}, bf16[4,48,1536]{2,1,0:T(8,128)(2,1)S(1)}, u32[]{:S(2)}, u32[]{:S(2)}) collective-permute-start(bf16[4,48,1536]{2,1,0:T(8,128)(2,1)S(1)} %fusion.31), channel_id=1, source_target_pairs={{0,1},{1,0},{2,3},{3,2},{4,5},{5,4},{6,7},{7,6},{8,9},{9,8},{10,11... | collective-permute-start | bytes 1769480 | tf_op jit(solution)/shard_map/ppermute | solution.py:144
  99.3 3.9 %collective-permute-done.20 = bf16[2,256,384]{2,1,0:T(8,128)(2,1)S(1)} collective-permute-done((bf16[2,256,384]{2,1,0:T(8,128)(2,1)S(1)}, bf16[2,256,384]{2,1,0:T(8,128)(2,1)S(1)}, u32[]{:S(2)}, u32[]{:S(2)}) %collective-permute-start.20) | collective-permute-done | bytes 393248 | tf_op jit(solution)/shard_map/ppermute | solution.py:141
  103.9 3.3 %collective-permute-start.27 = (bf16[48,1536]{1,0:T(8,128)(2,1)S(1)}, bf16[48,1536]{1,0:T(8,128)(2,1)S(1)}, u32[]{:S(2)}, u32[]{:S(2)}) collective-permute-start(bf16[48,1536]{1,0:T(8,128)(2,1)S(1)} %get-tuple-element.97), channel_id=1, source_target_pairs={{0,8},{4,12},{8,16},{12,20},{16,24},{20,28},{24,0},{28,4},{1,9},{5... | collective-permute-start | bytes 442376 | tf_op jit(solution)/shard_map/ppermute | solution.py:141
  107.5 4.4 %collective-permute-done.18 = bf16[2,256,384]{2,1,0:T(8,128)(2,1)S(1)} collective-permute-done((bf16[2,256,384]{2,1,0:T(8,128)(2,1)S(1)}, bf16[2,256,384]{2,1,0:T(8,128)(2,1)S(1)}, u32[]{:S(2)}, u32[]{:S(2)}) %collective-permute-start.18) | collective-permute-done | bytes 393248 | tf_op jit(solution)/shard_map/ppermute | solution.py:144
  111.9 1.8 %collective-permute-done.21 = bf16[2,256,384]{2,1,0:T(8,128)(2,1)S(1)} collective-permute-done((bf16[2,256,384]{2,1,0:T(8,128)(2,1)S(1)}, bf16[2,256,384]{2,1,0:T(8,128)(2,1)S(1)}, u32[]{:S(2)}, u32[]{:S(2)}) %collective-permute-start.21) | collective-permute-done | bytes 393248 | tf_op jit(solution)/shard_map/ppermute | solution.py:141
  115.7 2.3 %fusion.11 = bf16[1,256,1536]{2,1,0:T(8,128)(2,1)} fusion(bf16[384,1536]{1,0:T(8,128)(2,1)S(1)} %copy-done.5, bf16[384,1536]{1,0:T(8,128)(2,1)S(1)} %copy-done.4, bf16[384,1536]{1,0:T(8,128)(2,1)S(1)} %copy-done.8, bf16[384,1536]{1,0:T(8,128)(2,1)S(1)} %copy-done.7, bf16[256,384]{1,0:T(8,128)(2,1)S(1)} %get-tuple-element.105, ...), kind=kOutput, calls=%fused_computation.11 | convolution fusion | flops 1230372864 | bytes 6291456 | tf_op jit(solution)/shard_map/dot_general | solution.py:250
  118.0 3.7 %collective-permute-done.28 = bf16[48,1536]{1,0:T(8,128)(2,1)S(1)} collective-permute-done((bf16[48,1536]{1,0:T(8,128)(2,1)S(1)}, bf16[48,1536]{1,0:T(8,128)(2,1)S(1)}, u32[]{:S(2)}, u32[]{:S(2)}) %collective-permute-start.28) | collective-permute-done | bytes 147488 | tf_op jit(solution)/shard_map/ppermute | solution.py:141
  122.8 8.7 %collective-permute-done.24 = bf16[2,256,384]{2,1,0:T(8,128)(2,1)S(1)} collective-permute-done((bf16[2,256,384]{2,1,0:T(8,128)(2,1)S(1)}, bf16[2,256,384]{2,1,0:T(8,128)(2,1)S(1)}, u32[]{:S(2)}, u32[]{:S(2)}) %collective-permute-start.24) | collective-permute-done | bytes 393248 | tf_op jit(solution)/shard_map/ppermute | solution.py:141
  131.8 8.0 %collective-permute-start.31 = (bf16[48,1536]{1,0:T(8,128)(2,1)S(1)}, bf16[48,1536]{1,0:T(8,128)(2,1)S(1)}, u32[]{:S(2)}, u32[]{:S(2)}) collective-permute-start(bf16[48,1536]{1,0:T(8,128)(2,1)S(1)} %fusion.41), channel_id=1, source_target_pairs={{0,0},{1,4},{2,2},{3,6},{4,1},{5,5},{6,3},{7,7},{8,8},{9,12},{10,1... | collective-permute-start | bytes 442376 | tf_op jit(solution)/shard_map/ppermute | solution.py:258
  140.0 2.6 %collective-permute-done.31 = bf16[48,1536]{1,0:T(8,128)(2,1)S(1)} collective-permute-done((bf16[48,1536]{1,0:T(8,128)(2,1)S(1)}, bf16[48,1536]{1,0:T(8,128)(2,1)S(1)}, u32[]{:S(2)}, u32[]{:S(2)}) %collective-permute-start.31) | collective-permute-done | bytes 147488 | tf_op jit(solution)/shard_map/ppermute | solution.py:258
  (114 shorter events, 29.7 us)
Async XLA Ops:
  2.4 10.2 %collective-permute-start = (bf16[2,256,384]{2,1,0:T(8,128)(2,1)S(1)}, bf16[2,256,384]{2,1,0:T(8,128)(2,1)S(1)}, u32[]{:S(2)}, u32[]{:S(2)}) collective-permute-start(bf16[2,256,384]{2,1,0:T(8,128)(2,1)S(1)} %pad_maximum_fusion), channel_id=1, source_target_pairs={{0,4},{4,0},{8,12},{12,8},{16,20},{20,16},{24,28},{28,24},{1,5},{5... | collective-permute-start | bytes 1179656 | tf_op jit(solution)/shard_map/ppermute | solution.py:144
  3.8 40.8 %collective-permute-start.15 = (bf16[384,1536]{1,0:T(8,128)(2,1)}, bf16[384,1536]{1,0:T(8,128)(2,1)}, u32[]{:S(2)}, u32[]{:S(2)}) collective-permute-start(bf16[384,1536]{1,0:T(8,128)(2,1)} %param.12), channel_id=1, source_target_pairs={{0,1},{1,0},{2,3},{3,2},{4,5},{5,4},{6,7},{7,6},{8,9},{9,8},{10,11... | collective-permute-start | bytes 3538952 | tf_op jit(solution)/shard_map/ppermute | solution.py:144
  5.0 34.7 %collective-permute-start.2 = (bf16[384,1536]{1,0:T(8,128)(2,1)}, bf16[384,1536]{1,0:T(8,128)(2,1)}, u32[]{:S(2)}, u32[]{:S(2)}) collective-permute-start(bf16[384,1536]{1,0:T(8,128)(2,1)} %param.12), channel_id=1, source_target_pairs={{0,2},{1,3},{2,0},{3,1},{4,6},{5,7},{6,4},{7,5},{8,10},{9,11},{10,... | collective-permute-start | bytes 3538952 | tf_op jit(solution)/shard_map/ppermute | solution.py:141
  6.3 14.7 %collective-permute-start.8 = (bf16[2,256,384]{2,1,0:T(8,128)(2,1)S(1)}, bf16[2,256,384]{2,1,0:T(8,128)(2,1)S(1)}, u32[]{:S(2)}, u32[]{:S(2)}) collective-permute-start(bf16[2,256,384]{2,1,0:T(8,128)(2,1)S(1)} %pad_maximum_fusion.2), channel_id=1, source_target_pairs={{0,4},{4,0},{8,12},{12,8},{16,20},{20,16},{24,28},{28,24},{1,5},{5... | collective-permute-start | bytes 1179656 | tf_op jit(solution)/shard_map/ppermute | solution.py:144
  13.6 15.6 %collective-permute-start.5 = (bf16[2,256,384]{2,1,0:T(8,128)(2,1)S(1)}, bf16[2,256,384]{2,1,0:T(8,128)(2,1)S(1)}, u32[]{:S(2)}, u32[]{:S(2)}) collective-permute-start(bf16[2,256,384]{2,1,0:T(8,128)(2,1)S(1)} %collective-permute-done.kv_par), channel_id=1, source_target_pairs={{0,8},{4,12},{8,16},{12,20},{16,24},{20,28},{24,0},{28,4},{1,9},{5... | collective-permute-start | bytes 1179656 | tf_op jit(solution)/shard_map/ppermute | solution.py:141
  21.0 16.4 %collective-permute-start.13 = (bf16[2,256,384]{2,1,0:T(8,128)(2,1)S(1)}, bf16[2,256,384]{2,1,0:T(8,128)(2,1)S(1)}, u32[]{:S(2)}, u32[]{:S(2)}) collective-permute-start(bf16[2,256,384]{2,1,0:T(8,128)(2,1)S(1)} %collective-permute-done.8.kv_par), channel_id=1, source_target_pairs={{0,8},{4,12},{8,16},{12,20},{16,24},{20,28},{24,0},{28,4},{1,9},{5... | collective-permute-start | bytes 1179656 | tf_op jit(solution)/shard_map/ppermute | solution.py:141
  23.5 16.1 %collective-permute-start.1 = (bf16[128,1536]{1,0:T(8,128)(2,1)}, bf16[128,1536]{1,0:T(8,128)(2,1)S(1)}, u32[]{:S(2)}, u32[]{:S(2)}) collective-permute-start(bf16[128,1536]{1,0:T(8,128)(2,1)} %get-tuple-element.39), channel_id=1, source_target_pairs={{0,4},{4,0},{8,12},{12,8},{16,20},{20,16},{24,28},{28,24},{1,5},{5... | collective-permute-start | bytes 1179656 | tf_op jit(solution)/shard_map/ppermute | solution.py:144
  29.1 14.2 %collective-permute-start.9 = (bf16[128,1536]{1,0:T(8,128)(2,1)S(1)}, bf16[128,1536]{1,0:T(8,128)(2,1)S(1)}, u32[]{:S(2)}, u32[]{:S(2)}) collective-permute-start(bf16[128,1536]{1,0:T(8,128)(2,1)S(1)} %get-tuple-element.42), channel_id=1, source_target_pairs={{0,4},{4,0},{8,12},{12,8},{16,20},{20,16},{24,28},{28,24},{1,5},{5... | collective-permute-start | bytes 1179656 | tf_op jit(solution)/shard_map/ppermute | solution.py:144
  37.4 14.3 %collective-permute-start.6 = (bf16[2,256,384]{2,1,0:T(8,128)(2,1)S(1)}, bf16[2,256,384]{2,1,0:T(8,128)(2,1)S(1)}, u32[]{:S(2)}, u32[]{:S(2)}) collective-permute-start(bf16[2,256,384]{2,1,0:T(8,128)(2,1)S(1)} %broadcast_select_fusion.9), channel_id=1, source_target_pairs={{0,8},{4,12},{8,16},{12,20},{16,24},{20,28},{24,0},{28,4},{1,9},{5... | collective-permute-start | bytes 1179656 | tf_op jit(solution)/shard_map/ppermute | solution.py:141
  39.6 37.2 %collective-permute-start.14 = (bf16[2,256,384]{2,1,0:T(8,128)(2,1)S(1)}, bf16[2,256,384]{2,1,0:T(8,128)(2,1)S(1)}, u32[]{:S(2)}, u32[]{:S(2)}) collective-permute-start(bf16[2,256,384]{2,1,0:T(8,128)(2,1)S(1)} %broadcast_select_fusion.8), channel_id=1, source_target_pairs={{0,8},{4,12},{8,16},{12,20},{16,24},{20,28},{24,0},{28,4},{1,9},{5... | collective-permute-start | bytes 1179656 | tf_op jit(solution)/shard_map/ppermute | solution.py:141
  64.3 10.6 %collective-permute-start.16 = (bf16[2,256,384]{2,1,0:T(8,128)(2,1)S(1)}, bf16[2,256,384]{2,1,0:T(8,128)(2,1)S(1)}, u32[]{:S(2)}, u32[]{:S(2)}) collective-permute-start(bf16[2,256,384]{2,1,0:T(8,128)(2,1)S(1)} %get-tuple-element.49), channel_id=1, source_target_pairs={{0,24},{4,28},{8,0},{12,4},{16,8},{20,12},{24,16},{28,20},{1,25},{... | collective-permute-start | bytes 1179656 | tf_op jit(solution)/shard_map/ppermute | solution.py:141
  69.3 37.8 %collective-permute-start.10 = (bf16[2,256,384]{2,1,0:T(8,128)(2,1)S(1)}, bf16[2,256,384]{2,1,0:T(8,128)(2,1)S(1)}, u32[]{:S(2)}, u32[]{:S(2)}) collective-permute-start(bf16[2,256,384]{2,1,0:T(8,128)(2,1)S(1)} %get-tuple-element.46), channel_id=1, source_target_pairs={{0,4},{4,0},{8,12},{12,8},{16,20},{20,16},{24,28},{28,24},{1,5},{5... | collective-permute-start | bytes 1179656 | tf_op jit(solution)/shard_map/ppermute | solution.py:144
  74.9 15.8 %collective-permute-start.19 = (bf16[2,256,384]{2,1,0:T(8,128)(2,1)S(1)}, bf16[2,256,384]{2,1,0:T(8,128)(2,1)S(1)}, u32[]{:S(2)}, u32[]{:S(2)}) collective-permute-start(bf16[2,256,384]{2,1,0:T(8,128)(2,1)S(1)} %get-tuple-element.55), channel_id=1, source_target_pairs={{0,24},{4,28},{8,0},{12,4},{16,8},{20,12},{24,16},{28,20},{1,25},{... | collective-permute-start | bytes 1179656 | tf_op jit(solution)/shard_map/ppermute | solution.py:141
  76.4 16.5 %collective-permute-start.22 = (bf16[2,256,384]{2,1,0:T(8,128)(2,1)S(1)}, bf16[2,256,384]{2,1,0:T(8,128)(2,1)S(1)}, u32[]{:S(2)}, u32[]{:S(2)}) collective-permute-start(bf16[2,256,384]{2,1,0:T(8,128)(2,1)S(1)} %add_convert_fusion.3), channel_id=1, source_target_pairs={{0,24},{4,28},{8,0},{12,4},{16,8},{20,12},{24,16},{28,20},{1,25},{... | collective-permute-start | bytes 1179656 | tf_op jit(solution)/shard_map/ppermute | solution.py:141
  76.8 26.7 %collective-permute-start.25 = (bf16[4,48,1536]{2,1,0:T(8,128)(2,1)S(1)}, bf16[4,48,1536]{2,1,0:T(8,128)(2,1)S(1)}, u32[]{:S(2)}, u32[]{:S(2)}) collective-permute-start(bf16[4,48,1536]{2,1,0:T(8,128)(2,1)S(1)} %fusion.15), channel_id=1, source_target_pairs={{0,2},{1,3},{2,0},{3,1},{4,6},{5,7},{6,4},{7,5},{8,10},{9,11},{10,... | collective-permute-start | bytes 1769480 | tf_op jit(solution)/shard_map/ppermute | solution.py:141
  90.6 12.5 %collective-permute-start.20 = (bf16[2,256,384]{2,1,0:T(8,128)(2,1)S(1)}, bf16[2,256,384]{2,1,0:T(8,128)(2,1)S(1)}, u32[]{:S(2)}, u32[]{:S(2)}) collective-permute-start(bf16[2,256,384]{2,1,0:T(8,128)(2,1)S(1)} %get-tuple-element.56), channel_id=1, source_target_pairs={{0,24},{4,28},{8,0},{12,4},{16,8},{20,12},{24,16},{28,20},{1,25},{... | collective-permute-start | bytes 1179656 | tf_op jit(solution)/shard_map/ppermute | solution.py:141
  93.2 10.2 %collective-permute-start.23 = (bf16[2,256,384]{2,1,0:T(8,128)(2,1)S(1)}, bf16[2,256,384]{2,1,0:T(8,128)(2,1)S(1)}, u32[]{:S(2)}, u32[]{:S(2)}) collective-permute-start(bf16[2,256,384]{2,1,0:T(8,128)(2,1)S(1)} %get-tuple-element.79), channel_id=1, source_target_pairs={{0,4},{4,0},{8,12},{12,8},{16,20},{20,16},{24,28},{28,24},{1,5},{5... | collective-permute-start | bytes 1179656 | tf_op jit(solution)/shard_map/ppermute | solution.py:144
  103.4 10.3 %collective-permute-start.21 = (bf16[2,256,384]{2,1,0:T(8,128)(2,1)S(1)}, bf16[2,256,384]{2,1,0:T(8,128)(2,1)S(1)}, u32[]{:S(2)}, u32[]{:S(2)}) collective-permute-start(bf16[2,256,384]{2,1,0:T(8,128)(2,1)S(1)} %get-tuple-element.82), channel_id=1, source_target_pairs={{0,24},{4,28},{8,0},{12,4},{16,8},{20,12},{24,16},{28,20},{1,25},{... | collective-permute-start | bytes 1179656 | tf_op jit(solution)/shard_map/ppermute | solution.py:141
  103.9 14.2 %collective-permute-start.27 = (bf16[48,1536]{1,0:T(8,128)(2,1)S(1)}, bf16[48,1536]{1,0:T(8,128)(2,1)S(1)}, u32[]{:S(2)}, u32[]{:S(2)}) collective-permute-start(bf16[48,1536]{1,0:T(8,128)(2,1)S(1)} %get-tuple-element.97), channel_id=1, source_target_pairs={{0,8},{4,12},{8,16},{12,20},{16,24},{20,28},{24,0},{28,4},{1,9},{5... | collective-permute-start | bytes 442376 | tf_op jit(solution)/shard_map/ppermute | solution.py:141
  107.1 14.6 %collective-permute-start.28 = (bf16[48,1536]{1,0:T(8,128)(2,1)S(1)}, bf16[48,1536]{1,0:T(8,128)(2,1)S(1)}, u32[]{:S(2)}, u32[]{:S(2)}) collective-permute-start(bf16[48,1536]{1,0:T(8,128)(2,1)S(1)} %get-tuple-element.96), channel_id=1, source_target_pairs={{0,16},{4,20},{8,24},{12,28},{16,0},{20,4},{24,8},{28,12},{1,17},{... | collective-permute-start | bytes 442376 | tf_op jit(solution)/shard_map/ppermute | solution.py:141
  107.2 15.7 %collective-permute-start.29 = (bf16[48,1536]{1,0:T(8,128)(2,1)S(1)}, bf16[48,1536]{1,0:T(8,128)(2,1)S(1)}, u32[]{:S(2)}, u32[]{:S(2)}) collective-permute-start(bf16[48,1536]{1,0:T(8,128)(2,1)S(1)} %get-tuple-element.95), channel_id=1, source_target_pairs={{0,24},{4,28},{8,0},{12,4},{16,8},{20,12},{24,16},{28,20},{1,25},{... | collective-permute-start | bytes 442376 | tf_op jit(solution)/shard_map/ppermute | solution.py:141
  113.8 17.8 %collective-permute-start.24 = (bf16[2,256,384]{2,1,0:T(8,128)(2,1)S(1)}, bf16[2,256,384]{2,1,0:T(8,128)(2,1)S(1)}, u32[]{:S(2)}, u32[]{:S(2)}) collective-permute-start(bf16[2,256,384]{2,1,0:T(8,128)(2,1)S(1)} %get-tuple-element.66), channel_id=1, source_target_pairs={{0,24},{4,28},{8,0},{12,4},{16,8},{20,12},{24,16},{28,20},{1,25},{... | collective-permute-start | bytes 1179656 | tf_op jit(solution)/shard_map/ppermute | solution.py:141
  114.0 17.5 %collective-permute-start.30 = (bf16[2,256,384]{2,1,0:T(8,128)(2,1)S(1)}, bf16[2,256,384]{2,1,0:T(8,128)(2,1)S(1)}, u32[]{:S(2)}, u32[]{:S(2)}) collective-permute-start(bf16[2,256,384]{2,1,0:T(8,128)(2,1)S(1)} %add_convert_fusion.1), channel_id=1, source_target_pairs={{0,4},{4,0},{8,12},{12,8},{16,20},{20,16},{24,28},{28,24},{1,5},{5... | collective-permute-start | bytes 1179656 | tf_op jit(solution)/shard_map/ppermute | solution.py:144
  131.8 10.8 %collective-permute-start.31 = (bf16[48,1536]{1,0:T(8,128)(2,1)S(1)}, bf16[48,1536]{1,0:T(8,128)(2,1)S(1)}, u32[]{:S(2)}, u32[]{:S(2)}) collective-permute-start(bf16[48,1536]{1,0:T(8,128)(2,1)S(1)} %fusion.41), channel_id=1, source_target_pairs={{0,0},{1,4},{2,2},{3,6},{4,1},{5,5},{6,3},{7,7},{8,8},{9,12},{10,1... | collective-permute-start | bytes 442376 | tf_op jit(solution)/shard_map/ppermute | solution.py:258
  (20 other events, 152.8 us)

commit v3 on v2

--- a/solution.py
+++ b/solution.py
@@ -22,69 +22,64 @@
     return lax.dot_general(a, b, (((0,), (0,)), ((), ())), preferred_element_type=F32)
 
 
+def dot(a, b):
+    return jnp.dot(a, b, preferred_element_type=F32)
+
+
 def attention_body(
     place, q_own, q_par, k_own, v_own, kv_par, near_own, near_par, far, t_k, t_v, g_own, g_par,
     od_own, od_par, d_a, d_b, d_near_a, d_near_b, d_far,
-    k_all, v_all, dk_all, dv_all,
 ):
     tokens = q_own.shape[0]
-    col = place[1]
+    first = place[1] == 0
     scale = 1.0 / math.sqrt(q_own.shape[1])
     to_log2 = scale * math.log2(math.e)
 
-    def block(first, which):
-        return pl.ds(pl.multiple_of((first + which) * tokens, tokens), tokens)
-
-    at_far = pl.ds(0, tokens)
-    at_near_own, at_near_par = block(1, col), block(1, 1 - col)
-    at_own, at_par = block(3, col), block(3, 1 - col)
-    k_all[at_far] = far[0]
-    v_all[at_far] = far[1]
-    k_all[at_near_own] = near_own[0]
-    v_all[at_near_own] = near_own[1]
-    k_all[at_near_par] = near_par[0]
-    v_all[at_near_par] = near_par[1]
-    k_all[at_own] = k_own[...]
-    v_all[at_own] = v_own[...]
-    k_all[at_par] = kv_par[0]
-    v_all[at_par] = kv_par[1]
-    dk_all[...] = jnp.zeros_like(dk_all)
-    dv_all[...] = jnp.zeros_like(dv_all)
-
-    def one(q_ref, g_ref, od_ref, first):
-        window = pl.ds(pl.multiple_of(first * tokens, tokens), STEPS * tokens)
-        q = q_ref[...]
-        g = g_ref[...]
-        s_t = rows_dot(q, t_k[...])
-        s_i = rows_dot(q, k_all[window])
-        peak = jnp.maximum(jnp.max(s_t, axis=1, keepdims=True), jnp.max(s_i, axis=1, keepdims=True))
-        e_t = jnp.exp2((s_t - peak) * to_log2)
-        e_i = jnp.exp2((s_i - peak) * to_log2)
-        total = jnp.sum(e_t, axis=1, keepdims=True) + jnp.sum(e_i, axis=1, keepdims=True)
+    def by_block(own, par):
+        return jnp.where(first, own, par), jnp.where(first, par, own)
+
+    q = by_block(q_own[...], q_par[...])
+    g = by_block(g_own[...], g_par[...])
+    text = t_k.shape[0] // tokens
+    keys = [t_k[i * tokens : (i + 1) * tokens] for i in range(text)]
+    keys += [far[0], *by_block(near_own[0], near_par[0]), *by_block(k_own[...], kv_par[0])]
+    values = [t_v[i * tokens : (i + 1) * tokens] for i in range(text)]
+    values += [far[1], *by_block(near_own[1], near_par[1]), *by_block(v_own[...], kv_par[1])]
+    keys_t = [k.T for k in keys]
+    values_t = [v.T for v in values]
+    sets = [list(range(text)) + list(range(text + i, text + i + STEPS)) for i in range(2)]
+    score = [{j: rows_dot(keys[j], q[i]) for j in sets[i]} for i in range(2)]
+    prob, low, grad_low = [], [], []
+    out_t = []
+    for i in range(2):
+        peak = functools.reduce(jnp.maximum, [score[i][j] for j in sets[i]])
+        peak = jnp.max(peak, axis=0, keepdims=True)
+        e = {j: jnp.exp2((score[i][j] - peak) * to_log2) for j in sets[i]}
+        total = jnp.sum(functools.reduce(jnp.add, e.values()), axis=0, keepdims=True)
         inverse = 1.0 / total
-        p_t = e_t * inverse
-        p_i = e_i * inverse
-        low_t = p_t.astype(BF16)
-        low_i = p_i.astype(BF16)
-        out = jnp.dot(low_t, t_v[...], preferred_element_type=F32)
-        out += jnp.dot(low_i, v_all[window], preferred_element_type=F32)
-        out = out.astype(BF16)
-        od_ref[0] = out
-        delta = jnp.sum(g.astype(F32) * out.astype(F32), axis=1, keepdims=True)
-        ds_t = (p_t * ((rows_dot(g, t_v[...]) - delta) * scale)).astype(BF16)
-        ds_i = (p_i * ((rows_dot(g, v_all[window]) - delta) * scale)).astype(BF16)
-        dq = jnp.dot(ds_t, t_k[...], preferred_element_type=F32)
-        dq += jnp.dot(ds_i, k_all[window], preferred_element_type=F32)
-        od_ref[1] = dq.astype(BF16)
-        dk_all[window] += cols_dot(ds_i, q)
-        dv_all[window] += cols_dot(low_i, g)
-
-    one(q_own, g_own, od_own, col)
-    one(q_par, g_par, od_par, 1 - col)
-    for place_at, ref in enumerate((d_far, d_near_a, d_near_b, d_a, d_b)):
-        rows = pl.ds(place_at * tokens, tokens)
-        ref[0] = dk_all[rows].astype(BF16)
-        ref[1] = dv_all[rows].astype(BF16)
+        prob.append({j: e[j] * inverse for j in sets[i]})
+        low.append({j: prob[i][j].astype(BF16) for j in sets[i]})
+        out_t.append(functools.reduce(jnp.add, [dot(values_t[j], low[i][j]) for j in sets[i]]))
+    outs, dqs = [], []
+    for i in range(2):
+        out = out_t[i].T.astype(BF16)
+        outs.append(out)
+        delta = jnp.sum(g[i].T.astype(F32) * out_t[i].astype(BF16).astype(F32), axis=0, keepdims=True)
+        grad_low.append({
+            j: (prob[i][j] * (rows_dot(values[j], g[i]) - delta)).astype(BF16) for j in sets[i]
+        })
+        dq = functools.reduce(jnp.add, [dot(keys_t[j], grad_low[i][j]) for j in sets[i]])
+        dqs.append((dq * scale).T.astype(BF16))
+    for n, (own, par) in enumerate((by_block(*outs), by_block(*dqs))):
+        od_own[n] = own
+        od_par[n] = par
+    for n, ref in enumerate((d_far, d_near_a, d_near_b, d_a, d_b)):
+        j = text + n
+        users = [i for i in range(2) if j in sets[i]]
+        dk = functools.reduce(jnp.add, [dot(grad_low[i][j], q[i]) for i in users])
+        dv = functools.reduce(jnp.add, [dot(low[i][j], g[i]) for i in users])
+        ref[0] = (dk * scale).astype(BF16)
+        ref[1] = dv.astype(BF16)
 
 
 def attention(place, q, q_par, k, v, kv_par, near_own, near_par, far, t_k, t_v, g_own, g_par):
@@ -98,7 +93,6 @@
     keys = text + STEPS * tokens
     macs = heads * 2 * tokens * HEAD_DIM * (4 * keys + 2 * STEPS * tokens)
     out = jax.ShapeDtypeStruct((2, tokens, width), BF16)
-    image_rows = (STEPS + 1) * tokens
     return pl.pallas_call(
         attention_body,
         out_shape=(out,) * 7,
@@ -108,12 +102,6 @@
             in_specs=[whole(tokens), part, whole(tokens), whole(tokens), double, double, double, double,
                       whole(text), whole(text), part, part],
             out_specs=[double] * 7,
-            scratch_shapes=[
-                pltpu.VMEM((image_rows, HEAD_DIM), BF16),
-                pltpu.VMEM((image_rows, HEAD_DIM), BF16),
-                pltpu.VMEM((image_rows, HEAD_DIM), F32),
-                pltpu.VMEM((image_rows, HEAD_DIM), F32),
-            ],
         ),
         compiler_params=pltpu.CompilerParams(vmem_limit_bytes=48 * 1024 * 1024),
         cost_estimate=pl.CostEstimate(
@@ -159,7 +147,8 @@
         return jnp.stack([cut(k, index), cut(v, index)])
 
     half = tokens // 2
-    near_own = [shift(cut_two(shard[g]), "seq", 2) for g in every]
+    kv_own = [cut_two(shard[g]) for g in every]
+    near_own = [shift(kv_own[g], "seq", 2) for g in every]
     kv_par = [swap(cut_two(other[g]), "seq") for g in every]
     held = [shift(out_weight, "fsdp", -2 * (1 + g)) if g < last else out_weight for g in every]
     cot_par, near_par, far, q_par = [], [], [], []
@@ -167,10 +156,11 @@
         kv, = after([kv_par[g]], near_own[g])
         near_par.append(shift(kv, "seq", 2))
         if g < 2:
-            c, = after([cot[g * half : (g + 1) * half]], kv_par[g])
+            c, = after([cot[g * half : (g + 1) * half]], kv_par[g], near_own[g])
             cot_par.append(swap(c, "seq"))
     for g in every:
-        far.append(shift(jnp.where(col == 0, near_par[g], near_own[g]), "seq", 2))
+        b_near = jnp.where(col == 0, near_par[g], near_own[g])
+        far.append(shift(b_near, "seq", 2))
         c, = after([cut(q, other[g])], cot_par[min(g, 1)], *held[:last])
         q_par.append(swap(c, "seq"))
     cot_par = jnp.concatenate(cot_par, axis=0)
@@ -208,7 +198,8 @@
         own_od.append(od_own)
         if g < last:
             back = shift(d_far, "seq", -2)
-            par_od.append(swap(od_par, "seq"))
+            od_p, = after([od_par], back)
+            par_od.append(swap(od_p, "seq"))
             keep, give = terms_of(od_own, od_par)
             from_a = shift(d_near_a, "seq", -2)
             from_b = shift(add(d_near_b, back), "seq", -2)
@@ -220,43 +211,46 @@
             sum_o, sum_p = jnp.where(col == 0, sum_a, sum_b), jnp.where(col == 0, sum_b, sum_a)
             own_d.append((sum_o, swap(sum_p, "seq")))
         else:
-            keep, give = terms_of(*after([od_own, od_par], from_b, total))
+            keep, give = terms_of(od_own, od_par)
             d_far, = after([d_far], from_a)
             back = shift(d_far, "seq", -2)
+            od_par, = after([od_par], from_b)
             par_od.append(swap(od_par, "seq"))
             total = total + keep + swap(give, "fsdp").astype(F32)
             z = s // 2
             mine = lax.dynamic_index_in_dim(total, z, 0, keepdims=False)
             total = total.astype(BF16)
+            total, = after([total], back)
             pieces = []
             for by in range(1, pairs):
                 there = lax.dynamic_index_in_dim(total, (z + by) % pairs, 0, keepdims=False)
                 pieces.append(shift(there, "seq", 2 * by))
             near_b = add(d_near_b, back)
             from_p = shift(jnp.where(col == 0, near_b, d_near_a), "seq", -2)
-            own, = after([jnp.where(col == 0, d_near_a, near_b)], from_p)
+            own = jnp.where(col == 0, d_near_a, near_b)
+            own, = after([own], *pieces)
             from_o = shift(own, "seq", -2)
             sum_p = add(jnp.where(col == 0, d_b, d_a), from_p)
             par_od = list(after(par_od, from_p))
+            own_d = [(a, *after([b], from_p)) for a, b in own_d]
             for_own = swap(sum_p, "seq")
-            from_o, *pieces = after([from_o, *pieces], for_own)
-            sum_o = add(jnp.where(col == 0, d_a, d_b), from_o)
             for piece in pieces:
                 mine = mine + piece.astype(F32)
+            n = blocks * shards
+
+            def mirror(i):
+                ss, ff = divmod(i, shards)
+                return (ss - ss % 2 + ff % 2) * shards + ff - ff % 2 + ss % 2
+
+            crossed = lax.ppermute(mine.astype(BF16), ("seq", "fsdp"), [(i, mirror(i)) for i in range(n)])
+            grad_weight = jnp.where(core == col, mine, crossed.astype(F32))
+            from_o, = after([from_o], for_own, grad_weight)
+            sum_o = add(jnp.where(col == 0, d_a, d_b), from_o)
             own_d.append((sum_o, for_own))
 
     rel_out = jnp.concatenate([p for g in range(groups) for p in (own_od[g][0], par_od[g][0])], axis=1)
     rel_weight = jnp.concatenate([p for g in range(groups) for p in weight[g]], axis=0)
     image_out = jnp.dot(rel_out, rel_weight, preferred_element_type=F32).astype(BF16)
-
-    n = blocks * shards
-
-    def mirror(i):
-        ss, ff = divmod(i, shards)
-        return (ss - ss % 2 + ff % 2) * shards + ff - ff % 2 + ss % 2
-
-    crossed = lax.ppermute(mine.astype(BF16), ("seq", "fsdp"), [(i, mirror(i)) for i in range(n)])
-    grad_weight = jnp.where(core == col, mine, crossed.astype(F32))
 
     def assemble(pieces):
         whole = jnp.zeros((tokens, width * shards), BF16)

time: 144 us -> 139 us (0.965)
  the two profiles are of different devices: /device:TPU:25 before, /device:TPU:0 now
where the time goes in v3:
time: 139 us; the launch traced here: 138 us
  waiting for transfers between devices  57.7 us (42%)
  starting transfers between devices  37.3 us (27%)
  Pallas kernels  21.7 us (16%)
  other arithmetic  7.82 us (6%)
  matrix products  6.61 us (5%)
  local copies, waits for them, and re-layouts  6 us (4%)
    ppermute x17, waiting for transfers between devices, shift(): return lax.ppermute(a, axis, [(i, (i + by) % n) for i in range(n)])  43.6 us
    ppermute x17, starting transfers between devices, shift(): return lax.ppermute(a, axis, [(i, (i + by) % n) for i in range(n)])  22.7 us
    pallas_call x2, Pallas kernels, attention(): pl.pallas_call(attention_body, out_shape=(out,) * 7, grid_spec=pltpu.Pref...  21.7 us
    ppermute x14, waiting for transfers between devices, swap(): lax.ppermute(a, axis, [(i, i ^ 1) for i in range(lax.axis_size(axis))])  14.1 us
    ppermute x14, starting transfers between devices, swap(): lax.ppermute(a, axis, [(i, i ^ 1) for i in range(lax.axis_size(axis))])  14 us
    select_n x2, other arithmetic, per_device(): jnp.where(core == col, held[g], from_core)  5.32 us
  transfers between devices with their start and end apart: 32, of which 15 were waited for; matrix products, arithmetic and copies ran while one was open for 12% of the time, Pallas kernels for 16%

profile of v3, /device:TPU:0, one launch (start us, length us, event | category | flops | bytes accessed | tf_op | source)
XLA Modules:
  0.0 138.4 jit_solution(15321244392964666027)
XLA Ops:
  2.4 3.0 %collective-permute-start = (bf16[2,256,384]{2,1,0:T(8,128)(2,1)S(1)}, bf16[2,256,384]{2,1,0:T(8,128)(2,1)S(1)}, u32[]{:S(2)}, u32[]{:S(2)}) collective-permute-start(bf16[2,256,384]{2,1,0:T(8,128)(2,1)S(1)} %pad_maximum_fusion), channel_id=1, source_target_pairs={{0,4},{4,0},{8,12},{12,8},{16,20},{20,16},{24,28},{28,24},{1,5},{5... | collective-permute-start | bytes 1179656 | tf_op jit(solution)/shard_map/ppermute | solution.py:132
  9.3 6.0 %collective-permute-done.kv_par = bf16[2,256,384]{2,1,0:T(8,128)(2,1)S(1)} collective-permute-done((bf16[2,256,384]{2,1,0:T(8,128)(2,1)S(1)}, bf16[2,256,384]{2,1,0:T(8,128)(2,1)S(1)}, u32[]{:S(2)}, u32[]{:S(2)}) %collective-permute-start) | collective-permute-done | bytes 393248 | tf_op jit(solution)/shard_map/ppermute | solution.py:132
  15.4 2.1 %collective-permute-start.9 = (bf16[2,256,384]{2,1,0:T(8,128)(2,1)S(1)}, bf16[2,256,384]{2,1,0:T(8,128)(2,1)S(1)}, u32[]{:S(2)}, u32[]{:S(2)}) collective-permute-start(bf16[2,256,384]{2,1,0:T(8,128)(2,1)S(1)} %pad_maximum_fusion.3), channel_id=1, source_target_pairs={{0,8},{4,12},{8,16},{12,20},{16,24},{20,28},{24,0},{28,4},{1,9},{5... | collective-permute-start | bytes 1179656 | tf_op jit(solution)/shard_map/ppermute | solution.py:129
  20.0 3.0 %collective-permute-done.8.kv_par = bf16[2,256,384]{2,1,0:T(8,128)(2,1)S(1)} collective-permute-done((bf16[2,256,384]{2,1,0:T(8,128)(2,1)S(1)}, bf16[2,256,384]{2,1,0:T(8,128)(2,1)S(1)}, u32[]{:S(2)}, u32[]{:S(2)}) %collective-permute-start.8) | collective-permute-done | bytes 393248 | tf_op jit(solution)/shard_map/ppermute | solution.py:132
  23.0 6.6 %collective-permute-done.9.near_own = bf16[2,256,384]{2,1,0:T(8,128)(2,1)S(1)} collective-permute-done((bf16[2,256,384]{2,1,0:T(8,128)(2,1)S(1)}, bf16[2,256,384]{2,1,0:T(8,128)(2,1)S(1)}, u32[]{:S(2)}, u32[]{:S(2)}) %collective-permute-start.9) | collective-permute-done | bytes 393248 | tf_op jit(solution)/shard_map/ppermute | solution.py:129
  30.4 1.7 %collective-permute-start.2 = (bf16[128,1536]{1,0:T(8,128)(2,1)}, bf16[128,1536]{1,0:T(8,128)(2,1)S(1)}, u32[]{:S(2)}, u32[]{:S(2)}) collective-permute-start(bf16[128,1536]{1,0:T(8,128)(2,1)} %get-tuple-element.38), channel_id=1, source_target_pairs={{0,4},{4,0},{8,12},{12,8},{16,20},{20,16},{24,28},{28,24},{1,5},{5... | collective-permute-start | bytes 1179656 | tf_op jit(solution)/shard_map/ppermute | solution.py:132
  32.1 5.9 %collective-permute-done.5.near_par = bf16[2,256,384]{2,1,0:T(8,128)(2,1)S(1)} collective-permute-done((bf16[2,256,384]{2,1,0:T(8,128)(2,1)S(1)}, bf16[2,256,384]{2,1,0:T(8,128)(2,1)S(1)}, u32[]{:S(2)}, u32[]{:S(2)}) %collective-permute-start.5) | collective-permute-done | bytes 393248 | tf_op jit(solution)/shard_map/ppermute | solution.py:129
  38.0 1.7 %collective-permute-start.10 = (bf16[128,1536]{1,0:T(8,128)(2,1)S(1)}, bf16[128,1536]{1,0:T(8,128)(2,1)S(1)}, u32[]{:S(2)}, u32[]{:S(2)}) collective-permute-start(bf16[128,1536]{1,0:T(8,128)(2,1)S(1)} %get-tuple-element.41), channel_id=1, source_target_pairs={{0,4},{4,0},{8,12},{12,8},{16,20},{20,16},{24,28},{28,24},{1,5},{5... | collective-permute-start | bytes 1179656 | tf_op jit(solution)/shard_map/ppermute | solution.py:132
  39.8 3.8 %collective-permute-done.14.near_par = bf16[2,256,384]{2,1,0:T(8,128)(2,1)S(1)} collective-permute-done((bf16[2,256,384]{2,1,0:T(8,128)(2,1)S(1)}, bf16[2,256,384]{2,1,0:T(8,128)(2,1)S(1)}, u32[]{:S(2)}, u32[]{:S(2)}) %collective-permute-start.14) | collective-permute-done | bytes 393248 | tf_op jit(solution)/shard_map/ppermute | solution.py:129
  46.9 1.8 %collective-permute-start.4 = (bf16[256,384]{1,0:T(8,128)(2,1)S(1)}, bf16[256,384]{1,0:T(8,128)(2,1)S(1)}, u32[]{:S(2)}, u32[]{:S(2)}) collective-permute-start(bf16[256,384]{1,0:T(8,128)(2,1)S(1)} %get-tuple-element.39), channel_id=1, source_target_pairs={{0,4},{4,0},{8,12},{12,8},{16,20},{20,16},{24,28},{28,24},{1,5},{5... | collective-permute-start | bytes 589832 | tf_op jit(solution)/shard_map/ppermute | solution.py:132
  48.7 2.8 %broadcast_select_fusion.2 = (bf16[384,1536]{1,0:T(8,128)(2,1)S(1)}, bf16[384,1536]{1,0:T(8,128)(2,1)}) fusion(bf16[384,1536]{1,0:T(8,128)(2,1)} %param.12, bf16[384,1536]{1,0:T(8,128)(2,1)} %collective-permute-done.16, pred[]{:T(512)S(6)} %eq.28), kind=kLoop, calls=%fused_computation.20 | loop fusion | flops 1179648 | bytes 4718593 | tf_op jit(solution)/shard_map/jit(_where)/select_n | solution.py:171
  52.1 2.5 %broadcast_select_fusion.3 = (bf16[384,1536]{1,0:T(8,128)(2,1)S(1)}, bf16[384,1536]{1,0:T(8,128)(2,1)}) fusion(bf16[384,1536]{1,0:T(8,128)(2,1)} %collective-permute-done.3, bf16[384,1536]{1,0:T(8,128)(2,1)S(1)} %collective-permute-done.7, pred[]{:T(512)S(6)} %eq.28), kind=kLoop, calls=%fused_computation.21 | loop fusion | flops 1179648 | bytes 4718593 | tf_op jit(solution)/shard_map/jit(_where)/select_n | solution.py:171
  57.5 10.8 %attention.2 = (bf16[2,256,384]{2,1,0:T(8,128)(2,1)S(1)}, bf16[2,256,384]{2,1,0:T(8,128)(2,1)S(1)}, bf16[2,256,384]{2,1,0:T(8,128)(2,1)S(1)}, bf16[2,256,384]{2,...) custom-call(s32[2]{0:T(128)S(1)} %pad_add_fusion.place, ...), custom_call_target="tpu_custom_call" | custom-call | flops 6442450944 | bytes 4718592 | tf_op jit(solution)/shard_map/attention/pallas_call | solution.py:96
  72.5 6.0 %collective-permute-done.11 = bf16[2,256,384]{2,1,0:T(8,128)(2,1)S(1)} collective-permute-done((bf16[2,256,384]{2,1,0:T(8,128)(2,1)S(1)}, bf16[2,256,384]{2,1,0:T(8,128)(2,1)S(1)}, u32[]{:S(2)}, u32[]{:S(2)}) %collective-permute-start.11) | collective-permute-done | bytes 393248 | tf_op jit(solution)/shard_map/ppermute | solution.py:129
  79.8 4.5 %collective-permute-start.18 = (bf16[2,256,384]{2,1,0:T(8,128)(2,1)S(1)}, bf16[2,256,384]{2,1,0:T(8,128)(2,1)S(1)}, u32[]{:S(2)}, u32[]{:S(2)}) collective-permute-start(bf16[2,256,384]{2,1,0:T(8,128)(2,1)S(1)} %add_convert_fusion.5), channel_id=1, source_target_pairs={{0,24},{4,28},{8,0},{12,4},{16,8},{20,12},{24,16},{28,20},{1,25},{... | collective-permute-start | bytes 1179656 | tf_op jit(solution)/shard_map/ppermute | solution.py:129
  86.0 10.8 %attention.3 = (bf16[2,256,384]{2,1,0:T(8,128)(2,1)S(1)}, bf16[2,256,384]{2,1,0:T(8,128)(2,1)S(1)}, bf16[2,256,384]{2,1,0:T(8,128)(2,1)S(1)}, bf16[2,256,384]{2,...) custom-call(s32[2]{0:T(128)S(1)} %pad_add_fusion.1.place, ...), custom_call_target="tpu_custom_call" | custom-call | flops 6442450944 | bytes 4718592 | tf_op jit(solution)/shard_map/attention/pallas_call | solution.py:96
  100.3 4.4 %collective-permute-done.21 = bf16[2,256,384]{2,1,0:T(8,128)(2,1)S(1)} collective-permute-done((bf16[2,256,384]{2,1,0:T(8,128)(2,1)S(1)}, bf16[2,256,384]{2,1,0:T(8,128)(2,1)S(1)}, u32[]{:S(2)}, u32[]{:S(2)}) %collective-permute-start.21) | collective-permute-done | bytes 393248 | tf_op jit(solution)/shard_map/ppermute | solution.py:129
  104.8 2.5 %collective-permute-start.27 = (bf16[48,1536]{1,0:T(8,128)(2,1)S(1)}, bf16[48,1536]{1,0:T(8,128)(2,1)S(1)}, u32[]{:S(2)}, u32[]{:S(2)}) collective-permute-start(bf16[48,1536]{1,0:T(8,128)(2,1)S(1)} %get-tuple-element.94), channel_id=1, source_target_pairs={{0,16},{4,20},{8,24},{12,28},{16,0},{20,4},{24,8},{28,12},{1,17},{... | collective-permute-start | bytes 442376 | tf_op jit(solution)/shard_map/ppermute | solution.py:129
  108.8 3.1 %collective-permute-done.26 = bf16[48,1536]{1,0:T(8,128)(2,1)S(1)} collective-permute-done((bf16[48,1536]{1,0:T(8,128)(2,1)S(1)}, bf16[48,1536]{1,0:T(8,128)(2,1)S(1)}, u32[]{:S(2)}, u32[]{:S(2)}) %collective-permute-start.26) | collective-permute-done | bytes 147488 | tf_op jit(solution)/shard_map/ppermute | solution.py:129
  112.7 3.0 %collective-permute-done.27 = bf16[48,1536]{1,0:T(8,128)(2,1)S(1)} collective-permute-done((bf16[48,1536]{1,0:T(8,128)(2,1)S(1)}, bf16[48,1536]{1,0:T(8,128)(2,1)S(1)}, u32[]{:S(2)}, u32[]{:S(2)}) %collective-permute-start.27) | collective-permute-done | bytes 147488 | tf_op jit(solution)/shard_map/ppermute | solution.py:129
  115.7 3.5 %collective-permute-start.22 = (bf16[2,256,384]{2,1,0:T(8,128)(2,1)S(1)}, bf16[2,256,384]{2,1,0:T(8,128)(2,1)S(1)}, u32[]{:S(2)}, u32[]{:S(2)}) collective-permute-start(bf16[2,256,384]{2,1,0:T(8,128)(2,1)S(1)} %get-tuple-element.80), channel_id=1, source_target_pairs={{0,24},{4,28},{8,0},{12,4},{16,8},{20,12},{24,16},{28,20},{1,25},{... | collective-permute-start | bytes 1179656 | tf_op jit(solution)/shard_map/ppermute | solution.py:129
  120.0 8.8 %collective-permute-done.22 = bf16[2,256,384]{2,1,0:T(8,128)(2,1)S(1)} collective-permute-done((bf16[2,256,384]{2,1,0:T(8,128)(2,1)S(1)}, bf16[2,256,384]{2,1,0:T(8,128)(2,1)S(1)}, u32[]{:S(2)}, u32[]{:S(2)}) %collective-permute-start.22) | collective-permute-done | bytes 393248 | tf_op jit(solution)/shard_map/ppermute | solution.py:129
  130.8 2.3 %fusion.11 = bf16[1,256,1536]{2,1,0:T(8,128)(2,1)} fusion(bf16[384,1536]{1,0:T(8,128)(2,1)S(1)} %copy-done.5, bf16[384,1536]{1,0:T(8,128)(2,1)S(1)} %copy-done.4, bf16[384,1536]{1,0:T(8,128)(2,1)S(1)} %copy-done.8, bf16[384,1536]{1,0:T(8,128)(2,1)S(1)} %copy-done.7, bf16[256,384]{1,0:T(8,128)(2,1)S(1)} %get-tuple-element.103, ...), kind=kOutput, calls=%fused_computation.11 | convolution fusion | flops 1230372864 | bytes 6291456 | tf_op jit(solution)/shard_map/dot_general | solution.py:253
  134.0 2.9 %collective-permute-done.30 = bf16[2,256,384]{2,1,0:T(8,128)(2,1)S(1)} collective-permute-done((bf16[2,256,384]{2,1,0:T(8,128)(2,1)S(1)}, bf16[2,256,384]{2,1,0:T(8,128)(2,1)S(1)}, u32[]{:S(2)}, u32[]{:S(2)}) %collective-permute-start.30) | collective-permute-done | bytes 393248 | tf_op jit(solution)/shard_map/ppermute | solution.py:132
  (114 shorter events, 33.5 us)
Async XLA Ops:
  2.4 12.9 %collective-permute-start = (bf16[2,256,384]{2,1,0:T(8,128)(2,1)S(1)}, bf16[2,256,384]{2,1,0:T(8,128)(2,1)S(1)}, u32[]{:S(2)}, u32[]{:S(2)}) collective-permute-start(bf16[2,256,384]{2,1,0:T(8,128)(2,1)S(1)} %pad_maximum_fusion), channel_id=1, source_target_pairs={{0,4},{4,0},{8,12},{12,8},{16,20},{20,16},{24,28},{28,24},{1,5},{5... | collective-permute-start | bytes 1179656 | tf_op jit(solution)/shard_map/ppermute | solution.py:132
  5.5 12.5 %collective-permute-start.1 = (bf16[2,256,384]{2,1,0:T(8,128)(2,1)S(1)}, bf16[2,256,384]{2,1,0:T(8,128)(2,1)S(1)}, u32[]{:S(2)}, u32[]{:S(2)}) collective-permute-start(bf16[2,256,384]{2,1,0:T(8,128)(2,1)S(1)} %pad_maximum_fusion.1), channel_id=1, source_target_pairs={{0,8},{4,12},{8,16},{12,20},{16,24},{20,28},{24,0},{28,4},{1,9},{5... | collective-permute-start | bytes 1179656 | tf_op jit(solution)/shard_map/ppermute | solution.py:129
  7.1 41.6 %collective-permute-start.16 = (bf16[384,1536]{1,0:T(8,128)(2,1)}, bf16[384,1536]{1,0:T(8,128)(2,1)}, u32[]{:S(2)}, u32[]{:S(2)}) collective-permute-start(bf16[384,1536]{1,0:T(8,128)(2,1)} %param.12), channel_id=1, source_target_pairs={{0,1},{1,0},{2,3},{3,2},{4,5},{5,4},{6,7},{7,6},{8,9},{9,8},{10,11... | collective-permute-start | bytes 3538952 | tf_op jit(solution)/shard_map/ppermute | solution.py:132
  7.1 38.2 %collective-permute-start.3 = (bf16[384,1536]{1,0:T(8,128)(2,1)}, bf16[384,1536]{1,0:T(8,128)(2,1)}, u32[]{:S(2)}, u32[]{:S(2)}) collective-permute-start(bf16[384,1536]{1,0:T(8,128)(2,1)} %param.12), channel_id=1, source_target_pairs={{0,2},{1,3},{2,0},{3,1},{4,6},{5,7},{6,4},{7,5},{8,10},{9,11},{10,... | collective-permute-start | bytes 3538952 | tf_op jit(solution)/shard_map/ppermute | solution.py:129
  8.7 14.3 %collective-permute-start.8 = (bf16[2,256,384]{2,1,0:T(8,128)(2,1)S(1)}, bf16[2,256,384]{2,1,0:T(8,128)(2,1)S(1)}, u32[]{:S(2)}, u32[]{:S(2)}) collective-permute-start(bf16[2,256,384]{2,1,0:T(8,128)(2,1)S(1)} %pad_maximum_fusion.2), channel_id=1, source_target_pairs={{0,4},{4,0},{8,12},{12,8},{16,20},{20,16},{24,28},{28,24},{1,5},{5... | collective-permute-start | bytes 1179656 | tf_op jit(solution)/shard_map/ppermute | solution.py:132
  15.4 14.2 %collective-permute-start.9 = (bf16[2,256,384]{2,1,0:T(8,128)(2,1)S(1)}, bf16[2,256,384]{2,1,0:T(8,128)(2,1)S(1)}, u32[]{:S(2)}, u32[]{:S(2)}) collective-permute-start(bf16[2,256,384]{2,1,0:T(8,128)(2,1)S(1)} %pad_maximum_fusion.3), channel_id=1, source_target_pairs={{0,8},{4,12},{8,16},{12,20},{16,24},{20,28},{24,0},{28,4},{1,9},{5... | collective-permute-start | bytes 1179656 | tf_op jit(solution)/shard_map/ppermute | solution.py:129
  18.0 20.0 %collective-permute-start.5 = (bf16[2,256,384]{2,1,0:T(8,128)(2,1)S(1)}, bf16[2,256,384]{2,1,0:T(8,128)(2,1)S(1)}, u32[]{:S(2)}, u32[]{:S(2)}) collective-permute-start(bf16[2,256,384]{2,1,0:T(8,128)(2,1)S(1)} %collective-permute-done.kv_par), channel_id=1, source_target_pairs={{0,8},{4,12},{8,16},{12,20},{16,24},{20,28},{24,0},{28,4},{1,9},{5... | collective-permute-start | bytes 1179656 | tf_op jit(solution)/shard_map/ppermute | solution.py:129
  29.6 14.0 %collective-permute-start.14 = (bf16[2,256,384]{2,1,0:T(8,128)(2,1)S(1)}, bf16[2,256,384]{2,1,0:T(8,128)(2,1)S(1)}, u32[]{:S(2)}, u32[]{:S(2)}) collective-permute-start(bf16[2,256,384]{2,1,0:T(8,128)(2,1)S(1)} %collective-permute-done.8.kv_par), channel_id=1, source_target_pairs={{0,8},{4,12},{8,16},{12,20},{16,24},{20,28},{24,0},{28,4},{1,9},{5... | collective-permute-start | bytes 1179656 | tf_op jit(solution)/shard_map/ppermute | solution.py:129
  30.4 13.2 %collective-permute-start.2 = (bf16[128,1536]{1,0:T(8,128)(2,1)}, bf16[128,1536]{1,0:T(8,128)(2,1)S(1)}, u32[]{:S(2)}, u32[]{:S(2)}) collective-permute-start(bf16[128,1536]{1,0:T(8,128)(2,1)} %get-tuple-element.38), channel_id=1, source_target_pairs={{0,4},{4,0},{8,12},{12,8},{16,20},{20,16},{24,28},{28,24},{1,5},{5... | collective-permute-start | bytes 1179656 | tf_op jit(solution)/shard_map/ppermute | solution.py:132
  43.6 13.8 %collective-permute-start.6 = (bf16[2,256,384]{2,1,0:T(8,128)(2,1)S(1)}, bf16[2,256,384]{2,1,0:T(8,128)(2,1)S(1)}, u32[]{:S(2)}, u32[]{:S(2)}) collective-permute-start(bf16[2,256,384]{2,1,0:T(8,128)(2,1)S(1)} %broadcast_select_fusion.9), channel_id=1, source_target_pairs={{0,8},{4,12},{8,16},{12,20},{16,24},{20,28},{24,0},{28,4},{1,9},{5... | collective-permute-start | bytes 1179656 | tf_op jit(solution)/shard_map/ppermute | solution.py:129
  43.7 40.8 %collective-permute-start.15 = (bf16[2,256,384]{2,1,0:T(8,128)(2,1)S(1)}, bf16[2,256,384]{2,1,0:T(8,128)(2,1)S(1)}, u32[]{:S(2)}, u32[]{:S(2)}) collective-permute-start(bf16[2,256,384]{2,1,0:T(8,128)(2,1)S(1)} %broadcast_select_fusion.8), channel_id=1, source_target_pairs={{0,8},{4,12},{8,16},{12,20},{16,24},{20,28},{24,0},{28,4},{1,9},{5... | collective-permute-start | bytes 1179656 | tf_op jit(solution)/shard_map/ppermute | solution.py:129
  46.9 10.6 %collective-permute-start.4 = (bf16[256,384]{1,0:T(8,128)(2,1)S(1)}, bf16[256,384]{1,0:T(8,128)(2,1)S(1)}, u32[]{:S(2)}, u32[]{:S(2)}) collective-permute-start(bf16[256,384]{1,0:T(8,128)(2,1)S(1)} %get-tuple-element.39), channel_id=1, source_target_pairs={{0,4},{4,0},{8,12},{12,8},{16,20},{20,16},{24,28},{28,24},{1,5},{5... | collective-permute-start | bytes 589832 | tf_op jit(solution)/shard_map/ppermute | solution.py:132
  70.6 15.4 %collective-permute-start.13 = (bf16[256,384]{1,0:T(8,128)(2,1)}, bf16[256,384]{1,0:T(8,128)(2,1)S(1)}, u32[]{:S(2)}, u32[]{:S(2)}) collective-permute-start(bf16[256,384]{1,0:T(8,128)(2,1)} %get-tuple-element.48), channel_id=1, source_target_pairs={{0,4},{4,0},{8,12},{12,8},{16,20},{20,16},{24,28},{28,24},{1,5},{5... | collective-permute-start | bytes 589832 | tf_op jit(solution)/shard_map/ppermute | solution.py:132
  71.9 24.9 %collective-permute-start.20 = (bf16[2,256,384]{2,1,0:T(8,128)(2,1)S(1)}, bf16[2,256,384]{2,1,0:T(8,128)(2,1)S(1)}, u32[]{:S(2)}, u32[]{:S(2)}) collective-permute-start(bf16[2,256,384]{2,1,0:T(8,128)(2,1)S(1)} %get-tuple-element.57), channel_id=1, source_target_pairs={{0,24},{4,28},{8,0},{12,4},{16,8},{20,12},{24,16},{28,20},{1,25},{... | collective-permute-start | bytes 1179656 | tf_op jit(solution)/shard_map/ppermute | solution.py:129
  78.5 40.8 %collective-permute-start.12 = (bf16[2,256,384]{2,1,0:T(8,128)(2,1)S(1)}, bf16[2,256,384]{2,1,0:T(8,128)(2,1)S(1)}, u32[]{:S(2)}, u32[]{:S(2)}) collective-permute-start(bf16[2,256,384]{2,1,0:T(8,128)(2,1)S(1)} %get-tuple-element.47), channel_id=1, source_target_pairs={{0,4},{4,0},{8,12},{12,8},{16,20},{20,16},{24,28},{28,24},{1,5},{5... | collective-permute-start | bytes 1179656 | tf_op jit(solution)/shard_map/ppermute | solution.py:132
  79.8 18.3 %collective-permute-start.18 = (bf16[2,256,384]{2,1,0:T(8,128)(2,1)S(1)}, bf16[2,256,384]{2,1,0:T(8,128)(2,1)S(1)}, u32[]{:S(2)}, u32[]{:S(2)}) collective-permute-start(bf16[2,256,384]{2,1,0:T(8,128)(2,1)S(1)} %add_convert_fusion.5), channel_id=1, source_target_pairs={{0,24},{4,28},{8,0},{12,4},{16,8},{20,12},{24,16},{28,20},{1,25},{... | collective-permute-start | bytes 1179656 | tf_op jit(solution)/shard_map/ppermute | solution.py:129
  84.4 15.7 %collective-permute-start.24 = (bf16[4,48,1536]{2,1,0:T(8,128)(2,1)S(1)}, bf16[4,48,1536]{2,1,0:T(8,128)(2,1)S(1)}, u32[]{:S(2)}, u32[]{:S(2)}) collective-permute-start(bf16[4,48,1536]{2,1,0:T(8,128)(2,1)S(1)} %fusion.15), channel_id=1, source_target_pairs={{0,2},{1,3},{2,0},{3,1},{4,6},{5,7},{6,4},{7,5},{8,10},{9,11},{10,... | collective-permute-start | bytes 1769480 | tf_op jit(solution)/shard_map/ppermute | solution.py:129
  98.1 21.9 %collective-permute-start.19 = (bf16[2,256,384]{2,1,0:T(8,128)(2,1)S(1)}, bf16[2,256,384]{2,1,0:T(8,128)(2,1)S(1)}, u32[]{:S(2)}, u32[]{:S(2)}) collective-permute-start(bf16[2,256,384]{2,1,0:T(8,128)(2,1)S(1)} %get-tuple-element.54), channel_id=1, source_target_pairs={{0,4},{4,0},{8,12},{12,8},{16,20},{20,16},{24,28},{28,24},{1,5},{5... | collective-permute-start | bytes 1179656 | tf_op jit(solution)/shard_map/ppermute | solution.py:132
  104.8 10.9 %collective-permute-start.27 = (bf16[48,1536]{1,0:T(8,128)(2,1)S(1)}, bf16[48,1536]{1,0:T(8,128)(2,1)S(1)}, u32[]{:S(2)}, u32[]{:S(2)}) collective-permute-start(bf16[48,1536]{1,0:T(8,128)(2,1)S(1)} %get-tuple-element.94), channel_id=1, source_target_pairs={{0,16},{4,20},{8,24},{12,28},{16,0},{20,4},{24,8},{28,12},{1,17},{... | collective-permute-start | bytes 442376 | tf_op jit(solution)/shard_map/ppermute | solution.py:129
  107.3 11.9 %collective-permute-start.28 = (bf16[48,1536]{1,0:T(8,128)(2,1)S(1)}, bf16[48,1536]{1,0:T(8,128)(2,1)S(1)}, u32[]{:S(2)}, u32[]{:S(2)}) collective-permute-start(bf16[48,1536]{1,0:T(8,128)(2,1)S(1)} %get-tuple-element.93), channel_id=1, source_target_pairs={{0,24},{4,28},{8,0},{12,4},{16,8},{20,12},{24,16},{28,20},{1,25},{... | collective-permute-start | bytes 442376 | tf_op jit(solution)/shard_map/ppermute | solution.py:129
  111.9 17.0 %collective-permute-start.23 = (bf16[2,256,384]{2,1,0:T(8,128)(2,1)S(1)}, bf16[2,256,384]{2,1,0:T(8,128)(2,1)S(1)}, u32[]{:S(2)}, u32[]{:S(2)}) collective-permute-start(bf16[2,256,384]{2,1,0:T(8,128)(2,1)S(1)} %get-tuple-element.77), channel_id=1, source_target_pairs={{0,4},{4,0},{8,12},{12,8},{16,20},{20,16},{24,28},{28,24},{1,5},{5... | collective-permute-start | bytes 1179656 | tf_op jit(solution)/shard_map/ppermute | solution.py:132
  115.7 13.1 %collective-permute-start.22 = (bf16[2,256,384]{2,1,0:T(8,128)(2,1)S(1)}, bf16[2,256,384]{2,1,0:T(8,128)(2,1)S(1)}, u32[]{:S(2)}, u32[]{:S(2)}) collective-permute-start(bf16[2,256,384]{2,1,0:T(8,128)(2,1)S(1)} %get-tuple-element.80), channel_id=1, source_target_pairs={{0,24},{4,28},{8,0},{12,4},{16,8},{20,12},{24,16},{28,20},{1,25},{... | collective-permute-start | bytes 1179656 | tf_op jit(solution)/shard_map/ppermute | solution.py:129
  119.2 14.8 %collective-permute-start.29 = (bf16[2,256,384]{2,1,0:T(8,128)(2,1)S(1)}, bf16[2,256,384]{2,1,0:T(8,128)(2,1)S(1)}, u32[]{:S(2)}, u32[]{:S(2)}) collective-permute-start(bf16[2,256,384]{2,1,0:T(8,128)(2,1)S(1)} %get-tuple-element.69), channel_id=1, source_target_pairs={{0,24},{4,28},{8,0},{12,4},{16,8},{20,12},{24,16},{28,20},{1,25},{... | collective-permute-start | bytes 1179656 | tf_op jit(solution)/shard_map/ppermute | solution.py:129
  119.3 13.8 %collective-permute-start.31 = (bf16[48,1536]{1,0:T(8,128)(2,1)S(1)}, bf16[48,1536]{1,0:T(8,128)(2,1)S(1)}, u32[]{:S(2)}, u32[]{:S(2)}) collective-permute-start(bf16[48,1536]{1,0:T(8,128)(2,1)S(1)} %fusion.39), channel_id=1, source_target_pairs={{0,0},{1,4},{2,2},{3,6},{4,1},{5,5},{6,3},{7,7},{8,8},{9,12},{10,1... | collective-permute-start | bytes 442376 | tf_op jit(solution)/shard_map/ppermute | solution.py:245
  (20 other events, 150.2 us)

commit v4 on v3

--- a/solution.py
+++ b/solution.py
@@ -103,7 +103,7 @@
                       whole(text), whole(text), part, part],
             out_specs=[double] * 7,
         ),
-        compiler_params=pltpu.CompilerParams(vmem_limit_bytes=48 * 1024 * 1024),
+        compiler_params=pltpu.CompilerParams(vmem_limit_bytes=16 * 1024 * 1024),
         cost_estimate=pl.CostEstimate(
             flops=4 * macs, bytes_accessed=24 * tokens * width * 2, transcendentals=heads * 2 * tokens * keys
         ),
@@ -156,12 +156,12 @@
         kv, = after([kv_par[g]], near_own[g])
         near_par.append(shift(kv, "seq", 2))
         if g < 2:
-            c, = after([cot[g * half : (g + 1) * half]], kv_par[g], near_own[g])
+            c, = after([cot[g * half : (g + 1) * half]], kv_par[g])
             cot_par.append(swap(c, "seq"))
     for g in every:
         b_near = jnp.where(col == 0, near_par[g], near_own[g])
         far.append(shift(b_near, "seq", 2))
-        c, = after([cut(q, other[g])], cot_par[min(g, 1)], *held[:last])
+        c, = after([cut(q, other[g])], cot_par[min(g, len(cot_par) - 1)])
         q_par.append(swap(c, "seq"))
     cot_par = jnp.concatenate(cot_par, axis=0)
 
@@ -214,7 +214,7 @@
             keep, give = terms_of(od_own, od_par)
             d_far, = after([d_far], from_a)
             back = shift(d_far, "seq", -2)
-            od_par, = after([od_par], from_b)
+            od_par, = after([od_par], from_b, total)
             par_od.append(swap(od_par, "seq"))
             total = total + keep + swap(give, "fsdp").astype(F32)
             z = s // 2
@@ -227,9 +227,6 @@
                 pieces.append(shift(there, "seq", 2 * by))
             near_b = add(d_near_b, back)
             from_p = shift(jnp.where(col == 0, near_b, d_near_a), "seq", -2)
-            own = jnp.where(col == 0, d_near_a, near_b)
-            own, = after([own], *pieces)
-            from_o = shift(own, "seq", -2)
             sum_p = add(jnp.where(col == 0, d_b, d_a), from_p)
             par_od = list(after(par_od, from_p))
             own_d = [(a, *after([b], from_p)) for a, b in own_d]
@@ -244,6 +241,9 @@
 
             crossed = lax.ppermute(mine.astype(BF16), ("seq", "fsdp"), [(i, mirror(i)) for i in range(n)])
             grad_weight = jnp.where(core == col, mine, crossed.astype(F32))
+            own = jnp.where(col == 0, d_near_a, near_b)
+            own, = after([own], *pieces)
+            from_o = shift(own, "seq", -2)
             from_o, = after([from_o], for_own, grad_weight)
             sum_o = add(jnp.where(col == 0, d_a, d_b), from_o)
             own_d.append((sum_o, for_own))

time: 139 us -> 135 us (0.971)
  starting transfers between devices: 37.3 us -> 40.2 us
  waiting for transfers between devices: 57.7 us -> 55.3 us
  other arithmetic: 7.82 us -> 5.73 us
    ppermute x17, waiting for transfers between devices: 43.6 us -> 33.4 us  [shift(): return lax.ppermute(a, axis, [(i, (i + by) % n) for i in range(n)])]
    ppermute x14, waiting for transfers between devices: 14.1 us -> 21.9 us  [swap(): lax.ppermute(a, axis, [(i, i ^ 1) for i in range(lax.axis_size(axis))])]
    ppermute x17, starting transfers between devices: 22.7 us -> 27.1 us  [shift(): return lax.ppermute(a, axis, [(i, (i + by) % n) for i in range(n)])]
    select_n x2, other arithmetic: 5.32 us -> 1.7 us  [per_device(): jnp.where(core == col, held[g], from_core)]
    ppermute x14, starting transfers between devices: 14 us -> 12.4 us  [swap(): lax.ppermute(a, axis, [(i, i ^ 1) for i in range(lax.axis_size(axis))])]
    another operation x4, other arithmetic: 0.19 us -> 1.68 us  [cut_two(): return jnp.stack([cut(k, index), cut(v, index)])]
  transfers between devices with their start and end apart: 32 -> 32, of which waited for: 15 -> 15; matrix products, arithmetic and copies ran while one was open for 12% -> 12% of each run, Pallas kernels for 16% -> 15%
where the time goes in v4:
time: 135 us
  waiting for transfers between devices  55.3 us (41%)
  starting transfers between devices  40.2 us (30%)
  Pallas kernels  20.5 us (15%)
  matrix products  6.6 us (5%)
  other arithmetic  5.73 us (4%)
  local copies, waits for them, and re-layouts  5.67 us (4%)
    ppermute x17, waiting for transfers between devices, shift(): return lax.ppermute(a, axis, [(i, (i + by) % n) for i in range(n)])  33.4 us
    ppermute x17, starting transfers between devices, shift(): return lax.ppermute(a, axis, [(i, (i + by) % n) for i in range(n)])  27.1 us
    ppermute x14, waiting for transfers between devices, swap(): lax.ppermute(a, axis, [(i, i ^ 1) for i in range(lax.axis_size(axis))])  21.9 us
    pallas_call x2, Pallas kernels, attention(): pl.pallas_call(attention_body, out_shape=(out,) * 7, grid_spec=pltpu.Pref...  20.5 us
    ppermute x14, starting transfers between devices, swap(): lax.ppermute(a, axis, [(i, i ^ 1) for i in range(lax.axis_size(axis))])  12.4 us
  transfers between devices with their start and end apart: 32, of which 15 were waited for; matrix products, arithmetic and copies ran while one was open for 12% of the time, Pallas kernels for 15%

profile of v4, /device:TPU:0, one launch (start us, length us, event | category | flops | bytes accessed | tf_op | source)
XLA Modules:
  0.0 135.1 jit_solution(17930400994207476241)
XLA Ops:
  0.6 3.0 %collective-permute-start.6 = (bf16[384,1536]{1,0:T(8,128)(2,1)}, bf16[384,1536]{1,0:T(8,128)(2,1)}, u32[]{:S(2)}, u32[]{:S(2)}) collective-permute-start(bf16[384,1536]{1,0:T(8,128)(2,1)} %param.12), channel_id=1, source_target_pairs={{0,2},{1,3},{2,0},{3,1},{4,6},{5,7},{6,4},{7,5},{8,10},{9,11},{10,... | collective-permute-start | bytes 3538952 | tf_op jit(solution)/shard_map/ppermute | solution.py:129
  3.7 1.7 %constant_dynamic-slice_fusion = (bf16[1,256,384]{2,1,0:T(8,128)(2,1)S(1)}, bf16[1,256,384]{2,1,0:T(8,128)(2,1)S(1)}, bf16[1,256,384]{2,1,0:T(8,128)(2,1)S(1)}, ...) fusion(bf16[1,256,1536]{2,1,0:T(8,128)(2,1)} %param.9, ...), kind=kLoop, calls=%fused_computation.90 | loop fusion | bytes 3145744 | tf_op jit(solution)/shard_map/dynamic_slice | solution.py:144
  13.2 4.2 %collective-permute-done.kv_par = bf16[2,256,384]{2,1,0:T(8,128)(2,1)S(1)} collective-permute-done((bf16[2,256,384]{2,1,0:T(8,128)(2,1)S(1)}, bf16[2,256,384]{2,1,0:T(8,128)(2,1)S(1)}, u32[]{:S(2)}, u32[]{:S(2)}) %collective-permute-start) | collective-permute-done | bytes 393248 | tf_op jit(solution)/shard_map/ppermute | solution.py:132
  19.0 1.9 %collective-permute-done.3.near_own = bf16[2,256,384]{2,1,0:T(8,128)(2,1)S(1)} collective-permute-done((bf16[2,256,384]{2,1,0:T(8,128)(2,1)S(1)}, bf16[2,256,384]{2,1,0:T(8,128)(2,1)S(1)}, u32[]{:S(2)}, u32[]{:S(2)}) %collective-permute-start.3) | collective-permute-done | bytes 393248 | tf_op jit(solution)/shard_map/ppermute | solution.py:129
  21.0 4.9 %collective-permute-done.8.kv_par = bf16[2,256,384]{2,1,0:T(8,128)(2,1)S(1)} collective-permute-done((bf16[2,256,384]{2,1,0:T(8,128)(2,1)}, bf16[2,256,384]{2,1,0:T(8,128)(2,1)S(1)}, u32[]{:S(2)}, u32[]{:S(2)}) %collective-permute-start.8) | collective-permute-done | bytes 393248 | tf_op jit(solution)/shard_map/ppermute | solution.py:132
  26.0 3.3 %collective-permute-done.13.near_own = bf16[2,256,384]{2,1,0:T(8,128)(2,1)S(1)} collective-permute-done((bf16[2,256,384]{2,1,0:T(8,128)(2,1)}, bf16[2,256,384]{2,1,0:T(8,128)(2,1)S(1)}, u32[]{:S(2)}, u32[]{:S(2)}) %collective-permute-start.13) | collective-permute-done | bytes 393248 | tf_op jit(solution)/shard_map/ppermute | solution.py:129
  29.9 4.6 %collective-permute-done.1 = bf16[128,1536]{1,0:T(8,128)(2,1)} collective-permute-done((bf16[128,1536]{1,0:T(8,128)(2,1)}, bf16[128,1536]{1,0:T(8,128)(2,1)}, u32[]{:S(2)}, u32[]{:S(2)}) %collective-permute-start.1) | collective-permute-done | bytes 393248 | tf_op jit(solution)/shard_map/ppermute | solution.py:132
  38.6 4.2 %collective-permute-done.9 = bf16[128,1536]{1,0:T(8,128)(2,1)S(1)} collective-permute-done((bf16[128,1536]{1,0:T(8,128)(2,1)}, bf16[128,1536]{1,0:T(8,128)(2,1)S(1)}, u32[]{:S(2)}, u32[]{:S(2)}) %collective-permute-start.9) | collective-permute-done | bytes 393248 | tf_op jit(solution)/shard_map/ppermute | solution.py:132
  51.2 3.9 %collective-permute-done.5.far = bf16[2,256,384]{2,1,0:T(8,128)(2,1)S(1)} collective-permute-done((bf16[2,256,384]{2,1,0:T(8,128)(2,1)S(1)}, bf16[2,256,384]{2,1,0:T(8,128)(2,1)S(1)}, u32[]{:S(2)}, u32[]{:S(2)}) %collective-permute-start.5) | collective-permute-done | bytes 393248 | tf_op jit(solution)/shard_map/ppermute | solution.py:129
  55.1 10.2 %attention.2 = (bf16[2,256,384]{2,1,0:T(8,128)(2,1)S(1)}, bf16[2,256,384]{2,1,0:T(8,128)(2,1)S(1)}, bf16[2,256,384]{2,1,0:T(8,128)(2,1)S(1)}, bf16[2,256,384]{2,...) custom-call(s32[2]{0:T(128)S(1)} %pad_add_fusion.place, ...), custom_call_target="tpu_custom_call" | custom-call | flops 6442450944 | bytes 4718592 | tf_op jit(solution)/shard_map/attention/pallas_call | solution.py:96
  65.4 3.1 %collective-permute-start.10 = (bf16[2,256,384]{2,1,0:T(8,128)(2,1)S(1)}, bf16[2,256,384]{2,1,0:T(8,128)(2,1)S(1)}, u32[]{:S(2)}, u32[]{:S(2)}) collective-permute-start(bf16[2,256,384]{2,1,0:T(8,128)(2,1)S(1)} %get-tuple-element.46), channel_id=1, source_target_pairs={{0,24},{4,28},{8,0},{12,4},{16,8},{20,12},{24,16},{28,20},{1,25},{... | collective-permute-start | bytes 1179656 | tf_op jit(solution)/shard_map/ppermute | solution.py:129
  70.4 5.9 %collective-permute-done.10 = bf16[2,256,384]{2,1,0:T(8,128)(2,1)S(1)} collective-permute-done((bf16[2,256,384]{2,1,0:T(8,128)(2,1)S(1)}, bf16[2,256,384]{2,1,0:T(8,128)(2,1)S(1)}, u32[]{:S(2)}, u32[]{:S(2)}) %collective-permute-start.10) | collective-permute-done | bytes 393248 | tf_op jit(solution)/shard_map/ppermute | solution.py:129
  76.2 1.8 %collective-permute-start.11 = (bf16[2,256,384]{2,1,0:T(8,128)(2,1)S(1)}, bf16[2,256,384]{2,1,0:T(8,128)(2,1)S(1)}, u32[]{:S(2)}, u32[]{:S(2)}) collective-permute-start(bf16[2,256,384]{2,1,0:T(8,128)(2,1)S(1)} %get-tuple-element.47), channel_id=1, source_target_pairs={{0,4},{4,0},{8,12},{12,8},{16,20},{20,16},{24,28},{28,24},{1,5},{5... | collective-permute-start | bytes 1179656 | tf_op jit(solution)/shard_map/ppermute | solution.py:132
  78.2 4.5 %collective-permute-start.18 = (bf16[2,256,384]{2,1,0:T(8,128)(2,1)S(1)}, bf16[2,256,384]{2,1,0:T(8,128)(2,1)S(1)}, u32[]{:S(2)}, u32[]{:S(2)}) collective-permute-start(bf16[2,256,384]{2,1,0:T(8,128)(2,1)S(1)} %add_convert_fusion.5), channel_id=1, source_target_pairs={{0,24},{4,28},{8,0},{12,4},{16,8},{20,12},{24,16},{28,20},{1,25},{... | collective-permute-start | bytes 1179656 | tf_op jit(solution)/shard_map/ppermute | solution.py:129
  83.4 10.3 %attention.3 = (bf16[2,256,384]{2,1,0:T(8,128)(2,1)S(1)}, bf16[2,256,384]{2,1,0:T(8,128)(2,1)S(1)}, bf16[2,256,384]{2,1,0:T(8,128)(2,1)S(1)}, bf16[2,256,384]{2,...) custom-call(s32[2]{0:T(128)S(1)} %pad_add_fusion.1.place, ...), custom_call_target="tpu_custom_call" | custom-call | flops 6442450944 | bytes 4718592 | tf_op jit(solution)/shard_map/attention/pallas_call | solution.py:96
  97.1 4.4 %collective-permute-done.22 = bf16[2,256,384]{2,1,0:T(8,128)(2,1)S(1)} collective-permute-done((bf16[2,256,384]{2,1,0:T(8,128)(2,1)S(1)}, bf16[2,256,384]{2,1,0:T(8,128)(2,1)S(1)}, u32[]{:S(2)}, u32[]{:S(2)}) %collective-permute-start.22) | collective-permute-done | bytes 393248 | tf_op jit(solution)/shard_map/ppermute | solution.py:129
  101.6 2.5 %collective-permute-start.27 = (bf16[48,1536]{1,0:T(8,128)(2,1)S(1)}, bf16[48,1536]{1,0:T(8,128)(2,1)S(1)}, u32[]{:S(2)}, u32[]{:S(2)}) collective-permute-start(bf16[48,1536]{1,0:T(8,128)(2,1)S(1)} %get-tuple-element.94), channel_id=1, source_target_pairs={{0,16},{4,20},{8,24},{12,28},{16,0},{20,4},{24,8},{28,12},{1,17},{... | collective-permute-start | bytes 442376 | tf_op jit(solution)/shard_map/ppermute | solution.py:129
  105.6 3.1 %collective-permute-done.26 = bf16[48,1536]{1,0:T(8,128)(2,1)S(1)} collective-permute-done((bf16[48,1536]{1,0:T(8,128)(2,1)S(1)}, bf16[48,1536]{1,0:T(8,128)(2,1)S(1)}, u32[]{:S(2)}, u32[]{:S(2)}) %collective-permute-start.26) | collective-permute-done | bytes 147488 | tf_op jit(solution)/shard_map/ppermute | solution.py:129
  109.9 2.6 %collective-permute-done.27 = bf16[48,1536]{1,0:T(8,128)(2,1)S(1)} collective-permute-done((bf16[48,1536]{1,0:T(8,128)(2,1)S(1)}, bf16[48,1536]{1,0:T(8,128)(2,1)S(1)}, u32[]{:S(2)}, u32[]{:S(2)}) %collective-permute-start.27) | collective-permute-done | bytes 147488 | tf_op jit(solution)/shard_map/ppermute | solution.py:129
  112.5 3.4 %collective-permute-start.23 = (bf16[2,256,384]{2,1,0:T(8,128)(2,1)S(1)}, bf16[2,256,384]{2,1,0:T(8,128)(2,1)S(1)}, u32[]{:S(2)}, u32[]{:S(2)}) collective-permute-start(bf16[2,256,384]{2,1,0:T(8,128)(2,1)S(1)} %get-tuple-element.80), channel_id=1, source_target_pairs={{0,24},{4,28},{8,0},{12,4},{16,8},{20,12},{24,16},{28,20},{1,25},{... | collective-permute-start | bytes 1179656 | tf_op jit(solution)/shard_map/ppermute | solution.py:129
  117.4 8.2 %collective-permute-done.23 = bf16[2,256,384]{2,1,0:T(8,128)(2,1)S(1)} collective-permute-done((bf16[2,256,384]{2,1,0:T(8,128)(2,1)S(1)}, bf16[2,256,384]{2,1,0:T(8,128)(2,1)S(1)}, u32[]{:S(2)}, u32[]{:S(2)}) %collective-permute-start.23) | collective-permute-done | bytes 393248 | tf_op jit(solution)/shard_map/ppermute | solution.py:129
  125.8 1.9 %collective-permute-start.30 = (bf16[2,256,384]{2,1,0:T(8,128)(2,1)S(1)}, bf16[2,256,384]{2,1,0:T(8,128)(2,1)S(1)}, u32[]{:S(2)}, u32[]{:S(2)}) collective-permute-start(bf16[2,256,384]{2,1,0:T(8,128)(2,1)S(1)} %add_convert_fusion.1), channel_id=1, source_target_pairs={{0,4},{4,0},{8,12},{12,8},{16,20},{20,16},{24,28},{28,24},{1,5},{5... | collective-permute-start | bytes 1179656 | tf_op jit(solution)/shard_map/ppermute | solution.py:132
  127.8 2.3 %fusion.11 = bf16[1,256,1536]{2,1,0:T(8,128)(2,1)} fusion(bf16[384,1536]{1,0:T(8,128)(2,1)S(1)} %get-tuple-element.76, bf16[384,1536]{1,0:T(8,128)(2,1)S(1)} %get-tuple-element.75, bf16[384,1536]{1,0:T(8,128)(2,1)S(1)} %get-tuple-element.74, bf16[384,1536]{1,0:T(8,128)(2,1)S(1)} %get-tuple-element.73, bf16[256,384]{1,0:T(8,128)(2,1)S(1)} %get-tuple-element.103, ...), kind=kOutput, calls=%fused_computation.11 | convolution fusion | flops 1230372864 | bytes 6291456 | tf_op jit(solution)/shard_map/dot_general | solution.py:253
  131.0 2.7 %collective-permute-done.30 = bf16[2,256,384]{2,1,0:T(8,128)(2,1)S(1)} collective-permute-done((bf16[2,256,384]{2,1,0:T(8,128)(2,1)S(1)}, bf16[2,256,384]{2,1,0:T(8,128)(2,1)S(1)}, u32[]{:S(2)}, u32[]{:S(2)}) %collective-permute-start.30) | collective-permute-done | bytes 393248 | tf_op jit(solution)/shard_map/ppermute | solution.py:132
  (110 shorter events, 35.5 us)
Async XLA Ops:
  0.6 43.7 %collective-permute-start.6 = (bf16[384,1536]{1,0:T(8,128)(2,1)}, bf16[384,1536]{1,0:T(8,128)(2,1)}, u32[]{:S(2)}, u32[]{:S(2)}) collective-permute-start(bf16[384,1536]{1,0:T(8,128)(2,1)} %param.12), channel_id=1, source_target_pairs={{0,2},{1,3},{2,0},{3,1},{4,6},{5,7},{6,4},{7,5},{8,10},{9,11},{10,... | collective-permute-start | bytes 3538952 | tf_op jit(solution)/shard_map/ppermute | solution.py:129
  5.4 12.1 %collective-permute-start = (bf16[2,256,384]{2,1,0:T(8,128)(2,1)S(1)}, bf16[2,256,384]{2,1,0:T(8,128)(2,1)S(1)}, u32[]{:S(2)}, u32[]{:S(2)}) collective-permute-start(bf16[2,256,384]{2,1,0:T(8,128)(2,1)S(1)} %pad_maximum_fusion), channel_id=1, source_target_pairs={{0,4},{4,0},{8,12},{12,8},{16,20},{20,16},{24,28},{28,24},{1,5},{5... | collective-permute-start | bytes 1179656 | tf_op jit(solution)/shard_map/ppermute | solution.py:132
  7.0 13.9 %collective-permute-start.3 = (bf16[2,256,384]{2,1,0:T(8,128)(2,1)S(1)}, bf16[2,256,384]{2,1,0:T(8,128)(2,1)S(1)}, u32[]{:S(2)}, u32[]{:S(2)}) collective-permute-start(bf16[2,256,384]{2,1,0:T(8,128)(2,1)S(1)} %pad_maximum_fusion.1), channel_id=1, source_target_pairs={{0,8},{4,12},{8,16},{12,20},{16,24},{20,28},{24,0},{28,4},{1,9},{5... | collective-permute-start | bytes 1179656 | tf_op jit(solution)/shard_map/ppermute | solution.py:129
  9.4 16.5 %collective-permute-start.8 = (bf16[2,256,384]{2,1,0:T(8,128)(2,1)}, bf16[2,256,384]{2,1,0:T(8,128)(2,1)S(1)}, u32[]{:S(2)}, u32[]{:S(2)}) collective-permute-start(bf16[2,256,384]{2,1,0:T(8,128)(2,1)} %pad_maximum_fusion.2), channel_id=1, source_target_pairs={{0,4},{4,0},{8,12},{12,8},{16,20},{20,16},{24,28},{28,24},{1,5},{5... | collective-permute-start | bytes 1179656 | tf_op jit(solution)/shard_map/ppermute | solution.py:132
  10.7 18.6 %collective-permute-start.13 = (bf16[2,256,384]{2,1,0:T(8,128)(2,1)}, bf16[2,256,384]{2,1,0:T(8,128)(2,1)S(1)}, u32[]{:S(2)}, u32[]{:S(2)}) collective-permute-start(bf16[2,256,384]{2,1,0:T(8,128)(2,1)} %pad_maximum_fusion.3), channel_id=1, source_target_pairs={{0,8},{4,12},{8,16},{12,20},{16,24},{20,28},{24,0},{28,4},{1,9},{5... | collective-permute-start | bytes 1179656 | tf_op jit(solution)/shard_map/ppermute | solution.py:129
  17.5 17.0 %collective-permute-start.1 = (bf16[128,1536]{1,0:T(8,128)(2,1)}, bf16[128,1536]{1,0:T(8,128)(2,1)}, u32[]{:S(2)}, u32[]{:S(2)}) collective-permute-start(bf16[128,1536]{1,0:T(8,128)(2,1)} %get-tuple-element.38), channel_id=1, source_target_pairs={{0,4},{4,0},{8,12},{12,8},{16,20},{20,16},{24,28},{28,24},{1,5},{5... | collective-permute-start | bytes 1179656 | tf_op jit(solution)/shard_map/ppermute | solution.py:132
  20.9 15.2 %collective-permute-start.4 = (bf16[2,256,384]{2,1,0:T(8,128)(2,1)S(1)}, bf16[2,256,384]{2,1,0:T(8,128)(2,1)S(1)}, u32[]{:S(2)}, u32[]{:S(2)}) collective-permute-start(bf16[2,256,384]{2,1,0:T(8,128)(2,1)S(1)} %collective-permute-done.kv_par), channel_id=1, source_target_pairs={{0,8},{4,12},{8,16},{12,20},{16,24},{20,28},{24,0},{28,4},{1,9},{5... | collective-permute-start | bytes 1179656 | tf_op jit(solution)/shard_map/ppermute | solution.py:129
  25.9 20.2 %collective-permute-start.16 = (bf16[384,1536]{1,0:T(8,128)(2,1)}, bf16[384,1536]{1,0:T(8,128)(2,1)S(1)}, u32[]{:S(2)}, u32[]{:S(2)}) collective-permute-start(bf16[384,1536]{1,0:T(8,128)(2,1)} %param.12), channel_id=1, source_target_pairs={{0,1},{1,0},{2,3},{3,2},{4,5},{5,4},{6,7},{7,6},{8,9},{9,8},{10,11... | collective-permute-start | bytes 3538952 | tf_op jit(solution)/shard_map/ppermute | solution.py:132
  29.3 13.4 %collective-permute-start.9 = (bf16[128,1536]{1,0:T(8,128)(2,1)}, bf16[128,1536]{1,0:T(8,128)(2,1)S(1)}, u32[]{:S(2)}, u32[]{:S(2)}) collective-permute-start(bf16[128,1536]{1,0:T(8,128)(2,1)} %get-tuple-element.41), channel_id=1, source_target_pairs={{0,4},{4,0},{8,12},{12,8},{16,20},{20,16},{24,28},{28,24},{1,5},{5... | collective-permute-start | bytes 1179656 | tf_op jit(solution)/shard_map/ppermute | solution.py:132
  36.0 15.2 %collective-permute-start.2 = (bf16[256,384]{1,0:T(8,128)(2,1)S(1)}, bf16[256,384]{1,0:T(8,128)(2,1)S(1)}, u32[]{:S(2)}, u32[]{:S(2)}) collective-permute-start(bf16[256,384]{1,0:T(8,128)(2,1)S(1)} %get-tuple-element.39), channel_id=1, source_target_pairs={{0,4},{4,0},{8,12},{12,8},{16,20},{20,16},{24,28},{28,24},{1,5},{5... | collective-permute-start | bytes 589832 | tf_op jit(solution)/shard_map/ppermute | solution.py:132
  42.8 12.3 %collective-permute-start.5 = (bf16[2,256,384]{2,1,0:T(8,128)(2,1)S(1)}, bf16[2,256,384]{2,1,0:T(8,128)(2,1)S(1)}, u32[]{:S(2)}, u32[]{:S(2)}) collective-permute-start(bf16[2,256,384]{2,1,0:T(8,128)(2,1)S(1)} %broadcast_select_fusion.9), channel_id=1, source_target_pairs={{0,8},{4,12},{8,16},{12,20},{16,24},{20,28},{24,0},{28,4},{1,9},{5... | collective-permute-start | bytes 1179656 | tf_op jit(solution)/shard_map/ppermute | solution.py:129
  44.5 38.3 %collective-permute-start.12 = (bf16[256,384]{1,0:T(8,128)(2,1)S(1)}, bf16[256,384]{1,0:T(8,128)(2,1)S(1)}, u32[]{:S(2)}, u32[]{:S(2)}) collective-permute-start(bf16[256,384]{1,0:T(8,128)(2,1)S(1)} %get-tuple-element.48), channel_id=1, source_target_pairs={{0,4},{4,0},{8,12},{12,8},{16,20},{20,16},{24,28},{28,24},{1,5},{5... | collective-permute-start | bytes 589832 | tf_op jit(solution)/shard_map/ppermute | solution.py:132
  46.1 37.3 %collective-permute-start.15 = (bf16[2,256,384]{2,1,0:T(8,128)(2,1)S(1)}, bf16[2,256,384]{2,1,0:T(8,128)(2,1)S(1)}, u32[]{:S(2)}, u32[]{:S(2)}) collective-permute-start(bf16[2,256,384]{2,1,0:T(8,128)(2,1)S(1)} %broadcast_select_fusion.8), channel_id=1, source_target_pairs={{0,8},{4,12},{8,16},{12,20},{16,24},{20,28},{24,0},{28,4},{1,9},{5... | collective-permute-start | bytes 1179656 | tf_op jit(solution)/shard_map/ppermute | solution.py:129
  70.2 23.5 %collective-permute-start.21 = (bf16[2,256,384]{2,1,0:T(8,128)(2,1)S(1)}, bf16[2,256,384]{2,1,0:T(8,128)(2,1)S(1)}, u32[]{:S(2)}, u32[]{:S(2)}) collective-permute-start(bf16[2,256,384]{2,1,0:T(8,128)(2,1)S(1)} %get-tuple-element.57), channel_id=1, source_target_pairs={{0,24},{4,28},{8,0},{12,4},{16,8},{20,12},{24,16},{28,20},{1,25},{... | collective-permute-start | bytes 1179656 | tf_op jit(solution)/shard_map/ppermute | solution.py:129
  76.2 40.4 %collective-permute-start.11 = (bf16[2,256,384]{2,1,0:T(8,128)(2,1)S(1)}, bf16[2,256,384]{2,1,0:T(8,128)(2,1)S(1)}, u32[]{:S(2)}, u32[]{:S(2)}) collective-permute-start(bf16[2,256,384]{2,1,0:T(8,128)(2,1)S(1)} %get-tuple-element.47), channel_id=1, source_target_pairs={{0,4},{4,0},{8,12},{12,8},{16,20},{20,16},{24,28},{28,24},{1,5},{5... | collective-permute-start | bytes 1179656 | tf_op jit(solution)/shard_map/ppermute | solution.py:132
  78.2 16.7 %collective-permute-start.18 = (bf16[2,256,384]{2,1,0:T(8,128)(2,1)S(1)}, bf16[2,256,384]{2,1,0:T(8,128)(2,1)S(1)}, u32[]{:S(2)}, u32[]{:S(2)}) collective-permute-start(bf16[2,256,384]{2,1,0:T(8,128)(2,1)S(1)} %add_convert_fusion.5), channel_id=1, source_target_pairs={{0,24},{4,28},{8,0},{12,4},{16,8},{20,12},{24,16},{28,20},{1,25},{... | collective-permute-start | bytes 1179656 | tf_op jit(solution)/shard_map/ppermute | solution.py:129
  82.8 14.1 %collective-permute-start.19 = (bf16[4,48,1536]{2,1,0:T(8,128)(2,1)S(1)}, bf16[4,48,1536]{2,1,0:T(8,128)(2,1)S(1)}, u32[]{:S(2)}, u32[]{:S(2)}) collective-permute-start(bf16[4,48,1536]{2,1,0:T(8,128)(2,1)S(1)} %fusion.15), channel_id=1, source_target_pairs={{0,2},{1,3},{2,0},{3,1},{4,6},{5,7},{6,4},{7,5},{8,10},{9,11},{10,... | collective-permute-start | bytes 1769480 | tf_op jit(solution)/shard_map/ppermute | solution.py:129
  94.9 22.4 %collective-permute-start.20 = (bf16[2,256,384]{2,1,0:T(8,128)(2,1)S(1)}, bf16[2,256,384]{2,1,0:T(8,128)(2,1)S(1)}, u32[]{:S(2)}, u32[]{:S(2)}) collective-permute-start(bf16[2,256,384]{2,1,0:T(8,128)(2,1)S(1)} %get-tuple-element.54), channel_id=1, source_target_pairs={{0,4},{4,0},{8,12},{12,8},{16,20},{20,16},{24,28},{28,24},{1,5},{5... | collective-permute-start | bytes 1179656 | tf_op jit(solution)/shard_map/ppermute | solution.py:132
  101.6 10.9 %collective-permute-start.27 = (bf16[48,1536]{1,0:T(8,128)(2,1)S(1)}, bf16[48,1536]{1,0:T(8,128)(2,1)S(1)}, u32[]{:S(2)}, u32[]{:S(2)}) collective-permute-start(bf16[48,1536]{1,0:T(8,128)(2,1)S(1)} %get-tuple-element.94), channel_id=1, source_target_pairs={{0,16},{4,20},{8,24},{12,28},{16,0},{20,4},{24,8},{28,12},{1,17},{... | collective-permute-start | bytes 442376 | tf_op jit(solution)/shard_map/ppermute | solution.py:129
  104.1 11.9 %collective-permute-start.28 = (bf16[48,1536]{1,0:T(8,128)(2,1)S(1)}, bf16[48,1536]{1,0:T(8,128)(2,1)S(1)}, u32[]{:S(2)}, u32[]{:S(2)}) collective-permute-start(bf16[48,1536]{1,0:T(8,128)(2,1)S(1)} %get-tuple-element.93), channel_id=1, source_target_pairs={{0,24},{4,28},{8,0},{12,4},{16,8},{20,12},{24,16},{28,20},{1,25},{... | collective-permute-start | bytes 442376 | tf_op jit(solution)/shard_map/ppermute | solution.py:129
  108.7 16.9 %collective-permute-start.24 = (bf16[2,256,384]{2,1,0:T(8,128)(2,1)S(1)}, bf16[2,256,384]{2,1,0:T(8,128)(2,1)S(1)}, u32[]{:S(2)}, u32[]{:S(2)}) collective-permute-start(bf16[2,256,384]{2,1,0:T(8,128)(2,1)S(1)} %get-tuple-element.77), channel_id=1, source_target_pairs={{0,4},{4,0},{8,12},{12,8},{16,20},{20,16},{24,28},{28,24},{1,5},{5... | collective-permute-start | bytes 1179656 | tf_op jit(solution)/shard_map/ppermute | solution.py:132
  112.5 13.0 %collective-permute-start.23 = (bf16[2,256,384]{2,1,0:T(8,128)(2,1)S(1)}, bf16[2,256,384]{2,1,0:T(8,128)(2,1)S(1)}, u32[]{:S(2)}, u32[]{:S(2)}) collective-permute-start(bf16[2,256,384]{2,1,0:T(8,128)(2,1)S(1)} %get-tuple-element.80), channel_id=1, source_target_pairs={{0,24},{4,28},{8,0},{12,4},{16,8},{20,12},{24,16},{28,20},{1,25},{... | collective-permute-start | bytes 1179656 | tf_op jit(solution)/shard_map/ppermute | solution.py:129
  116.0 15.0 %collective-permute-start.29 = (bf16[2,256,384]{2,1,0:T(8,128)(2,1)S(1)}, bf16[2,256,384]{2,1,0:T(8,128)(2,1)S(1)}, u32[]{:S(2)}, u32[]{:S(2)}) collective-permute-start(bf16[2,256,384]{2,1,0:T(8,128)(2,1)S(1)} %get-tuple-element.69), channel_id=1, source_target_pairs={{0,24},{4,28},{8,0},{12,4},{16,8},{20,12},{24,16},{28,20},{1,25},{... | collective-permute-start | bytes 1179656 | tf_op jit(solution)/shard_map/ppermute | solution.py:129
  116.7 13.5 %collective-permute-start.31 = (bf16[48,1536]{1,0:T(8,128)(2,1)S(1)}, bf16[48,1536]{1,0:T(8,128)(2,1)S(1)}, u32[]{:S(2)}, u32[]{:S(2)}) collective-permute-start(bf16[48,1536]{1,0:T(8,128)(2,1)S(1)} %fusion.39), channel_id=1, source_target_pairs={{0,0},{1,4},{2,2},{3,6},{4,1},{5,5},{6,3},{7,7},{8,8},{9,12},{10,1... | collective-permute-start | bytes 442376 | tf_op jit(solution)/shard_map/ppermute | solution.py:242
  (18 other events, 114.2 us)

commit v5 on v4

--- a/solution.py
+++ b/solution.py
@@ -59,7 +59,7 @@
         inverse = 1.0 / total
         prob.append({j: e[j] * inverse for j in sets[i]})
         low.append({j: prob[i][j].astype(BF16) for j in sets[i]})
-        out_t.append(functools.reduce(jnp.add, [dot(values_t[j], low[i][j]) for j in sets[i]]))
+        out_t.append(dot(jnp.concatenate([values_t[j] for j in sets[i]], axis=1), jnp.concatenate([low[i][j] for j in sets[i]], axis=0)))
     outs, dqs = [], []
     for i in range(2):
         out = out_t[i].T.astype(BF16)
@@ -68,7 +68,7 @@
         grad_low.append({
             j: (prob[i][j] * (rows_dot(values[j], g[i]) - delta)).astype(BF16) for j in sets[i]
         })
-        dq = functools.reduce(jnp.add, [dot(keys_t[j], grad_low[i][j]) for j in sets[i]])
+        dq = dot(jnp.concatenate([keys_t[j] for j in sets[i]], axis=1), jnp.concatenate([grad_low[i][j] for j in sets[i]], axis=0))
         dqs.append((dq * scale).T.astype(BF16))
     for n, (own, par) in enumerate((by_block(*outs), by_block(*dqs))):
         od_own[n] = own

time: 135 us -> 135 us (level)
  no operation moved by 1% of the time
where the time goes in v5:
time: 135 us
  waiting for transfers between devices  55.1 us (41%)
  starting transfers between devices  40.4 us (30%)
  Pallas kernels  20.4 us (15%)
  matrix products  6.6 us (5%)
  other arithmetic  5.73 us (4%)
  local copies, waits for them, and re-layouts  5.67 us (4%)
    ppermute x17, waiting for transfers between devices, shift(): return lax.ppermute(a, axis, [(i, (i + by) % n) for i in range(n)])  33.3 us
    ppermute x17, starting transfers between devices, shift(): return lax.ppermute(a, axis, [(i, (i + by) % n) for i in range(n)])  27.2 us
    ppermute x14, waiting for transfers between devices, swap(): lax.ppermute(a, axis, [(i, i ^ 1) for i in range(lax.axis_size(axis))])  21.8 us
    pallas_call x2, Pallas kernels, attention(): pl.pallas_call(attention_body, out_shape=(out,) * 7, grid_spec=pltpu.Pref...  20.4 us
    ppermute x14, starting transfers between devices, swap(): lax.ppermute(a, axis, [(i, i ^ 1) for i in range(lax.axis_size(axis))])  12.5 us
  transfers between devices with their start and end apart: 32, of which 15 were waited for; matrix products, arithmetic and copies ran while one was open for 12% of the time, Pallas kernels for 15%

profile of v5, /device:TPU:0, one launch (start us, length us, event | category | flops | bytes accessed | tf_op | source)
XLA Modules:
  0.0 135.0 jit_solution(13668447131610860154)
XLA Ops:
  0.6 3.0 %collective-permute-start.6 = (bf16[384,1536]{1,0:T(8,128)(2,1)}, bf16[384,1536]{1,0:T(8,128)(2,1)}, u32[]{:S(2)}, u32[]{:S(2)}) collective-permute-start(bf16[384,1536]{1,0:T(8,128)(2,1)} %param.12), channel_id=1, source_target_pairs={{0,2},{1,3},{2,0},{3,1},{4,6},{5,7},{6,4},{7,5},{8,10},{9,11},{10,... | collective-permute-start | bytes 3538952 | tf_op jit(solution)/shard_map/ppermute | solution.py:129
  3.7 1.7 %constant_dynamic-slice_fusion = (bf16[1,256,384]{2,1,0:T(8,128)(2,1)S(1)}, bf16[1,256,384]{2,1,0:T(8,128)(2,1)S(1)}, bf16[1,256,384]{2,1,0:T(8,128)(2,1)S(1)}, ...) fusion(bf16[1,256,1536]{2,1,0:T(8,128)(2,1)} %param.9, ...), kind=kLoop, calls=%fused_computation.90 | loop fusion | bytes 3145744 | tf_op jit(solution)/shard_map/dynamic_slice | solution.py:144
  13.2 4.2 %collective-permute-done.kv_par = bf16[2,256,384]{2,1,0:T(8,128)(2,1)S(1)} collective-permute-done((bf16[2,256,384]{2,1,0:T(8,128)(2,1)S(1)}, bf16[2,256,384]{2,1,0:T(8,128)(2,1)S(1)}, u32[]{:S(2)}, u32[]{:S(2)}) %collective-permute-start) | collective-permute-done | bytes 393248 | tf_op jit(solution)/shard_map/ppermute | solution.py:132
  19.0 1.9 %collective-permute-done.3.near_own = bf16[2,256,384]{2,1,0:T(8,128)(2,1)S(1)} collective-permute-done((bf16[2,256,384]{2,1,0:T(8,128)(2,1)S(1)}, bf16[2,256,384]{2,1,0:T(8,128)(2,1)S(1)}, u32[]{:S(2)}, u32[]{:S(2)}) %collective-permute-start.3) | collective-permute-done | bytes 393248 | tf_op jit(solution)/shard_map/ppermute | solution.py:129
  21.0 4.9 %collective-permute-done.8.kv_par = bf16[2,256,384]{2,1,0:T(8,128)(2,1)S(1)} collective-permute-done((bf16[2,256,384]{2,1,0:T(8,128)(2,1)}, bf16[2,256,384]{2,1,0:T(8,128)(2,1)S(1)}, u32[]{:S(2)}, u32[]{:S(2)}) %collective-permute-start.8) | collective-permute-done | bytes 393248 | tf_op jit(solution)/shard_map/ppermute | solution.py:132
  26.0 3.3 %collective-permute-done.13.near_own = bf16[2,256,384]{2,1,0:T(8,128)(2,1)S(1)} collective-permute-done((bf16[2,256,384]{2,1,0:T(8,128)(2,1)}, bf16[2,256,384]{2,1,0:T(8,128)(2,1)S(1)}, u32[]{:S(2)}, u32[]{:S(2)}) %collective-permute-start.13) | collective-permute-done | bytes 393248 | tf_op jit(solution)/shard_map/ppermute | solution.py:129
  29.9 4.6 %collective-permute-done.1 = bf16[128,1536]{1,0:T(8,128)(2,1)} collective-permute-done((bf16[128,1536]{1,0:T(8,128)(2,1)}, bf16[128,1536]{1,0:T(8,128)(2,1)}, u32[]{:S(2)}, u32[]{:S(2)}) %collective-permute-start.1) | collective-permute-done | bytes 393248 | tf_op jit(solution)/shard_map/ppermute | solution.py:132
  38.6 4.2 %collective-permute-done.9 = bf16[128,1536]{1,0:T(8,128)(2,1)S(1)} collective-permute-done((bf16[128,1536]{1,0:T(8,128)(2,1)}, bf16[128,1536]{1,0:T(8,128)(2,1)S(1)}, u32[]{:S(2)}, u32[]{:S(2)}) %collective-permute-start.9) | collective-permute-done | bytes 393248 | tf_op jit(solution)/shard_map/ppermute | solution.py:132
  51.2 3.9 %collective-permute-done.5.far = bf16[2,256,384]{2,1,0:T(8,128)(2,1)S(1)} collective-permute-done((bf16[2,256,384]{2,1,0:T(8,128)(2,1)S(1)}, bf16[2,256,384]{2,1,0:T(8,128)(2,1)S(1)}, u32[]{:S(2)}, u32[]{:S(2)}) %collective-permute-start.5) | collective-permute-done | bytes 393248 | tf_op jit(solution)/shard_map/ppermute | solution.py:129
  55.1 10.2 %attention.2 = (bf16[2,256,384]{2,1,0:T(8,128)(2,1)S(1)}, bf16[2,256,384]{2,1,0:T(8,128)(2,1)S(1)}, bf16[2,256,384]{2,1,0:T(8,128)(2,1)S(1)}, bf16[2,256,384]{2,...) custom-call(s32[2]{0:T(128)S(1)} %pad_add_fusion.place, ...), custom_call_target="tpu_custom_call" | custom-call | flops 6442450944 | bytes 4718592 | tf_op jit(solution)/shard_map/attention/pallas_call | solution.py:96
  65.3 3.1 %collective-permute-start.10 = (bf16[2,256,384]{2,1,0:T(8,128)(2,1)S(1)}, bf16[2,256,384]{2,1,0:T(8,128)(2,1)S(1)}, u32[]{:S(2)}, u32[]{:S(2)}) collective-permute-start(bf16[2,256,384]{2,1,0:T(8,128)(2,1)S(1)} %get-tuple-element.46), channel_id=1, source_target_pairs={{0,24},{4,28},{8,0},{12,4},{16,8},{20,12},{24,16},{28,20},{1,25},{... | collective-permute-start | bytes 1179656 | tf_op jit(solution)/shard_map/ppermute | solution.py:129
  70.3 5.9 %collective-permute-done.10 = bf16[2,256,384]{2,1,0:T(8,128)(2,1)S(1)} collective-permute-done((bf16[2,256,384]{2,1,0:T(8,128)(2,1)S(1)}, bf16[2,256,384]{2,1,0:T(8,128)(2,1)S(1)}, u32[]{:S(2)}, u32[]{:S(2)}) %collective-permute-start.10) | collective-permute-done | bytes 393248 | tf_op jit(solution)/shard_map/ppermute | solution.py:129
  76.2 1.8 %collective-permute-start.11 = (bf16[2,256,384]{2,1,0:T(8,128)(2,1)S(1)}, bf16[2,256,384]{2,1,0:T(8,128)(2,1)S(1)}, u32[]{:S(2)}, u32[]{:S(2)}) collective-permute-start(bf16[2,256,384]{2,1,0:T(8,128)(2,1)S(1)} %get-tuple-element.47), channel_id=1, source_target_pairs={{0,4},{4,0},{8,12},{12,8},{16,20},{20,16},{24,28},{28,24},{1,5},{5... | collective-permute-start | bytes 1179656 | tf_op jit(solution)/shard_map/ppermute | solution.py:132
  78.1 4.5 %collective-permute-start.18 = (bf16[2,256,384]{2,1,0:T(8,128)(2,1)S(1)}, bf16[2,256,384]{2,1,0:T(8,128)(2,1)S(1)}, u32[]{:S(2)}, u32[]{:S(2)}) collective-permute-start(bf16[2,256,384]{2,1,0:T(8,128)(2,1)S(1)} %add_convert_fusion.5), channel_id=1, source_target_pairs={{0,24},{4,28},{8,0},{12,4},{16,8},{20,12},{24,16},{28,20},{1,25},{... | collective-permute-start | bytes 1179656 | tf_op jit(solution)/shard_map/ppermute | solution.py:129
  83.3 10.2 %attention.3 = (bf16[2,256,384]{2,1,0:T(8,128)(2,1)S(1)}, bf16[2,256,384]{2,1,0:T(8,128)(2,1)S(1)}, bf16[2,256,384]{2,1,0:T(8,128)(2,1)S(1)}, bf16[2,256,384]{2,...) custom-call(s32[2]{0:T(128)S(1)} %pad_add_fusion.1.place, ...), custom_call_target="tpu_custom_call" | custom-call | flops 6442450944 | bytes 4718592 | tf_op jit(solution)/shard_map/attention/pallas_call | solution.py:96
  97.0 4.4 %collective-permute-done.22 = bf16[2,256,384]{2,1,0:T(8,128)(2,1)S(1)} collective-permute-done((bf16[2,256,384]{2,1,0:T(8,128)(2,1)S(1)}, bf16[2,256,384]{2,1,0:T(8,128)(2,1)S(1)}, u32[]{:S(2)}, u32[]{:S(2)}) %collective-permute-start.22) | collective-permute-done | bytes 393248 | tf_op jit(solution)/shard_map/ppermute | solution.py:129
  101.5 2.5 %collective-permute-start.27 = (bf16[48,1536]{1,0:T(8,128)(2,1)S(1)}, bf16[48,1536]{1,0:T(8,128)(2,1)S(1)}, u32[]{:S(2)}, u32[]{:S(2)}) collective-permute-start(bf16[48,1536]{1,0:T(8,128)(2,1)S(1)} %get-tuple-element.94), channel_id=1, source_target_pairs={{0,16},{4,20},{8,24},{12,28},{16,0},{20,4},{24,8},{28,12},{1,17},{... | collective-permute-start | bytes 442376 | tf_op jit(solution)/shard_map/ppermute | solution.py:129
  105.5 3.1 %collective-permute-done.26 = bf16[48,1536]{1,0:T(8,128)(2,1)S(1)} collective-permute-done((bf16[48,1536]{1,0:T(8,128)(2,1)S(1)}, bf16[48,1536]{1,0:T(8,128)(2,1)S(1)}, u32[]{:S(2)}, u32[]{:S(2)}) %collective-permute-start.26) | collective-permute-done | bytes 147488 | tf_op jit(solution)/shard_map/ppermute | solution.py:129
  109.9 2.5 %collective-permute-done.27 = bf16[48,1536]{1,0:T(8,128)(2,1)S(1)} collective-permute-done((bf16[48,1536]{1,0:T(8,128)(2,1)S(1)}, bf16[48,1536]{1,0:T(8,128)(2,1)S(1)}, u32[]{:S(2)}, u32[]{:S(2)}) %collective-permute-start.27) | collective-permute-done | bytes 147488 | tf_op jit(solution)/shard_map/ppermute | solution.py:129
  112.4 3.5 %collective-permute-start.23 = (bf16[2,256,384]{2,1,0:T(8,128)(2,1)S(1)}, bf16[2,256,384]{2,1,0:T(8,128)(2,1)S(1)}, u32[]{:S(2)}, u32[]{:S(2)}) collective-permute-start(bf16[2,256,384]{2,1,0:T(8,128)(2,1)S(1)} %get-tuple-element.80), channel_id=1, source_target_pairs={{0,24},{4,28},{8,0},{12,4},{16,8},{20,12},{24,16},{28,20},{1,25},{... | collective-permute-start | bytes 1179656 | tf_op jit(solution)/shard_map/ppermute | solution.py:129
  117.3 8.1 %collective-permute-done.23 = bf16[2,256,384]{2,1,0:T(8,128)(2,1)S(1)} collective-permute-done((bf16[2,256,384]{2,1,0:T(8,128)(2,1)S(1)}, bf16[2,256,384]{2,1,0:T(8,128)(2,1)S(1)}, u32[]{:S(2)}, u32[]{:S(2)}) %collective-permute-start.23) | collective-permute-done | bytes 393248 | tf_op jit(solution)/shard_map/ppermute | solution.py:129
  125.7 1.9 %collective-permute-start.30 = (bf16[2,256,384]{2,1,0:T(8,128)(2,1)S(1)}, bf16[2,256,384]{2,1,0:T(8,128)(2,1)S(1)}, u32[]{:S(2)}, u32[]{:S(2)}) collective-permute-start(bf16[2,256,384]{2,1,0:T(8,128)(2,1)S(1)} %add_convert_fusion.1), channel_id=1, source_target_pairs={{0,4},{4,0},{8,12},{12,8},{16,20},{20,16},{24,28},{28,24},{1,5},{5... | collective-permute-start | bytes 1179656 | tf_op jit(solution)/shard_map/ppermute | solution.py:132
  127.7 2.3 %fusion.11 = bf16[1,256,1536]{2,1,0:T(8,128)(2,1)} fusion(bf16[384,1536]{1,0:T(8,128)(2,1)S(1)} %get-tuple-element.76, bf16[384,1536]{1,0:T(8,128)(2,1)S(1)} %get-tuple-element.75, bf16[384,1536]{1,0:T(8,128)(2,1)S(1)} %get-tuple-element.74, bf16[384,1536]{1,0:T(8,128)(2,1)S(1)} %get-tuple-element.73, bf16[256,384]{1,0:T(8,128)(2,1)S(1)} %get-tuple-element.103, ...), kind=kOutput, calls=%fused_computation.11 | convolution fusion | flops 1230372864 | bytes 6291456 | tf_op jit(solution)/shard_map/dot_general | solution.py:253
  130.9 2.7 %collective-permute-done.30 = bf16[2,256,384]{2,1,0:T(8,128)(2,1)S(1)} collective-permute-done((bf16[2,256,384]{2,1,0:T(8,128)(2,1)S(1)}, bf16[2,256,384]{2,1,0:T(8,128)(2,1)S(1)}, u32[]{:S(2)}, u32[]{:S(2)}) %collective-permute-start.30) | collective-permute-done | bytes 393248 | tf_op jit(solution)/shard_map/ppermute | solution.py:132
  (110 shorter events, 35.6 us)
Async XLA Ops:
  0.6 43.7 %collective-permute-start.6 = (bf16[384,1536]{1,0:T(8,128)(2,1)}, bf16[384,1536]{1,0:T(8,128)(2,1)}, u32[]{:S(2)}, u32[]{:S(2)}) collective-permute-start(bf16[384,1536]{1,0:T(8,128)(2,1)} %param.12), channel_id=1, source_target_pairs={{0,2},{1,3},{2,0},{3,1},{4,6},{5,7},{6,4},{7,5},{8,10},{9,11},{10,... | collective-permute-start | bytes 3538952 | tf_op jit(solution)/shard_map/ppermute | solution.py:129
  5.4 12.1 %collective-permute-start = (bf16[2,256,384]{2,1,0:T(8,128)(2,1)S(1)}, bf16[2,256,384]{2,1,0:T(8,128)(2,1)S(1)}, u32[]{:S(2)}, u32[]{:S(2)}) collective-permute-start(bf16[2,256,384]{2,1,0:T(8,128)(2,1)S(1)} %pad_maximum_fusion), channel_id=1, source_target_pairs={{0,4},{4,0},{8,12},{12,8},{16,20},{20,16},{24,28},{28,24},{1,5},{5... | collective-permute-start | bytes 1179656 | tf_op jit(solution)/shard_map/ppermute | solution.py:132
  7.0 13.9 %collective-permute-start.3 = (bf16[2,256,384]{2,1,0:T(8,128)(2,1)S(1)}, bf16[2,256,384]{2,1,0:T(8,128)(2,1)S(1)}, u32[]{:S(2)}, u32[]{:S(2)}) collective-permute-start(bf16[2,256,384]{2,1,0:T(8,128)(2,1)S(1)} %pad_maximum_fusion.1), channel_id=1, source_target_pairs={{0,8},{4,12},{8,16},{12,20},{16,24},{20,28},{24,0},{28,4},{1,9},{5... | collective-permute-start | bytes 1179656 | tf_op jit(solution)/shard_map/ppermute | solution.py:129
  9.4 16.5 %collective-permute-start.8 = (bf16[2,256,384]{2,1,0:T(8,128)(2,1)}, bf16[2,256,384]{2,1,0:T(8,128)(2,1)S(1)}, u32[]{:S(2)}, u32[]{:S(2)}) collective-permute-start(bf16[2,256,384]{2,1,0:T(8,128)(2,1)} %pad_maximum_fusion.2), channel_id=1, source_target_pairs={{0,4},{4,0},{8,12},{12,8},{16,20},{20,16},{24,28},{28,24},{1,5},{5... | collective-permute-start | bytes 1179656 | tf_op jit(solution)/shard_map/ppermute | solution.py:132
  10.7 18.6 %collective-permute-start.13 = (bf16[2,256,384]{2,1,0:T(8,128)(2,1)}, bf16[2,256,384]{2,1,0:T(8,128)(2,1)S(1)}, u32[]{:S(2)}, u32[]{:S(2)}) collective-permute-start(bf16[2,256,384]{2,1,0:T(8,128)(2,1)} %pad_maximum_fusion.3), channel_id=1, source_target_pairs={{0,8},{4,12},{8,16},{12,20},{16,24},{20,28},{24,0},{28,4},{1,9},{5... | collective-permute-start | bytes 1179656 | tf_op jit(solution)/shard_map/ppermute | solution.py:129
  17.5 17.0 %collective-permute-start.1 = (bf16[128,1536]{1,0:T(8,128)(2,1)}, bf16[128,1536]{1,0:T(8,128)(2,1)}, u32[]{:S(2)}, u32[]{:S(2)}) collective-permute-start(bf16[128,1536]{1,0:T(8,128)(2,1)} %get-tuple-element.38), channel_id=1, source_target_pairs={{0,4},{4,0},{8,12},{12,8},{16,20},{20,16},{24,28},{28,24},{1,5},{5... | collective-permute-start | bytes 1179656 | tf_op jit(solution)/shard_map/ppermute | solution.py:132
  20.9 15.2 %collective-permute-start.4 = (bf16[2,256,384]{2,1,0:T(8,128)(2,1)S(1)}, bf16[2,256,384]{2,1,0:T(8,128)(2,1)S(1)}, u32[]{:S(2)}, u32[]{:S(2)}) collective-permute-start(bf16[2,256,384]{2,1,0:T(8,128)(2,1)S(1)} %collective-permute-done.kv_par), channel_id=1, source_target_pairs={{0,8},{4,12},{8,16},{12,20},{16,24},{20,28},{24,0},{28,4},{1,9},{5... | collective-permute-start | bytes 1179656 | tf_op jit(solution)/shard_map/ppermute | solution.py:129
  25.9 20.2 %collective-permute-start.16 = (bf16[384,1536]{1,0:T(8,128)(2,1)}, bf16[384,1536]{1,0:T(8,128)(2,1)S(1)}, u32[]{:S(2)}, u32[]{:S(2)}) collective-permute-start(bf16[384,1536]{1,0:T(8,128)(2,1)} %param.12), channel_id=1, source_target_pairs={{0,1},{1,0},{2,3},{3,2},{4,5},{5,4},{6,7},{7,6},{8,9},{9,8},{10,11... | collective-permute-start | bytes 3538952 | tf_op jit(solution)/shard_map/ppermute | solution.py:132
  29.3 13.4 %collective-permute-start.9 = (bf16[128,1536]{1,0:T(8,128)(2,1)}, bf16[128,1536]{1,0:T(8,128)(2,1)S(1)}, u32[]{:S(2)}, u32[]{:S(2)}) collective-permute-start(bf16[128,1536]{1,0:T(8,128)(2,1)} %get-tuple-element.41), channel_id=1, source_target_pairs={{0,4},{4,0},{8,12},{12,8},{16,20},{20,16},{24,28},{28,24},{1,5},{5... | collective-permute-start | bytes 1179656 | tf_op jit(solution)/shard_map/ppermute | solution.py:132
  36.0 15.2 %collective-permute-start.2 = (bf16[256,384]{1,0:T(8,128)(2,1)S(1)}, bf16[256,384]{1,0:T(8,128)(2,1)S(1)}, u32[]{:S(2)}, u32[]{:S(2)}) collective-permute-start(bf16[256,384]{1,0:T(8,128)(2,1)S(1)} %get-tuple-element.39), channel_id=1, source_target_pairs={{0,4},{4,0},{8,12},{12,8},{16,20},{20,16},{24,28},{28,24},{1,5},{5... | collective-permute-start | bytes 589832 | tf_op jit(solution)/shard_map/ppermute | solution.py:132
  42.8 12.3 %collective-permute-start.5 = (bf16[2,256,384]{2,1,0:T(8,128)(2,1)S(1)}, bf16[2,256,384]{2,1,0:T(8,128)(2,1)S(1)}, u32[]{:S(2)}, u32[]{:S(2)}) collective-permute-start(bf16[2,256,384]{2,1,0:T(8,128)(2,1)S(1)} %broadcast_select_fusion.9), channel_id=1, source_target_pairs={{0,8},{4,12},{8,16},{12,20},{16,24},{20,28},{24,0},{28,4},{1,9},{5... | collective-permute-start | bytes 1179656 | tf_op jit(solution)/shard_map/ppermute | solution.py:129
  44.5 38.2 %collective-permute-start.12 = (bf16[256,384]{1,0:T(8,128)(2,1)S(1)}, bf16[256,384]{1,0:T(8,128)(2,1)S(1)}, u32[]{:S(2)}, u32[]{:S(2)}) collective-permute-start(bf16[256,384]{1,0:T(8,128)(2,1)S(1)} %get-tuple-element.48), channel_id=1, source_target_pairs={{0,4},{4,0},{8,12},{12,8},{16,20},{20,16},{24,28},{28,24},{1,5},{5... | collective-permute-start | bytes 589832 | tf_op jit(solution)/shard_map/ppermute | solution.py:132
  46.1 37.2 %collective-permute-start.15 = (bf16[2,256,384]{2,1,0:T(8,128)(2,1)S(1)}, bf16[2,256,384]{2,1,0:T(8,128)(2,1)S(1)}, u32[]{:S(2)}, u32[]{:S(2)}) collective-permute-start(bf16[2,256,384]{2,1,0:T(8,128)(2,1)S(1)} %broadcast_select_fusion.8), channel_id=1, source_target_pairs={{0,8},{4,12},{8,16},{12,20},{16,24},{20,28},{24,0},{28,4},{1,9},{5... | collective-permute-start | bytes 1179656 | tf_op jit(solution)/shard_map/ppermute | solution.py:129
  70.1 23.4 %collective-permute-start.21 = (bf16[2,256,384]{2,1,0:T(8,128)(2,1)S(1)}, bf16[2,256,384]{2,1,0:T(8,128)(2,1)S(1)}, u32[]{:S(2)}, u32[]{:S(2)}) collective-permute-start(bf16[2,256,384]{2,1,0:T(8,128)(2,1)S(1)} %get-tuple-element.57), channel_id=1, source_target_pairs={{0,24},{4,28},{8,0},{12,4},{16,8},{20,12},{24,16},{28,20},{1,25},{... | collective-permute-start | bytes 1179656 | tf_op jit(solution)/shard_map/ppermute | solution.py:129
  76.2 40.4 %collective-permute-start.11 = (bf16[2,256,384]{2,1,0:T(8,128)(2,1)S(1)}, bf16[2,256,384]{2,1,0:T(8,128)(2,1)S(1)}, u32[]{:S(2)}, u32[]{:S(2)}) collective-permute-start(bf16[2,256,384]{2,1,0:T(8,128)(2,1)S(1)} %get-tuple-element.47), channel_id=1, source_target_pairs={{0,4},{4,0},{8,12},{12,8},{16,20},{20,16},{24,28},{28,24},{1,5},{5... | collective-permute-start | bytes 1179656 | tf_op jit(solution)/shard_map/ppermute | solution.py:132
  78.1 16.6 %collective-permute-start.18 = (bf16[2,256,384]{2,1,0:T(8,128)(2,1)S(1)}, bf16[2,256,384]{2,1,0:T(8,128)(2,1)S(1)}, u32[]{:S(2)}, u32[]{:S(2)}) collective-permute-start(bf16[2,256,384]{2,1,0:T(8,128)(2,1)S(1)} %add_convert_fusion.5), channel_id=1, source_target_pairs={{0,24},{4,28},{8,0},{12,4},{16,8},{20,12},{24,16},{28,20},{1,25},{... | collective-permute-start | bytes 1179656 | tf_op jit(solution)/shard_map/ppermute | solution.py:129
  82.8 14.0 %collective-permute-start.19 = (bf16[4,48,1536]{2,1,0:T(8,128)(2,1)S(1)}, bf16[4,48,1536]{2,1,0:T(8,128)(2,1)S(1)}, u32[]{:S(2)}, u32[]{:S(2)}) collective-permute-start(bf16[4,48,1536]{2,1,0:T(8,128)(2,1)S(1)} %fusion.15), channel_id=1, source_target_pairs={{0,2},{1,3},{2,0},{3,1},{4,6},{5,7},{6,4},{7,5},{8,10},{9,11},{10,... | collective-permute-start | bytes 1769480 | tf_op jit(solution)/shard_map/ppermute | solution.py:129
  94.8 22.5 %collective-permute-start.20 = (bf16[2,256,384]{2,1,0:T(8,128)(2,1)S(1)}, bf16[2,256,384]{2,1,0:T(8,128)(2,1)S(1)}, u32[]{:S(2)}, u32[]{:S(2)}) collective-permute-start(bf16[2,256,384]{2,1,0:T(8,128)(2,1)S(1)} %get-tuple-element.54), channel_id=1, source_target_pairs={{0,4},{4,0},{8,12},{12,8},{16,20},{20,16},{24,28},{28,24},{1,5},{5... | collective-permute-start | bytes 1179656 | tf_op jit(solution)/shard_map/ppermute | solution.py:132
  101.5 10.9 %collective-permute-start.27 = (bf16[48,1536]{1,0:T(8,128)(2,1)S(1)}, bf16[48,1536]{1,0:T(8,128)(2,1)S(1)}, u32[]{:S(2)}, u32[]{:S(2)}) collective-permute-start(bf16[48,1536]{1,0:T(8,128)(2,1)S(1)} %get-tuple-element.94), channel_id=1, source_target_pairs={{0,16},{4,20},{8,24},{12,28},{16,0},{20,4},{24,8},{28,12},{1,17},{... | collective-permute-start | bytes 442376 | tf_op jit(solution)/shard_map/ppermute | solution.py:129
  104.0 11.9 %collective-permute-start.28 = (bf16[48,1536]{1,0:T(8,128)(2,1)S(1)}, bf16[48,1536]{1,0:T(8,128)(2,1)S(1)}, u32[]{:S(2)}, u32[]{:S(2)}) collective-permute-start(bf16[48,1536]{1,0:T(8,128)(2,1)S(1)} %get-tuple-element.93), channel_id=1, source_target_pairs={{0,24},{4,28},{8,0},{12,4},{16,8},{20,12},{24,16},{28,20},{1,25},{... | collective-permute-start | bytes 442376 | tf_op jit(solution)/shard_map/ppermute | solution.py:129
  108.6 17.0 %collective-permute-start.24 = (bf16[2,256,384]{2,1,0:T(8,128)(2,1)S(1)}, bf16[2,256,384]{2,1,0:T(8,128)(2,1)S(1)}, u32[]{:S(2)}, u32[]{:S(2)}) collective-permute-start(bf16[2,256,384]{2,1,0:T(8,128)(2,1)S(1)} %get-tuple-element.77), channel_id=1, source_target_pairs={{0,4},{4,0},{8,12},{12,8},{16,20},{20,16},{24,28},{28,24},{1,5},{5... | collective-permute-start | bytes 1179656 | tf_op jit(solution)/shard_map/ppermute | solution.py:132
  112.4 13.1 %collective-permute-start.23 = (bf16[2,256,384]{2,1,0:T(8,128)(2,1)S(1)}, bf16[2,256,384]{2,1,0:T(8,128)(2,1)S(1)}, u32[]{:S(2)}, u32[]{:S(2)}) collective-permute-start(bf16[2,256,384]{2,1,0:T(8,128)(2,1)S(1)} %get-tuple-element.80), channel_id=1, source_target_pairs={{0,24},{4,28},{8,0},{12,4},{16,8},{20,12},{24,16},{28,20},{1,25},{... | collective-permute-start | bytes 1179656 | tf_op jit(solution)/shard_map/ppermute | solution.py:129
  115.9 15.0 %collective-permute-start.29 = (bf16[2,256,384]{2,1,0:T(8,128)(2,1)S(1)}, bf16[2,256,384]{2,1,0:T(8,128)(2,1)S(1)}, u32[]{:S(2)}, u32[]{:S(2)}) collective-permute-start(bf16[2,256,384]{2,1,0:T(8,128)(2,1)S(1)} %get-tuple-element.69), channel_id=1, source_target_pairs={{0,24},{4,28},{8,0},{12,4},{16,8},{20,12},{24,16},{28,20},{1,25},{... | collective-permute-start | bytes 1179656 | tf_op jit(solution)/shard_map/ppermute | solution.py:129
  116.6 13.4 %collective-permute-start.31 = (bf16[48,1536]{1,0:T(8,128)(2,1)S(1)}, bf16[48,1536]{1,0:T(8,128)(2,1)S(1)}, u32[]{:S(2)}, u32[]{:S(2)}) collective-permute-start(bf16[48,1536]{1,0:T(8,128)(2,1)S(1)} %fusion.39), channel_id=1, source_target_pairs={{0,0},{1,4},{2,2},{3,6},{4,1},{5,5},{6,3},{7,7},{8,8},{9,12},{10,1... | collective-permute-start | bytes 442376 | tf_op jit(solution)/shard_map/ppermute | solution.py:242
  (18 other events, 114.2 us)

commit v6 on v4

--- a/solution.py
+++ b/solution.py
@@ -153,10 +153,10 @@
     held = [shift(out_weight, "fsdp", -2 * (1 + g)) if g < last else out_weight for g in every]
     cot_par, near_par, far, q_par = [], [], [], []
     for g in every:
-        kv, = after([kv_par[g]], near_own[g])
+        kv, = after([kv_par[g]], *near_own[: 1 if g == 0 else groups])
         near_par.append(shift(kv, "seq", 2))
         if g < 2:
-            c, = after([cot[g * half : (g + 1) * half]], kv_par[g])
+            c, = after([cot[g * half : (g + 1) * half]], kv_par[g], near_own[g])
             cot_par.append(swap(c, "seq"))
     for g in every:
         b_near = jnp.where(col == 0, near_par[g], near_own[g])
@@ -212,7 +212,7 @@
             own_d.append((sum_o, swap(sum_p, "seq")))
         else:
             keep, give = terms_of(od_own, od_par)
-            d_far, = after([d_far], from_a)
+            d_far, = after([d_far])
             back = shift(d_far, "seq", -2)
             od_par, = after([od_par], from_b, total)
             par_od.append(swap(od_par, "seq"))
@@ -244,7 +244,7 @@
             own = jnp.where(col == 0, d_near_a, near_b)
             own, = after([own], *pieces)
             from_o = shift(own, "seq", -2)
-            from_o, = after([from_o], for_own, grad_weight)
+            from_o, = after([from_o], for_own)
             sum_o = add(jnp.where(col == 0, d_a, d_b), from_o)
             own_d.append((sum_o, for_own))
 

time: 135 us -> 135 us (level)
    ppermute x17, waiting for transfers between devices: 33.4 us -> 34.9 us  [shift(): return lax.ppermute(a, axis, [(i, (i + by) % n) for i in range(n)])]
where the time goes in v6:
time: 135 us
  waiting for transfers between devices  56.2 us (42%)
  starting transfers between devices  39.3 us (29%)
  Pallas kernels  20.5 us (15%)
  matrix products  6.6 us (5%)
  other arithmetic  5.73 us (4%)
  local copies, waits for them, and re-layouts  5.67 us (4%)
    ppermute x17, waiting for transfers between devices, shift(): return lax.ppermute(a, axis, [(i, (i + by) % n) for i in range(n)])  34.9 us
    ppermute x17, starting transfers between devices, shift(): return lax.ppermute(a, axis, [(i, (i + by) % n) for i in range(n)])  27.2 us
    ppermute x14, waiting for transfers between devices, swap(): lax.ppermute(a, axis, [(i, i ^ 1) for i in range(lax.axis_size(axis))])  21.3 us
    pallas_call x2, Pallas kernels, attention(): pl.pallas_call(attention_body, out_shape=(out,) * 7, grid_spec=pltpu.Pref...  20.5 us
    ppermute x14, starting transfers between devices, swap(): lax.ppermute(a, axis, [(i, i ^ 1) for i in range(lax.axis_size(axis))])  11.5 us
  transfers between devices with their start and end apart: 32, of which 15 were waited for; matrix products, arithmetic and copies ran while one was open for 12% of the time, Pallas kernels for 15%

profile of v6, /device:TPU:0, one launch (start us, length us, event | category | flops | bytes accessed | tf_op | source)
XLA Modules:
  0.0 135.1 jit_solution(13580274297823667982)
XLA Ops:
  0.6 3.0 %collective-permute-start.6 = (bf16[384,1536]{1,0:T(8,128)(2,1)}, bf16[384,1536]{1,0:T(8,128)(2,1)}, u32[]{:S(2)}, u32[]{:S(2)}) collective-permute-start(bf16[384,1536]{1,0:T(8,128)(2,1)} %param.12), channel_id=1, source_target_pairs={{0,2},{1,3},{2,0},{3,1},{4,6},{5,7},{6,4},{7,5},{8,10},{9,11},{10,... | collective-permute-start | bytes 3538952 | tf_op jit(solution)/shard_map/ppermute | solution.py:129
  3.7 1.7 %constant_dynamic-slice_fusion = (bf16[1,256,384]{2,1,0:T(8,128)(2,1)S(1)}, bf16[1,256,384]{2,1,0:T(8,128)(2,1)S(1)}, bf16[1,256,384]{2,1,0:T(8,128)(2,1)S(1)}, ...) fusion(bf16[1,256,1536]{2,1,0:T(8,128)(2,1)} %param.9, ...), kind=kLoop, calls=%fused_computation.90 | loop fusion | bytes 3145744 | tf_op jit(solution)/shard_map/dynamic_slice | solution.py:144
  13.2 4.2 %collective-permute-done.kv_par = bf16[2,256,384]{2,1,0:T(8,128)(2,1)S(1)} collective-permute-done((bf16[2,256,384]{2,1,0:T(8,128)(2,1)S(1)}, bf16[2,256,384]{2,1,0:T(8,128)(2,1)S(1)}, u32[]{:S(2)}, u32[]{:S(2)}) %collective-permute-start) | collective-permute-done | bytes 393248 | tf_op jit(solution)/shard_map/ppermute | solution.py:132
  17.5 3.4 %collective-permute-done.1.near_own = bf16[2,256,384]{2,1,0:T(8,128)(2,1)S(1)} collective-permute-done((bf16[2,256,384]{2,1,0:T(8,128)(2,1)S(1)}, bf16[2,256,384]{2,1,0:T(8,128)(2,1)S(1)}, u32[]{:S(2)}, u32[]{:S(2)}) %collective-permute-start.1) | collective-permute-done | bytes 393248 | tf_op jit(solution)/shard_map/ppermute | solution.py:129
  21.5 4.4 %collective-permute-done.8.kv_par = bf16[2,256,384]{2,1,0:T(8,128)(2,1)S(1)} collective-permute-done((bf16[2,256,384]{2,1,0:T(8,128)(2,1)}, bf16[2,256,384]{2,1,0:T(8,128)(2,1)S(1)}, u32[]{:S(2)}, u32[]{:S(2)}) %collective-permute-start.8) | collective-permute-done | bytes 393248 | tf_op jit(solution)/shard_map/ppermute | solution.py:132
  26.0 3.3 %collective-permute-done.9.near_own = bf16[2,256,384]{2,1,0:T(8,128)(2,1)S(1)} collective-permute-done((bf16[2,256,384]{2,1,0:T(8,128)(2,1)}, bf16[2,256,384]{2,1,0:T(8,128)(2,1)S(1)}, u32[]{:S(2)}, u32[]{:S(2)}) %collective-permute-start.9) | collective-permute-done | bytes 393248 | tf_op jit(solution)/shard_map/ppermute | solution.py:129
  29.9 4.6 %collective-permute-done.2 = bf16[128,1536]{1,0:T(8,128)(2,1)} collective-permute-done((bf16[128,1536]{1,0:T(8,128)(2,1)}, bf16[128,1536]{1,0:T(8,128)(2,1)}, u32[]{:S(2)}, u32[]{:S(2)}) %collective-permute-start.2) | collective-permute-done | bytes 393248 | tf_op jit(solution)/shard_map/ppermute | solution.py:132
  38.6 4.2 %collective-permute-done.10 = bf16[128,1536]{1,0:T(8,128)(2,1)S(1)} collective-permute-done((bf16[128,1536]{1,0:T(8,128)(2,1)}, bf16[128,1536]{1,0:T(8,128)(2,1)S(1)}, u32[]{:S(2)}, u32[]{:S(2)}) %collective-permute-start.10) | collective-permute-done | bytes 393248 | tf_op jit(solution)/shard_map/ppermute | solution.py:132
  51.2 3.9 %collective-permute-done.5.far = bf16[2,256,384]{2,1,0:T(8,128)(2,1)S(1)} collective-permute-done((bf16[2,256,384]{2,1,0:T(8,128)(2,1)S(1)}, bf16[2,256,384]{2,1,0:T(8,128)(2,1)S(1)}, u32[]{:S(2)}, u32[]{:S(2)}) %collective-permute-start.5) | collective-permute-done | bytes 393248 | tf_op jit(solution)/shard_map/ppermute | solution.py:129
  55.1 10.2 %attention.2 = (bf16[2,256,384]{2,1,0:T(8,128)(2,1)S(1)}, bf16[2,256,384]{2,1,0:T(8,128)(2,1)S(1)}, bf16[2,256,384]{2,1,0:T(8,128)(2,1)S(1)}, bf16[2,256,384]{2,...) custom-call(s32[2]{0:T(128)S(1)} %pad_add_fusion.place, ...), custom_call_target="tpu_custom_call" | custom-call | flops 6442450944 | bytes 4718592 | tf_op jit(solution)/shard_map/attention/pallas_call | solution.py:96
  65.4 3.1 %collective-permute-start.11 = (bf16[2,256,384]{2,1,0:T(8,128)(2,1)S(1)}, bf16[2,256,384]{2,1,0:T(8,128)(2,1)S(1)}, u32[]{:S(2)}, u32[]{:S(2)}) collective-permute-start(bf16[2,256,384]{2,1,0:T(8,128)(2,1)S(1)} %get-tuple-element.45), channel_id=1, source_target_pairs={{0,24},{4,28},{8,0},{12,4},{16,8},{20,12},{24,16},{28,20},{1,25},{... | collective-permute-start | bytes 1179656 | tf_op jit(solution)/shard_map/ppermute | solution.py:129
  70.4 5.9 %collective-permute-done.11 = bf16[2,256,384]{2,1,0:T(8,128)(2,1)S(1)} collective-permute-done((bf16[2,256,384]{2,1,0:T(8,128)(2,1)S(1)}, bf16[2,256,384]{2,1,0:T(8,128)(2,1)S(1)}, u32[]{:S(2)}, u32[]{:S(2)}) %collective-permute-start.11) | collective-permute-done | bytes 393248 | tf_op jit(solution)/shard_map/ppermute | solution.py:129
  76.2 1.8 %collective-permute-start.12 = (bf16[2,256,384]{2,1,0:T(8,128)(2,1)S(1)}, bf16[2,256,384]{2,1,0:T(8,128)(2,1)S(1)}, u32[]{:S(2)}, u32[]{:S(2)}) collective-permute-start(bf16[2,256,384]{2,1,0:T(8,128)(2,1)S(1)} %get-tuple-element.46), channel_id=1, source_target_pairs={{0,4},{4,0},{8,12},{12,8},{16,20},{20,16},{24,28},{28,24},{1,5},{5... | collective-permute-start | bytes 1179656 | tf_op jit(solution)/shard_map/ppermute | solution.py:132
  78.2 4.5 %collective-permute-start.18 = (bf16[2,256,384]{2,1,0:T(8,128)(2,1)S(1)}, bf16[2,256,384]{2,1,0:T(8,128)(2,1)S(1)}, u32[]{:S(2)}, u32[]{:S(2)}) collective-permute-start(bf16[2,256,384]{2,1,0:T(8,128)(2,1)S(1)} %add_convert_fusion.5), channel_id=1, source_target_pairs={{0,24},{4,28},{8,0},{12,4},{16,8},{20,12},{24,16},{28,20},{1,25},{... | collective-permute-start | bytes 1179656 | tf_op jit(solution)/shard_map/ppermute | solution.py:129
  83.4 10.3 %attention.3 = (bf16[2,256,384]{2,1,0:T(8,128)(2,1)S(1)}, bf16[2,256,384]{2,1,0:T(8,128)(2,1)S(1)}, bf16[2,256,384]{2,1,0:T(8,128)(2,1)S(1)}, bf16[2,256,384]{2,...) custom-call(s32[2]{0:T(128)S(1)} %pad_add_fusion.1.place, ...), custom_call_target="tpu_custom_call" | custom-call | flops 6442450944 | bytes 4718592 | tf_op jit(solution)/shard_map/attention/pallas_call | solution.py:96
  97.1 4.3 %collective-permute-done.21 = bf16[2,256,384]{2,1,0:T(8,128)(2,1)S(1)} collective-permute-done((bf16[2,256,384]{2,1,0:T(8,128)(2,1)S(1)}, bf16[2,256,384]{2,1,0:T(8,128)(2,1)S(1)}, u32[]{:S(2)}, u32[]{:S(2)}) %collective-permute-start.21) | collective-permute-done | bytes 393248 | tf_op jit(solution)/shard_map/ppermute | solution.py:129
  101.6 2.5 %collective-permute-start.27 = (bf16[48,1536]{1,0:T(8,128)(2,1)S(1)}, bf16[48,1536]{1,0:T(8,128)(2,1)S(1)}, u32[]{:S(2)}, u32[]{:S(2)}) collective-permute-start(bf16[48,1536]{1,0:T(8,128)(2,1)S(1)} %get-tuple-element.92), channel_id=1, source_target_pairs={{0,16},{4,20},{8,24},{12,28},{16,0},{20,4},{24,8},{28,12},{1,17},{... | collective-permute-start | bytes 442376 | tf_op jit(solution)/shard_map/ppermute | solution.py:129
  105.6 3.1 %collective-permute-done.26 = bf16[48,1536]{1,0:T(8,128)(2,1)S(1)} collective-permute-done((bf16[48,1536]{1,0:T(8,128)(2,1)S(1)}, bf16[48,1536]{1,0:T(8,128)(2,1)S(1)}, u32[]{:S(2)}, u32[]{:S(2)}) %collective-permute-start.26) | collective-permute-done | bytes 147488 | tf_op jit(solution)/shard_map/ppermute | solution.py:129
  109.9 2.6 %collective-permute-done.27 = bf16[48,1536]{1,0:T(8,128)(2,1)S(1)} collective-permute-done((bf16[48,1536]{1,0:T(8,128)(2,1)S(1)}, bf16[48,1536]{1,0:T(8,128)(2,1)S(1)}, u32[]{:S(2)}, u32[]{:S(2)}) %collective-permute-start.27) | collective-permute-done | bytes 147488 | tf_op jit(solution)/shard_map/ppermute | solution.py:129
  112.5 3.4 %collective-permute-start.22 = (bf16[2,256,384]{2,1,0:T(8,128)(2,1)S(1)}, bf16[2,256,384]{2,1,0:T(8,128)(2,1)S(1)}, u32[]{:S(2)}, u32[]{:S(2)}) collective-permute-start(bf16[2,256,384]{2,1,0:T(8,128)(2,1)S(1)} %get-tuple-element.78), channel_id=1, source_target_pairs={{0,24},{4,28},{8,0},{12,4},{16,8},{20,12},{24,16},{28,20},{1,25},{... | collective-permute-start | bytes 1179656 | tf_op jit(solution)/shard_map/ppermute | solution.py:129
  117.4 8.2 %collective-permute-done.22 = bf16[2,256,384]{2,1,0:T(8,128)(2,1)S(1)} collective-permute-done((bf16[2,256,384]{2,1,0:T(8,128)(2,1)S(1)}, bf16[2,256,384]{2,1,0:T(8,128)(2,1)S(1)}, u32[]{:S(2)}, u32[]{:S(2)}) %collective-permute-start.22) | collective-permute-done | bytes 393248 | tf_op jit(solution)/shard_map/ppermute | solution.py:129
  125.8 1.9 %collective-permute-start.30 = (bf16[2,256,384]{2,1,0:T(8,128)(2,1)S(1)}, bf16[2,256,384]{2,1,0:T(8,128)(2,1)S(1)}, u32[]{:S(2)}, u32[]{:S(2)}) collective-permute-start(bf16[2,256,384]{2,1,0:T(8,128)(2,1)S(1)} %add_convert_fusion.1), channel_id=1, source_target_pairs={{0,4},{4,0},{8,12},{12,8},{16,20},{20,16},{24,28},{28,24},{1,5},{5... | collective-permute-start | bytes 1179656 | tf_op jit(solution)/shard_map/ppermute | solution.py:132
  127.8 2.3 %fusion.11 = bf16[1,256,1536]{2,1,0:T(8,128)(2,1)} fusion(bf16[384,1536]{1,0:T(8,128)(2,1)S(1)} %get-tuple-element.74, bf16[384,1536]{1,0:T(8,128)(2,1)S(1)} %get-tuple-element.73, bf16[384,1536]{1,0:T(8,128)(2,1)S(1)} %get-tuple-element.72, bf16[384,1536]{1,0:T(8,128)(2,1)S(1)} %get-tuple-element.71, bf16[256,384]{1,0:T(8,128)(2,1)S(1)} %get-tuple-element.101, ...), kind=kOutput, calls=%fused_computation.11 | convolution fusion | flops 1230372864 | bytes 6291456 | tf_op jit(solution)/shard_map/dot_general | solution.py:253
  131.0 2.7 %collective-permute-done.30 = bf16[2,256,384]{2,1,0:T(8,128)(2,1)S(1)} collective-permute-done((bf16[2,256,384]{2,1,0:T(8,128)(2,1)S(1)}, bf16[2,256,384]{2,1,0:T(8,128)(2,1)S(1)}, u32[]{:S(2)}, u32[]{:S(2)}) %collective-permute-start.30) | collective-permute-done | bytes 393248 | tf_op jit(solution)/shard_map/ppermute | solution.py:132
  (110 shorter events, 34.6 us)
Async XLA Ops:
  0.6 43.7 %collective-permute-start.6 = (bf16[384,1536]{1,0:T(8,128)(2,1)}, bf16[384,1536]{1,0:T(8,128)(2,1)}, u32[]{:S(2)}, u32[]{:S(2)}) collective-permute-start(bf16[384,1536]{1,0:T(8,128)(2,1)} %param.12), channel_id=1, source_target_pairs={{0,2},{1,3},{2,0},{3,1},{4,6},{5,7},{6,4},{7,5},{8,10},{9,11},{10,... | collective-permute-start | bytes 3538952 | tf_op jit(solution)/shard_map/ppermute | solution.py:129
  5.4 12.1 %collective-permute-start = (bf16[2,256,384]{2,1,0:T(8,128)(2,1)S(1)}, bf16[2,256,384]{2,1,0:T(8,128)(2,1)S(1)}, u32[]{:S(2)}, u32[]{:S(2)}) collective-permute-start(bf16[2,256,384]{2,1,0:T(8,128)(2,1)S(1)} %pad_maximum_fusion), channel_id=1, source_target_pairs={{0,4},{4,0},{8,12},{12,8},{16,20},{20,16},{24,28},{28,24},{1,5},{5... | collective-permute-start | bytes 1179656 | tf_op jit(solution)/shard_map/ppermute | solution.py:132
  7.0 13.9 %collective-permute-start.1 = (bf16[2,256,384]{2,1,0:T(8,128)(2,1)S(1)}, bf16[2,256,384]{2,1,0:T(8,128)(2,1)S(1)}, u32[]{:S(2)}, u32[]{:S(2)}) collective-permute-start(bf16[2,256,384]{2,1,0:T(8,128)(2,1)S(1)} %pad_maximum_fusion.1), channel_id=1, source_target_pairs={{0,8},{4,12},{8,16},{12,20},{16,24},{20,28},{24,0},{28,4},{1,9},{5... | collective-permute-start | bytes 1179656 | tf_op jit(solution)/shard_map/ppermute | solution.py:129
  9.4 16.5 %collective-permute-start.8 = (bf16[2,256,384]{2,1,0:T(8,128)(2,1)}, bf16[2,256,384]{2,1,0:T(8,128)(2,1)S(1)}, u32[]{:S(2)}, u32[]{:S(2)}) collective-permute-start(bf16[2,256,384]{2,1,0:T(8,128)(2,1)} %pad_maximum_fusion.2), channel_id=1, source_target_pairs={{0,4},{4,0},{8,12},{12,8},{16,20},{20,16},{24,28},{28,24},{1,5},{5... | collective-permute-start | bytes 1179656 | tf_op jit(solution)/shard_map/ppermute | solution.py:132
  10.7 18.6 %collective-permute-start.9 = (bf16[2,256,384]{2,1,0:T(8,128)(2,1)}, bf16[2,256,384]{2,1,0:T(8,128)(2,1)S(1)}, u32[]{:S(2)}, u32[]{:S(2)}) collective-permute-start(bf16[2,256,384]{2,1,0:T(8,128)(2,1)} %pad_maximum_fusion.3), channel_id=1, source_target_pairs={{0,8},{4,12},{8,16},{12,20},{16,24},{20,28},{24,0},{28,4},{1,9},{5... | collective-permute-start | bytes 1179656 | tf_op jit(solution)/shard_map/ppermute | solution.py:129
  20.9 13.6 %collective-permute-start.2 = (bf16[128,1536]{1,0:T(8,128)(2,1)}, bf16[128,1536]{1,0:T(8,128)(2,1)}, u32[]{:S(2)}, u32[]{:S(2)}) collective-permute-start(bf16[128,1536]{1,0:T(8,128)(2,1)} %get-tuple-element.37), channel_id=1, source_target_pairs={{0,4},{4,0},{8,12},{12,8},{16,20},{20,16},{24,28},{28,24},{1,5},{5... | collective-permute-start | bytes 1179656 | tf_op jit(solution)/shard_map/ppermute | solution.py:132
  21.4 14.6 %collective-permute-start.4 = (bf16[2,256,384]{2,1,0:T(8,128)(2,1)S(1)}, bf16[2,256,384]{2,1,0:T(8,128)(2,1)S(1)}, u32[]{:S(2)}, u32[]{:S(2)}) collective-permute-start(bf16[2,256,384]{2,1,0:T(8,128)(2,1)S(1)} %collective-permute-done.kv_par), channel_id=1, source_target_pairs={{0,8},{4,12},{8,16},{12,20},{16,24},{20,28},{24,0},{28,4},{1,9},{5... | collective-permute-start | bytes 1179656 | tf_op jit(solution)/shard_map/ppermute | solution.py:129
  25.9 20.2 %collective-permute-start.16 = (bf16[384,1536]{1,0:T(8,128)(2,1)}, bf16[384,1536]{1,0:T(8,128)(2,1)S(1)}, u32[]{:S(2)}, u32[]{:S(2)}) collective-permute-start(bf16[384,1536]{1,0:T(8,128)(2,1)} %param.12), channel_id=1, source_target_pairs={{0,1},{1,0},{2,3},{3,2},{4,5},{5,4},{6,7},{7,6},{8,9},{9,8},{10,11... | collective-permute-start | bytes 3538952 | tf_op jit(solution)/shard_map/ppermute | solution.py:132
  29.3 13.4 %collective-permute-start.10 = (bf16[128,1536]{1,0:T(8,128)(2,1)}, bf16[128,1536]{1,0:T(8,128)(2,1)S(1)}, u32[]{:S(2)}, u32[]{:S(2)}) collective-permute-start(bf16[128,1536]{1,0:T(8,128)(2,1)} %get-tuple-element.40), channel_id=1, source_target_pairs={{0,4},{4,0},{8,12},{12,8},{16,20},{20,16},{24,28},{28,24},{1,5},{5... | collective-permute-start | bytes 1179656 | tf_op jit(solution)/shard_map/ppermute | solution.py:132
  36.0 15.2 %collective-permute-start.3 = (bf16[256,384]{1,0:T(8,128)(2,1)S(1)}, bf16[256,384]{1,0:T(8,128)(2,1)S(1)}, u32[]{:S(2)}, u32[]{:S(2)}) collective-permute-start(bf16[256,384]{1,0:T(8,128)(2,1)S(1)} %get-tuple-element.38), channel_id=1, source_target_pairs={{0,4},{4,0},{8,12},{12,8},{16,20},{20,16},{24,28},{28,24},{1,5},{5... | collective-permute-start | bytes 589832 | tf_op jit(solution)/shard_map/ppermute | solution.py:132
  42.8 12.3 %collective-permute-start.5 = (bf16[2,256,384]{2,1,0:T(8,128)(2,1)S(1)}, bf16[2,256,384]{2,1,0:T(8,128)(2,1)S(1)}, u32[]{:S(2)}, u32[]{:S(2)}) collective-permute-start(bf16[2,256,384]{2,1,0:T(8,128)(2,1)S(1)} %broadcast_select_fusion.9), channel_id=1, source_target_pairs={{0,8},{4,12},{8,16},{12,20},{16,24},{20,28},{24,0},{28,4},{1,9},{5... | collective-permute-start | bytes 1179656 | tf_op jit(solution)/shard_map/ppermute | solution.py:129
  44.5 38.3 %collective-permute-start.13 = (bf16[256,384]{1,0:T(8,128)(2,1)S(1)}, bf16[256,384]{1,0:T(8,128)(2,1)S(1)}, u32[]{:S(2)}, u32[]{:S(2)}) collective-permute-start(bf16[256,384]{1,0:T(8,128)(2,1)S(1)} %get-tuple-element.47), channel_id=1, source_target_pairs={{0,4},{4,0},{8,12},{12,8},{16,20},{20,16},{24,28},{28,24},{1,5},{5... | collective-permute-start | bytes 589832 | tf_op jit(solution)/shard_map/ppermute | solution.py:132
  46.1 37.3 %collective-permute-start.15 = (bf16[2,256,384]{2,1,0:T(8,128)(2,1)S(1)}, bf16[2,256,384]{2,1,0:T(8,128)(2,1)S(1)}, u32[]{:S(2)}, u32[]{:S(2)}) collective-permute-start(bf16[2,256,384]{2,1,0:T(8,128)(2,1)S(1)} %broadcast_select_fusion.8), channel_id=1, source_target_pairs={{0,8},{4,12},{8,16},{12,20},{16,24},{20,28},{24,0},{28,4},{1,9},{5... | collective-permute-start | bytes 1179656 | tf_op jit(solution)/shard_map/ppermute | solution.py:129
  70.2 24.7 %collective-permute-start.23 = (bf16[2,256,384]{2,1,0:T(8,128)(2,1)S(1)}, bf16[2,256,384]{2,1,0:T(8,128)(2,1)S(1)}, u32[]{:S(2)}, u32[]{:S(2)}) collective-permute-start(bf16[2,256,384]{2,1,0:T(8,128)(2,1)S(1)} %get-tuple-element.61), channel_id=1, source_target_pairs={{0,24},{4,28},{8,0},{12,4},{16,8},{20,12},{24,16},{28,20},{1,25},{... | collective-permute-start | bytes 1179656 | tf_op jit(solution)/shard_map/ppermute | solution.py:129
  76.2 40.4 %collective-permute-start.12 = (bf16[2,256,384]{2,1,0:T(8,128)(2,1)S(1)}, bf16[2,256,384]{2,1,0:T(8,128)(2,1)S(1)}, u32[]{:S(2)}, u32[]{:S(2)}) collective-permute-start(bf16[2,256,384]{2,1,0:T(8,128)(2,1)S(1)} %get-tuple-element.46), channel_id=1, source_target_pairs={{0,4},{4,0},{8,12},{12,8},{16,20},{20,16},{24,28},{28,24},{1,5},{5... | collective-permute-start | bytes 1179656 | tf_op jit(solution)/shard_map/ppermute | solution.py:132
  78.2 16.6 %collective-permute-start.18 = (bf16[2,256,384]{2,1,0:T(8,128)(2,1)S(1)}, bf16[2,256,384]{2,1,0:T(8,128)(2,1)S(1)}, u32[]{:S(2)}, u32[]{:S(2)}) collective-permute-start(bf16[2,256,384]{2,1,0:T(8,128)(2,1)S(1)} %add_convert_fusion.5), channel_id=1, source_target_pairs={{0,24},{4,28},{8,0},{12,4},{16,8},{20,12},{24,16},{28,20},{1,25},{... | collective-permute-start | bytes 1179656 | tf_op jit(solution)/shard_map/ppermute | solution.py:129
  82.8 14.1 %collective-permute-start.19 = (bf16[4,48,1536]{2,1,0:T(8,128)(2,1)S(1)}, bf16[4,48,1536]{2,1,0:T(8,128)(2,1)S(1)}, u32[]{:S(2)}, u32[]{:S(2)}) collective-permute-start(bf16[4,48,1536]{2,1,0:T(8,128)(2,1)S(1)} %fusion.15), channel_id=1, source_target_pairs={{0,2},{1,3},{2,0},{3,1},{4,6},{5,7},{6,4},{7,5},{8,10},{9,11},{10,... | collective-permute-start | bytes 1769480 | tf_op jit(solution)/shard_map/ppermute | solution.py:129
  94.9 22.4 %collective-permute-start.20 = (bf16[2,256,384]{2,1,0:T(8,128)(2,1)S(1)}, bf16[2,256,384]{2,1,0:T(8,128)(2,1)S(1)}, u32[]{:S(2)}, u32[]{:S(2)}) collective-permute-start(bf16[2,256,384]{2,1,0:T(8,128)(2,1)S(1)} %get-tuple-element.53), channel_id=1, source_target_pairs={{0,4},{4,0},{8,12},{12,8},{16,20},{20,16},{24,28},{28,24},{1,5},{5... | collective-permute-start | bytes 1179656 | tf_op jit(solution)/shard_map/ppermute | solution.py:132
  101.6 10.9 %collective-permute-start.27 = (bf16[48,1536]{1,0:T(8,128)(2,1)S(1)}, bf16[48,1536]{1,0:T(8,128)(2,1)S(1)}, u32[]{:S(2)}, u32[]{:S(2)}) collective-permute-start(bf16[48,1536]{1,0:T(8,128)(2,1)S(1)} %get-tuple-element.92), channel_id=1, source_target_pairs={{0,16},{4,20},{8,24},{12,28},{16,0},{20,4},{24,8},{28,12},{1,17},{... | collective-permute-start | bytes 442376 | tf_op jit(solution)/shard_map/ppermute | solution.py:129
  104.0 11.9 %collective-permute-start.28 = (bf16[48,1536]{1,0:T(8,128)(2,1)S(1)}, bf16[48,1536]{1,0:T(8,128)(2,1)S(1)}, u32[]{:S(2)}, u32[]{:S(2)}) collective-permute-start(bf16[48,1536]{1,0:T(8,128)(2,1)S(1)} %get-tuple-element.91), channel_id=1, source_target_pairs={{0,24},{4,28},{8,0},{12,4},{16,8},{20,12},{24,16},{28,20},{1,25},{... | collective-permute-start | bytes 442376 | tf_op jit(solution)/shard_map/ppermute | solution.py:129
  108.7 16.9 %collective-permute-start.24 = (bf16[2,256,384]{2,1,0:T(8,128)(2,1)S(1)}, bf16[2,256,384]{2,1,0:T(8,128)(2,1)S(1)}, u32[]{:S(2)}, u32[]{:S(2)}) collective-permute-start(bf16[2,256,384]{2,1,0:T(8,128)(2,1)S(1)} %get-tuple-element.75), channel_id=1, source_target_pairs={{0,4},{4,0},{8,12},{12,8},{16,20},{20,16},{24,28},{28,24},{1,5},{5... | collective-permute-start | bytes 1179656 | tf_op jit(solution)/shard_map/ppermute | solution.py:132
  112.5 13.0 %collective-permute-start.22 = (bf16[2,256,384]{2,1,0:T(8,128)(2,1)S(1)}, bf16[2,256,384]{2,1,0:T(8,128)(2,1)S(1)}, u32[]{:S(2)}, u32[]{:S(2)}) collective-permute-start(bf16[2,256,384]{2,1,0:T(8,128)(2,1)S(1)} %get-tuple-element.78), channel_id=1, source_target_pairs={{0,24},{4,28},{8,0},{12,4},{16,8},{20,12},{24,16},{28,20},{1,25},{... | collective-permute-start | bytes 1179656 | tf_op jit(solution)/shard_map/ppermute | solution.py:129
  116.0 15.0 %collective-permute-start.29 = (bf16[2,256,384]{2,1,0:T(8,128)(2,1)S(1)}, bf16[2,256,384]{2,1,0:T(8,128)(2,1)S(1)}, u32[]{:S(2)}, u32[]{:S(2)}) collective-permute-start(bf16[2,256,384]{2,1,0:T(8,128)(2,1)S(1)} %get-tuple-element.67), channel_id=1, source_target_pairs={{0,24},{4,28},{8,0},{12,4},{16,8},{20,12},{24,16},{28,20},{1,25},{... | collective-permute-start | bytes 1179656 | tf_op jit(solution)/shard_map/ppermute | solution.py:129
  116.7 13.5 %collective-permute-start.31 = (bf16[48,1536]{1,0:T(8,128)(2,1)S(1)}, bf16[48,1536]{1,0:T(8,128)(2,1)S(1)}, u32[]{:S(2)}, u32[]{:S(2)}) collective-permute-start(bf16[48,1536]{1,0:T(8,128)(2,1)S(1)} %fusion.39), channel_id=1, source_target_pairs={{0,0},{1,4},{2,2},{3,6},{4,1},{5,5},{6,3},{7,7},{8,8},{9,12},{10,1... | collective-permute-start | bytes 442376 | tf_op jit(solution)/shard_map/ppermute | solution.py:242
  (18 other events, 114.2 us)
